TPU v7x, 512 devices: a whole 4x4x16 slice. The times are simulated.
512 devices in a mesh: pb: 32 (over x, z_hi, core), row: 16 (over y, z_lo).
Axes of the slice: x: 4, y: 4, z: 16 (z_hi: 4, z_lo: 4; z = z_hi * 4 + z_lo), core: 2. Of those that a mesh axis runs over, the one named last changes fastest.
Arguments:
- dec_states: bfloat16 [32, 64, 2048], P('pb'), may hold values from -6 to 6
- enc_states: bfloat16 [32, 2048, 2048], P('pb', 'row'), may hold values from -6 to 6
- passage_lengths: int32 [32, 16], P('pb'), may hold values from 1 to 128, as said below
- q_weight: bfloat16 [2048, 4096], P('pb', 'row'), may hold values from -0.125 to 0.125
- kv_weight: bfloat16 [2048, 256], P('pb'), may hold values from -0.125 to 0.125
- o_weight: bfloat16 [4096, 2048], P('row', 'pb'), may hold values from -0.09375 to 0.09375
- out_grad: bfloat16 [32, 64, 2048], P('pb'), may hold values from -192 to 192
Outputs:
- dec_grad: bfloat16 [32, 64, 2048], P('pb', None, 'row')
- enc_grad: bfloat16 [32, 2048, 2048], P('pb', 'row')
- q_weight_grad: float32 [2048, 4096], P(None, 'row')
- kv_weight_grad: float32 [2048, 256], P('pb')
- o_weight_grad: bfloat16 [4096, 2048], P('row')
Inputs may be any that keep to these rules, and one draw needn't show every extreme that they name: passage_lengths[q, p] counts the real tokens at the start of passage p of question q; every question has a passage of full length 128.
All inputs are finite; a program needn't handle non-finite values.
Results may differ from a plain program's by a relative error of at most 0.034.
Values may be sent and summed in bfloat16 or wider, within the bound.
No kernel may reach another device: no remote copies, remote signals or barrier semaphores. Data moves between devices by JAX's collectives and lax.ppermute only.
A program may use at most 64 MiB of HBM per device.

v0:
```python
import jax
import jax.numpy as jnp
from jax import lax
from jax.sharding import PartitionSpec as P

HD = 128
PT = 128


def local(dec_states, enc_states, passage_lengths, q_weight, kv_weight, o_weight, out_grad):
    f32 = jnp.float32
    score_scale = HD ** (-0.5)
    dec_rows = dec_states[0]
    enc_rows = enc_states[0]
    length_row = passage_lengths[0]
    grad_rows = out_grad[0]
    row_count = dec_rows.shape[0]
    head_cols = q_weight.shape[1]
    local_heads = head_cols // HD
    wq_full, wkv_full, wo_full = (
        lax.all_gather(q_weight, "pb", axis=0, tiled=True),
        lax.all_gather(kv_weight, "pb", axis=0, tiled=True),
        lax.all_gather(o_weight, "pb", axis=1, tiled=True),
    )
    queries = jnp.dot(dec_rows, wq_full, preferred_element_type=f32).astype(jnp.bfloat16)
    key_values = jnp.dot(enc_rows, wkv_full, preferred_element_type=f32).astype(jnp.bfloat16)
    attn_grad = jnp.dot(grad_rows, wo_full.T, preferred_element_type=f32).astype(jnp.bfloat16)
    all_kv = lax.all_gather(key_values, "row", axis=0, tiled=True)
    key_rows = all_kv[:, :HD]
    value_rows = all_kv[:, HD:]
    valid_mask = (jnp.arange(PT)[None, :] < length_row[:, None]).reshape(-1)
    query_heads = queries.reshape(row_count, local_heads, HD)
    scores = (
        jnp.einsum("ahd,td->hat", query_heads, key_rows, preferred_element_type=f32) * score_scale
    )
    weights = jnp.where(valid_mask[None, None, :], jnp.exp(scores), 0.0)
    totals = jnp.sum(weights, -1)
    weights_b = weights.astype(jnp.bfloat16)
    mixed = (
        jnp.einsum("hat,td->ahd", weights_b, value_rows, preferred_element_type=f32)
        / totals.T[:, :, None]
    )
    mixed_own = mixed.reshape(row_count, head_cols).astype(jnp.bfloat16)
    grad_heads = attn_grad.reshape(row_count, local_heads, HD)
    probs = weights / totals[..., None]
    dprob = jnp.einsum("ahd,td->hat", grad_heads, value_rows, preferred_element_type=f32)
    delta_rows = jnp.sum(grad_heads.astype(f32) * mixed, -1).T
    dscore_b = (probs * (dprob - delta_rows[..., None]) * score_scale).astype(jnp.bfloat16)
    probs_b = probs.astype(jnp.bfloat16)
    query_grad = (
        jnp.einsum("hat,td->ahd", dscore_b, key_rows, preferred_element_type=f32)
        .reshape(row_count, head_cols)
        .astype(jnp.bfloat16)
    )
    key_part = jnp.einsum("cat,acd->td", dscore_b, query_heads, preferred_element_type=f32)
    value_part = jnp.einsum("cat,acd->td", probs_b, grad_heads, preferred_element_type=f32)
    kv_grad = lax.psum_scatter(
        jnp.concatenate([key_part, value_part], -1).astype(jnp.bfloat16),
        "row",
        scatter_dimension=0,
        tiled=True,
    )
    enc_grad = jnp.dot(kv_grad, wkv_full.T, preferred_element_type=f32).astype(jnp.bfloat16)
    kv_term = jnp.dot(enc_rows.T, kv_grad, preferred_element_type=f32)
    kv_share = lax.psum_scatter(kv_term.astype(jnp.bfloat16), "pb", scatter_dimension=0, tiled=True)
    kv_weight_grad = lax.psum(kv_share, "row").astype(jnp.float32)
    o_term = jnp.dot(mixed_own.T, grad_rows, preferred_element_type=f32)
    o_weight_grad = lax.psum(o_term.astype(jnp.bfloat16), "pb")
    q_term = jnp.dot(dec_rows.T, query_grad, preferred_element_type=f32)
    q_weight_grad = lax.psum(q_term.astype(jnp.bfloat16), "pb").astype(jnp.float32)
    dec_part = jnp.dot(query_grad, wq_full.T, preferred_element_type=f32)
    dec_grad = lax.psum_scatter(
        dec_part.astype(jnp.bfloat16), "row", scatter_dimension=1, tiled=True
    )
    return (dec_grad[None], enc_grad[None], q_weight_grad, kv_weight_grad, o_weight_grad)


def solution(mesh):
    placed = (
        P("pb", None, None),
        P("pb", "row", None),
        P("pb", None),
        P("pb", "row"),
        P("pb", None),
        P("row", "pb"),
        P("pb", None, None),
    )
    return jax.shard_map(
        local,
        mesh=mesh,
        in_specs=placed,
        out_specs=(
            P("pb", None, "row"),
            P("pb", "row", None),
            P(None, "row"),
            P("pb", None),
            P("row", None),
        ),
        check_vma=False,
    )
```

profile of v0, /device:TPU:1, one launch (start us, length us, event | category | flops | bytes accessed | tf_op | source)
XLA Modules:
  0.0 1033.5 jit_solution(15171273449287406881)
XLA Ops:
  7.2 0.7 all-gather.5.cloned.1.call-update
  8.0 0.7 all-gather.11.cloned.1.call-update
  8.7 0.7 all-gather.9.cloned.1.call-update
  9.5 79.1 %all-gather.5.cloned.1.call-done = bf16[2048,256]{1,0:T(8,128)(2,1)} async-done(((bf16[64,256]{1,0:T(8,128)(2,1)}), bf16[2048,256]{1,0:T(8,128)(2,1)}) %all-gather.5.cloned.1.call-update) | async-done | bytes 1048592 | tf_op jit(solution)/shard_map/all_gather | solution.py:22
  88.6 2.2 convolution_convert_fusion.5
  90.8 0.7 fusion.38
  91.6 65.6 %all-gather.11.cloned.1.call-done = bf16[256,2048]{0,1:T(8,128)(2,1)} async-done(((bf16[256,64]{0,1:T(8,128)(2,1)}), bf16[256,2048]{0,1:T(8,128)(2,1)}) %all-gather.11.cloned.1.call-update) | async-done | bytes 1048592 | tf_op jit(solution)/shard_map/all_gather | solution.py:23
  157.2 1.6 fusion.14
  158.8 67.0 %all-gather.9.cloned.1.call-done = bf16[2048,256]{1,0:T(8,128)(2,1)} async-done(((bf16[64,256]{1,0:T(8,128)(2,1)}), bf16[2048,256]{1,0:T(8,128)(2,1)}) %all-gather.9.cloned.1.call-update) | async-done | bytes 1048592 | tf_op jit(solution)/shard_map/all_gather | solution.py:21
  225.8 1.5 fusion.13
  227.3 72.3 %all-gather.7.cloned.1.call-done = bf16[2048,256]{1,0:T(8,128)(2,1)} async-done(((bf16[128,256]{1,0:T(8,128)(2,1)}), bf16[2048,256]{1,0:T(8,128)(2,1)}) %all-gather.7.cloned.1.call-update) | async-done | bytes 1048592 | tf_op jit(solution)/shard_map/all_gather | solution.py:28
  299.6 1.5 fusion.39
  301.5 0.8 copy-done.7
  303.5 1.3 copy.39
  304.9 1.3 fusion.15
  306.2 0.4 convolution_convert_fusion.4
  306.7 1.0 copy.37
  307.8 1.4 fusion
  309.2 1.5 convolution_convert_fusion.1
  310.7 82.7 %reduce-scatter.12.cloned.1.call-done = bf16[128,256]{1,0:T(8,128)(2,1)} async-done(((bf16[2048,256]{1,0:T(8,128)(2,1)}), bf16[128,256]{1,0:T(8,128)(2,1)}) %reduce-scatter.12.cloned.1.call-update) | async-done | bytes 65552
  393.4 1.3 fusion.1
  394.7 1.3 copy.41
  396.0 86.5 %reduce-scatter.10.cloned.1.call-done = bf16[128,64]{1,0:T(8,128)(2,1)} async-done(((bf16[2048,64]{1,0:T(8,128)(2,1)}), bf16[128,64]{1,0:T(8,128)(2,1)}) %reduce-scatter.10.cloned.1.call-update) | async-done | bytes 16400
  482.5 1.4 copy.38
  483.9 363.9 %all-reduce.3.cloned.1.call-done = (bf16[2048,256]{0,1:T(8,128)(2,1)}, bf16[256,2048]{1,0:T(8,128)(2,1)}) async-done(((bf16[2048,256]{0,1:T(8,128)(2,1)}, bf16[256,2048]{1,0:T(8,128)(2,1)}), (bf16[2048,256]{0,1:T(8,128)(2,1)}, bf16[256,2048]{1,0:T(8,128)(2,1)})) %all-reduce.3.cloned.1.call-update) | async-done | bytes 2097168 | tf_op jit(solution)/shard_map/psum | solution.py:70
  847.8 2.7 copy.35
  850.5 1.3 fusion.11
  851.7 109.1 %reduce-scatter.14.cloned.1.call-done = bf16[64,256]{1,0:T(8,128)(2,1)} async-done(((bf16[2048,256]{1,0:T(8,128)(2,1)}), bf16[64,256]{1,0:T(8,128)(2,1)}) %reduce-scatter.14.cloned.1.call-update) | async-done | bytes 32784
  960.8 0.9 copy.42
  961.7 63.3 %psum.22 = bf16[64,256]{0,1:T(8,128)(2,1)S(1)} all-reduce(bf16[64,256]{0,1:T(8,128)(2,1)S(1)} %copy.42), channel_id=1, replica_groups=mesh['pb'=32,'row'=16] {'row'}, use_global_device_ids=true, to_apply=%region_6.7 | all-reduce | flops 16384 | bytes 65536 | tf_op jit(solution)/shard_map/psum | solution.py:66
  1025.0 0.7 copy.36
  1025.7 1.0 copy.80
  (33 shorter events, 1.9 us)
Async XLA Ops:
  7.2 81.4 %copy-start = (bf16[1,128,2048]{2,1,0:T(8,128)(2,1)S(1)}, bf16[1,128,2048]{2,1,0:T(8,128)(2,1)}, u32[]{:S(2)}) copy-start(bf16[1,128,2048]{2,1,0:T(8,128)(2,1)} %param.8) | copy-start | bytes 1572868
  7.2 218.6 %copy-start.4 = (bf16[1,64,2048]{2,1,0:T(8,128)(2,1)S(1)}, bf16[1,64,2048]{2,1,0:T(8,128)(2,1)}, u32[]{:S(2)}) copy-start(bf16[1,64,2048]{2,1,0:T(8,128)(2,1)} %param.7) | copy-start | bytes 786436
  7.2 81.4 %all-gather.5.cloned.1.call-start = ((), (), s32[]{:S(2)}) async-start(), calls=%async_computation.3 | async-start | bytes 1081344 | tf_op jit(solution)/shard_map/all_gather | solution.py:22
  7.9 149.3 %all-gather.11.cloned.1.call-start = ((), (), s32[]{:S(2)}) async-start(), calls=%async_computation.6 | async-start | bytes 1081344 | tf_op jit(solution)/shard_map/all_gather | solution.py:23
  8.7 217.1 %all-gather.9.cloned.1.call-start = ((), (), s32[]{:S(2)}) async-start(), calls=%async_computation.5 | async-start | bytes 1081344 | tf_op jit(solution)/shard_map/all_gather | solution.py:21
  9.4 290.2 %all-gather.7.cloned.1.call-start = ((), (), s32[]{:S(2)}) async-start(), calls=%async_computation.4 | async-start | bytes 1114112 | tf_op jit(solution)/shard_map/all_gather | solution.py:28
  90.8 302.6 %reduce-scatter.12.cloned.1.call-start = ((), (), s32[]{:S(2)}) async-start(), calls=%async_computation.8 | async-start | bytes 1114112
  301.1 1.2 copy-start.7
  303.5 2.7 copy-start.2
  304.8 177.7 %reduce-scatter.10.cloned.1.call-start = ((), (), s32[]{:S(2)}) async-start(), calls=%async_computation.7 | async-start | bytes 557056
  306.2 3.0 copy-start.5
  307.7 540.1 %all-reduce.3.cloned.1.call-start = ((), (), s32[]{:S(2)}) async-start(), calls=%async_computation.10 | async-start | bytes 4194304 | tf_op jit(solution)/shard_map/psum | solution.py:70
  310.7 650.1 %reduce-scatter.14.cloned.1.call-start = ((), (), s32[]{:S(2)}) async-start(), calls=%async_computation.9 | async-start | bytes 1081344
  396.0 454.5 %copy-start.1 = (bf16[2048,256]{1,0:T(8,128)(2,1)S(1)}, bf16[2048,256]{1,0:T(8,128)(2,1)}, u32[]{:S(2)}) copy-start(bf16[2048,256]{1,0:T(8,128)(2,1)} %all-gather.5.cloned.1.call-done) | copy-start | bytes 3145732
  396.0 454.5 %copy-start.6 = (bf16[128,256]{1,0:T(8,128)(2,1)S(1)}, bf16[128,256]{1,0:T(8,128)(2,1)}, u32[]{:S(2)}) copy-start(bf16[128,256]{1,0:T(8,128)(2,1)} %reduce-scatter.12.cloned.1.call-done) | copy-start | bytes 196612
  847.8 177.9 %copy-start.3 = (bf16[256,2048]{1,0:T(8,128)(2,1)S(1)}, bf16[256,2048]{1,0:T(8,128)(2,1)}, u32[]{:S(2)}) copy-start(bf16[256,2048]{1,0:T(8,128)(2,1)} %get-tuple-element.30) | copy-start | bytes 3145732
Sparse Core Ops, SparseCore 0:
  11.2 77.3 all-gather.4
  91.7 65.4 all-gather.10
  160.3 65.4 all-gather.8
  228.3 71.2 all-gather.6
  305.0 88.3 reduce-scatter.11
  396.8 85.6 reduce-scatter.9
  486.0 361.7 all-reduce.2
  853.4 107.3 reduce-scatter.13
where the time goes:
time: 1050 us; the launch traced here: 1030 us
  waiting for transfers between devices  928 us (88%)
  blocking collectives  63.3 us (6%)
  matrix products  15.4 us (1%)
  between operations  14.3 us (1%)
  local copies, waits for them, and re-layouts  11.2 us (1%)
    psum x1, waiting for transfers between devices, local(): lax.psum(q_term.astype(jnp.bfloat16), 'pb').astype(jnp.float32)  364 us
    unnamed x11, waiting for transfers between devices  280 us
    all_gather x1, waiting for transfers between devices, local(): lax.all_gather(kv_weight, 'pb', axis=0, tiled=True)  79.1 us
    all_gather x1, waiting for transfers between devices, local(): all_kv = lax.all_gather(key_values, 'row', axis=0, tiled=True)  72.3 us
    all_gather x1, waiting for transfers between devices, local(): lax.all_gather(q_weight, 'pb', axis=0, tiled=True)  67 us
    all_gather x1, waiting for transfers between devices, local(): lax.all_gather(o_weight, 'pb', axis=1, tiled=True)  65.6 us
    psum x1, blocking collectives, local(): kv_weight_grad = lax.psum(kv_share, 'row').astype(jnp.float32)  63.3 us
  transfers between devices with their start and end apart: 8, of which 8 were waited for; matrix products, arithmetic and copies ran while one was open for 2% of the time, Pallas kernels for 0%

commit v1 on v0

v1 whole, which is shorter than its diff:
```python
import jax
import jax.numpy as jnp
from jax import lax
from jax.sharding import Mesh, PartitionSpec as P

HD = 128
PT = 128
f32 = jnp.float32
bf16 = jnp.bfloat16


def spread(block, axis, count):
    copies = jnp.broadcast_to(block[None], (count,) + block.shape)
    return lax.all_to_all(copies, axis, 0, 0)


def exchange(parts, axis):
    return jnp.sum(lax.all_to_all(parts, axis, 0, 0).astype(f32), 0)


def swap(block):
    return lax.ppermute(block, "co", [(0, 1), (1, 0)])


def local(dec_states, enc_states, passage_lengths, q_weight, kv_weight, o_weight, out_grad):
    score_scale = HD ** (-0.5)
    dec_rows = dec_states[0]
    enc_rows = enc_states[0]
    grad_rows = out_grad[0]
    co = lax.axis_index("co")
    zl = lax.axis_index("zl")
    first_core = co == 0

    shard = jnp.concatenate([q_weight, kv_weight, o_weight.T], 1)
    own = lax.all_gather(shard, "zh", axis=0, tiled=True)
    own = spread(own, "x", 4).reshape(16, 64, 768)
    other = swap(own)
    weights_all = jnp.stack(
        [jnp.where(first_core, own, other), jnp.where(first_core, other, own)], 1
    ).reshape(2048, 768)
    wq_full = weights_all[:, :256]
    wkv_full = weights_all[:, 256:512]
    wo_t = weights_all[:, 512:]

    key_values = jnp.dot(enc_rows, wkv_full, preferred_element_type=f32).astype(bf16)
    queries = jnp.dot(dec_rows, wq_full, preferred_element_type=f32).astype(bf16)
    attn_grad = jnp.dot(grad_rows, wo_t, preferred_element_type=f32).astype(bf16)

    kv_all = spread(key_values, "y", 4).reshape(512, 256)
    qa_all = spread(jnp.concatenate([queries, attn_grad], 1), "zl", 4)
    key_rows = kv_all[:, :HD]
    value_rows = kv_all[:, HD:]
    query_heads = qa_all[:, :, :256].reshape(4, 64, 2, HD)
    grad_heads = qa_all[:, :, 256:].reshape(4, 64, 2, HD)
    lengths = lax.dynamic_index_in_dim(passage_lengths[0].reshape(4, 4), zl, 1, keepdims=False)
    valid_mask = (jnp.arange(PT)[None, :] < lengths[:, None]).reshape(-1)

    scores = jnp.einsum("zacd,td->zcat", query_heads, key_rows, preferred_element_type=f32)
    weights = jnp.where(valid_mask, jnp.exp(scores * score_scale), 0.0)
    dprob = jnp.einsum("zacd,td->zcat", grad_heads, value_rows, preferred_element_type=f32)
    part_total = jnp.sum(weights, -1)
    part_safe = jnp.where(part_total > 0, part_total, 1.0)
    part_delta = jnp.sum(weights / part_safe[..., None] * dprob, -1)
    stats = spread(jnp.stack([part_total, part_delta]).reshape(8, 128), "zl", 4)
    stats = stats.reshape(4, 2, 4, 2, 64)
    totals = jnp.sum(stats[:, 0], 0)
    delta = jnp.sum(stats[:, 0] / totals * stats[:, 1], 0)
    weights_b = weights.astype(bf16)
    probs = weights / totals[..., None]
    dscore_b = (probs * (dprob - delta[..., None]) * score_scale).astype(bf16)
    probs_b = probs.astype(bf16)
    mixed_part = jnp.einsum(
        "zcat,td->zacd", weights_b, value_rows, preferred_element_type=f32
    ) / totals.transpose(0, 2, 1)[..., None]
    query_part = jnp.einsum("zcat,td->zacd", dscore_b, key_rows, preferred_element_type=f32)
    own_parts = jnp.concatenate(
        [mixed_part.reshape(4, 64, 256), query_part.reshape(4, 64, 256)], 2
    ).astype(bf16)
    own_heads = exchange(own_parts, "zl").astype(bf16)
    mixed_own = own_heads[:, :256]
    query_grad = own_heads[:, 256:]

    key_part = jnp.einsum("zcat,zacd->td", dscore_b, query_heads, preferred_element_type=f32)
    value_part = jnp.einsum("zcat,zacd->td", probs_b, grad_heads, preferred_element_type=f32)
    kv_part = jnp.concatenate([key_part, value_part], -1).astype(bf16).reshape(4, PT, 256)
    dec_part = jnp.dot(query_grad, wq_full.T, preferred_element_type=f32).astype(bf16)
    dec_part = dec_part.reshape(64, 4, 2, 256).transpose(1, 2, 0, 3).reshape(4, 128, 256)
    y_sum = exchange(jnp.concatenate([kv_part, dec_part], 1), "y").astype(bf16)
    kv_grad = y_sum[:PT]
    dec_half = y_sum[PT:].reshape(2, 64, 2, 128).transpose(0, 2, 1, 3).reshape(4, 64, 128)
    dec_grad = exchange(dec_half, "zl").astype(bf16)
    enc_grad = jnp.dot(kv_grad, wkv_full.T, preferred_element_type=f32).astype(bf16)

    q_term = jnp.dot(dec_rows.T, query_grad, preferred_element_type=f32).astype(bf16)
    o_term = jnp.dot(grad_rows.T, mixed_own, preferred_element_type=f32).astype(bf16)
    kv_term = jnp.dot(enc_rows.T, kv_grad, preferred_element_type=f32).astype(bf16)
    kv_term = kv_term.reshape(16, 2, 64, 256).transpose(1, 0, 2, 3).reshape(2, 1024, 256)
    terms = jnp.concatenate(
        [q_term.reshape(2, 1024, 256), o_term.reshape(2, 1024, 256), kv_term], 2
    )
    keep = jnp.where(first_core, terms[0], terms[1])
    send = jnp.where(first_core, terms[1], terms[0])
    chip_sum = (keep.astype(f32) + swap(send).astype(f32)).astype(bf16)
    x_sum = exchange(chip_sum.reshape(4, 256, 768), "x").astype(bf16)
    z_sum = exchange(x_sum.reshape(4, 64, 768), "zh").astype(bf16)
    kv_y = jnp.sum(spread(z_sum[:, 512:], "y", 4).astype(f32), 0).astype(bf16)
    kv_weight_grad = jnp.sum(spread(kv_y, "zl", 4).astype(f32), 0)

    mine = lax.all_gather(z_sum[:, :512], "zh", axis=0, tiled=True)
    mine = spread(mine, "x", 4).reshape(1024, 512)
    theirs = swap(mine)
    both = jnp.concatenate(
        [jnp.where(first_core, mine, theirs), jnp.where(first_core, theirs, mine)], 0
    )
    q_weight_grad = both[:, :256].astype(f32)
    o_weight_grad = both[:, 256:].T
    return (dec_grad[None], enc_grad[None], q_weight_grad, kv_weight_grad, o_weight_grad)


def solution(mesh):
    fine = Mesh(mesh.devices.reshape(4, 4, 2, 4, 4), ("x", "zh", "co", "y", "zl"))
    pb = ("x", "zh", "co")
    row = ("y", "zl")
    placed = (
        P(pb, None, None),
        P(pb, row, None),
        P(pb, None),
        P(pb, row),
        P(pb, None),
        P(row, pb),
        P(pb, None, None),
    )
    return jax.shard_map(
        local,
        mesh=fine,
        in_specs=placed,
        out_specs=(
            P(pb, None, row),
            P(pb, row, None),
            P(None, row),
            P(pb, None),
            P(row, None),
        ),
        check_vma=False,
    )
```

time: 1050 us -> 258 us (0.25); the launches traced: 1030 us -> 255 us
  waiting for transfers between devices: 928 us -> 32.4 us
  blocking collectives: 63.3 us -> 135 us
  starting transfers between devices: 0.32 us -> 51.3 us
  between operations: 14.3 us -> 1.17 us
    psum x1 -> x0, waiting for transfers between devices: 364 us -> none  [local(): lax.psum(q_term.astype(jnp.bfloat16), 'pb').astype(jnp.float32)]
    all_gather x4 -> x0, waiting for transfers between devices: 284 us -> none  [the longest x1 79.1 us: local(): lax.all_gather(kv_weight, 'pb', axis=0, tiled=True)]
    unnamed x11 -> x0, waiting for transfers between devices: 280 us -> none
    all_to_all x0 -> x5, blocking collectives: none -> 90.8 us  [the longest x2 50.9 us: exchange(): return jnp.sum(lax.all_to_all(parts, axis, 0, 0).astype(f32), 0)]
    psum x1 -> x0, blocking collectives: 63.3 us -> none  [local(): kv_weight_grad = lax.psum(kv_share, 'row').astype(jnp.float32)]
    all_gather x0 -> x2, blocking collectives: none -> 44.6 us  [the longest x1 27.8 us: local(): own = lax.all_gather(shard, 'zh', axis=0, tiled=True)]
    all_to_all x0 -> x7, starting transfers between devices: none -> 27 us  [the longest x4 14.2 us: spread(): return lax.all_to_all(copies, axis, 0, 0)]
    all_to_all x0 -> x7, waiting for transfers between devices: none -> 26.3 us  [the longest x4 15.4 us: spread(): return lax.all_to_all(copies, axis, 0, 0)]
  transfers between devices with their start and end apart: 8 -> 10, of which waited for: 8 -> 9; matrix products, arithmetic and copies ran while one was open for 2% -> 6% of each run, Pallas kernels for 0% -> 0%
where the time goes in v1:
time: 258 us; the launch traced here: 255 us
  blocking collectives  135 us (52%)
  starting transfers between devices  51.3 us (20%)
  waiting for transfers between devices  32.4 us (13%)
  local copies, waits for them, and re-layouts  14 us (5%)
  other arithmetic  11.3 us (4%)
  matrix products  9.79 us (4%)
    all_to_all x2, blocking collectives, exchange(): return jnp.sum(lax.all_to_all(parts, axis, 0, 0).astype(f32), 0)  50.9 us
    all_to_all x3, blocking collectives, spread(): return lax.all_to_all(copies, axis, 0, 0)  39.9 us
    all_gather x1, blocking collectives, local(): own = lax.all_gather(shard, 'zh', axis=0, tiled=True)  27.8 us
    ppermute x3, starting transfers between devices, swap(): return lax.ppermute(block, 'co', [(0, 1), (1, 0)])  24.2 us
    all_gather x1, blocking collectives, local(): mine = lax.all_gather(z_sum[:, :512], 'zh', axis=0, tiled=True)  16.8 us
    all_to_all x4, waiting for transfers between devices, spread(): return lax.all_to_all(copies, axis, 0, 0)  15.4 us
    all_to_all x4, starting transfers between devices, spread(): return lax.all_to_all(copies, axis, 0, 0)  14.2 us
    all_to_all x3, starting transfers between devices, exchange(): return jnp.sum(lax.all_to_all(parts, axis, 0, 0).astype(f32), 0)  12.8 us
  transfers between devices with their start and end apart: 10, of which 9 were waited for; matrix products, arithmetic and copies ran while one was open for 6% of the time, Pallas kernels for 0%

profile of v1, /device:TPU:1, one launch (start us, length us, event | category | flops | bytes accessed | tf_op | source)
XLA Modules:
  0.0 255.3 jit_solution(8331498898221787068)
XLA Ops:
  1.5 27.8 %all_gather.6 = bf16[256,768]{1,0:T(8,128)(2,1)S(1)} all-gather(bf16[64,768]{1,0:T(8,128)(2,1)S(1)} %pad_maximum_fusion.5), channel_id=1, replica_groups=mesh['x'=4,'zh'=4,'co'=2,'y'=4,'zl'=4] {'zh'}, dimensions={0}, use_global_device_ids=true | all-gather | bytes 491520 | tf_op jit(solution)/shard_map/all_gather | solution.py:35
  29.4 20.1 %all_to_all.60 = bf16[4,256,768]{2,1,0:T(8,128)(2,1)S(1)} all-to-all(bf16[4,256,768]{2,1,0:T(8,128)(2,1)S(1)} %broadcast_in_dim.33), channel_id=1, replica_groups=mesh['x'=4,'zh'=4,'co'=2,'y'=4,'zl'=4] {'x'}, dimensions={0} | all-to-all | bytes 3145728 | tf_op jit(solution)/shard_map/all_to_all | solution.py:14
  49.5 7.3 %collective-permute-start = (bf16[16,64,768]{2,1,0:T(8,128)(2,1)S(1)}, bf16[16,64,768]{2,1,0:T(8,128)(2,1)}, u32[]{:S(2)}, u32[]{:S(2)}) collective-permute-start(bf16[16,64,768]{2,1,0:T(8,128)(2,1)S(1)} %bitcast.220), channel_id=1, source_target_pairs={{0,16},{16,0},{1,17},{17,1},{2,18},{18,2},{3,19},{19,3},{4,20},{20... | collective-permute-start | bytes 4718600 | tf_op jit(solution)/shard_map/ppermute | solution.py:22
  56.8 3.1 %collective-permute-done = bf16[16,64,768]{2,1,0:T(8,128)(2,1)} collective-permute-done((bf16[16,64,768]{2,1,0:T(8,128)(2,1)S(1)}, bf16[16,64,768]{2,1,0:T(8,128)(2,1)}, u32[]{:S(2)}, u32[]{:S(2)}) %collective-permute-start) | collective-permute-done | bytes 1572896 | tf_op jit(solution)/shard_map/ppermute | solution.py:22
  59.9 1.6 select_bitcast_fusion.2
  64.6 3.4 %all-to-all-start.2 = ((bf16[4,64,512]{2,1,0:T(8,128)(2,1)}), bf16[4,64,512]{2,1,0:T(8,128)(2,1)S(1)}, u32[]{:S(2)}, u32[]{:S(2)}) async-start(bf16[4,64,512]{2,1,0:T(8,128)(2,1)} %broadcast_in_dim.35), calls=%async_computation.2 | async-start | bytes 524288 | tf_op jit(solution)/shard_map/all_to_all | solution.py:14
  69.5 1.7 fusion.13
  71.4 4.0 %all-to-all-done.2 = bf16[4,64,512]{2,1,0:T(8,128)(2,1)S(1)} async-done(((bf16[4,64,512]{2,1,0:T(8,128)(2,1)}), bf16[4,64,512]{2,1,0:T(8,128)(2,1)S(1)}, u32[]{:S(2)}, u32[]{:S(2)}) %all-to-all-start.2) | async-done | bytes 262176 | tf_op jit(solution)/shard_map/all_to_all | solution.py:14
  76.1 4.2 %all-to-all-start.1 = ((bf16[4,128,256]{2,1,0:T(8,128)(2,1)}), bf16[4,128,256]{2,1,0:T(8,128)(2,1)S(1)}, u32[]{:S(2)}, u32[]{:S(2)}) async-start(bf16[4,128,256]{2,1,0:T(8,128)(2,1)} %broadcast_in_dim.34), calls=%async_computation.1 | async-start | bytes 524288 | tf_op jit(solution)/shard_map/all_to_all | solution.py:14
  80.3 5.5 %all-to-all-done.1 = bf16[4,128,256]{2,1,0:T(8,128)(2,1)S(1)} async-done(((bf16[4,128,256]{2,1,0:T(8,128)(2,1)}), bf16[4,128,256]{2,1,0:T(8,128)(2,1)S(1)}, u32[]{:S(2)}, u32[]{:S(2)}) %all-to-all-start.1) | async-done | bytes 262176 | tf_op jit(solution)/shard_map/all_to_all | solution.py:14
  86.8 7.7 %all_to_all.61 = f32[4,8,128]{2,1,0:T(8,128)S(1)} all-to-all(f32[4,8,128]{2,1,0:T(8,128)S(1)} %broadcast_in_dim.39), channel_id=1, replica_groups=mesh['x'=4,'zh'=4,'co'=2,'y'=4,'zl'=4] {'zl'}, dimensions={0} | all-to-all | bytes 32768 | tf_op jit(solution)/shard_map/all_to_all | solution.py:14
  96.1 3.4 %all-to-all-start.4 = ((bf16[4,64,512]{2,1,0:T(8,128)(2,1)}), bf16[4,64,512]{2,1,0:T(8,128)(2,1)S(1)}, u32[]{:S(2)}, u32[]{:S(2)}) async-start(bf16[4,64,512]{2,1,0:T(8,128)(2,1)} %pad_maximum_fusion.4), calls=%async_computation.4 | async-start | bytes 524288 | tf_op jit(solution)/shard_map/all_to_all | solution.py:18
  99.5 1.5 fusion.22
  102.3 2.9 %all-to-all-done.4 = bf16[4,64,512]{2,1,0:T(8,128)(2,1)S(1)} async-done(((bf16[4,64,512]{2,1,0:T(8,128)(2,1)}), bf16[4,64,512]{2,1,0:T(8,128)(2,1)S(1)}, u32[]{:S(2)}, u32[]{:S(2)}) %all-to-all-start.4) | async-done | bytes 262176 | tf_op jit(solution)/shard_map/all_to_all | solution.py:18
  105.2 1.7 convolution_convert_fusion.4
  108.1 3.5 %all-to-all-start.5 = ((bf16[4,256,256]{1,2,0:T(8,128)(2,1)}), bf16[4,256,256]{1,2,0:T(8,128)(2,1)S(1)}, u32[]{:S(2)}, u32[]{:S(2)}) async-start(bf16[4,256,256]{1,2,0:T(8,128)(2,1)} %pad_maximum_fusion.3), calls=%async_computation.5 | async-start | bytes 1048576 | tf_op jit(solution)/shard_map/all_to_all | solution.py:18
  115.1 3.4 %all-to-all-done.5 = bf16[4,256,256]{1,2,0:T(8,128)(2,1)S(1)} async-done(((bf16[4,256,256]{1,2,0:T(8,128)(2,1)}), bf16[4,256,256]{1,2,0:T(8,128)(2,1)S(1)}, u32[]{:S(2)}, u32[]{:S(2)}) %all-to-all-start.5) | async-done | bytes 524320 | tf_op jit(solution)/shard_map/all_to_all | solution.py:18
  121.5 8.5 %collective-permute-start.1 = (bf16[1024,768]{1,0:T(8,128)(2,1)S(1)}, bf16[1024,768]{1,0:T(8,128)(2,1)S(1)}, u32[]{:S(2)}, u32[]{:S(2)}) collective-permute-start(bf16[1024,768]{1,0:T(8,128)(2,1)S(1)} %select_bitcast_fusion), channel_id=1, source_target_pairs={{0,16},{16,0},{1,17},{17,1},{2,18},{18,2},{3,19},{19,3},{4,20},{20... | collective-permute-start | bytes 4718600 | tf_op jit(solution)/shard_map/ppermute | solution.py:22
  130.0 3.0 %collective-permute-done.1 = bf16[1024,768]{1,0:T(8,128)(2,1)S(1)} collective-permute-done((bf16[1024,768]{1,0:T(8,128)(2,1)S(1)}, bf16[1024,768]{1,0:T(8,128)(2,1)S(1)}, u32[]{:S(2)}, u32[]{:S(2)}) %collective-permute-start.1) | collective-permute-done | bytes 1572896 | tf_op jit(solution)/shard_map/ppermute | solution.py:22
  133.6 22.9 %all_to_all.62 = bf16[4,256,768]{2,1,0:T(8,128)(2,1)S(1)} all-to-all(bf16[4,256,768]{2,1,0:T(8,128)(2,1)S(1)} %bitcast.222), channel_id=1, replica_groups=mesh['x'=4,'zh'=4,'co'=2,'y'=4,'zl'=4] {'x'}, dimensions={0} | all-to-all | bytes 3145728 | tf_op jit(solution)/shard_map/all_to_all | solution.py:18
  156.9 28.0 %all_to_all.63 = bf16[4,64,768]{2,1,0:T(8,128)(2,1)S(1)} all-to-all(bf16[4,64,768]{2,1,0:T(8,128)(2,1)S(1)} %bitcast.228), channel_id=1, replica_groups=mesh['x'=4,'zh'=4,'co'=2,'y'=4,'zl'=4] {'zh'}, dimensions={0} | all-to-all | bytes 786432 | tf_op jit(solution)/shard_map/all_to_all | solution.py:18
  185.0 16.8 %all_gather.7 = bf16[256,512]{1,0:T(8,128)(2,1)S(1)} all-gather(bf16[64,512]{1,0:T(8,128)(2,1)S(1)} %slice.94), channel_id=1, replica_groups=mesh['x'=4,'zh'=4,'co'=2,'y'=4,'zl'=4] {'zh'}, dimensions={0}, use_global_device_ids=true | all-gather | bytes 327680 | tf_op jit(solution)/shard_map/all_gather | solution.py:109
  202.0 12.2 %all_to_all.64 = bf16[4,256,512]{1,2,0:T(8,128)(2,1)S(1)} all-to-all(bf16[4,256,512]{1,2,0:T(8,128)(2,1)S(1)} %broadcast_in_dim.78), channel_id=1, replica_groups=mesh['x'=4,'zh'=4,'co'=2,'y'=4,'zl'=4] {'x'}, dimensions={0} | all-to-all | bytes 2097152 | tf_op jit(solution)/shard_map/all_to_all | solution.py:14
  214.7 8.4 %collective-permute-start.2 = (bf16[1024,512]{1,0:T(8,128)(2,1)S(1)}, bf16[1024,512]{1,0:T(8,128)(2,1)S(1)}, u32[]{:S(2)}, u32[]{:S(2)}) collective-permute-start(bf16[1024,512]{1,0:T(8,128)(2,1)S(1)} %bitcast.223), channel_id=1, source_target_pairs={{0,16},{16,0},{1,17},{17,1},{2,18},{18,2},{3,19},{19,3},{4,20},{20... | collective-permute-start | bytes 3145736 | tf_op jit(solution)/shard_map/ppermute | solution.py:22
  223.9 3.3 %all-to-all-start.10 = ((bf16[4,64,256]{2,1,0:T(8,128)(2,1)}), bf16[4,64,256]{2,1,0:T(8,128)(2,1)S(1)}, u32[]{:S(2)}, u32[]{:S(2)}) async-start(bf16[4,64,256]{2,1,0:T(8,128)(2,1)} %broadcast_in_dim.79), calls=%async_computation.10 | async-start | bytes 262144 | tf_op jit(solution)/shard_map/all_to_all | solution.py:14
  228.0 4.3 %all-to-all-done.10 = bf16[4,64,256]{2,1,0:T(8,128)(2,1)S(1)} async-done(((bf16[4,64,256]{2,1,0:T(8,128)(2,1)}), bf16[4,64,256]{2,1,0:T(8,128)(2,1)S(1)}, u32[]{:S(2)}, u32[]{:S(2)}) %all-to-all-start.10) | async-done | bytes 131104 | tf_op jit(solution)/shard_map/all_to_all | solution.py:14
  232.3 5.9 %all-to-all-start.6 = ((bf16[4,64,128]{2,1,0:T(8,128)(2,1)}), bf16[4,64,128]{2,1,0:T(8,128)(2,1)S(1)}, u32[]{:S(2)}, u32[]{:S(2)}) async-start(bf16[4,64,128]{2,1,0:T(8,128)(2,1)} %bitcast.42), calls=%async_computation.6 | async-start | bytes 131072 | tf_op jit(solution)/shard_map/all_to_all | solution.py:18
  238.2 4.6 %all-to-all-done.6 = bf16[4,64,128]{2,1,0:T(8,128)(2,1)S(1)} async-done(((bf16[4,64,128]{2,1,0:T(8,128)(2,1)}), bf16[4,64,128]{2,1,0:T(8,128)(2,1)S(1)}, u32[]{:S(2)}, u32[]{:S(2)}) %all-to-all-start.6) | async-done | bytes 65568 | tf_op jit(solution)/shard_map/all_to_all | solution.py:18
  243.5 3.3 %all-to-all-start.11 = ((bf16[4,64,256]{2,1,0:T(8,128)(2,1)}), bf16[4,64,256]{2,1,0:T(8,128)(2,1)S(1)}, u32[]{:S(2)}, u32[]{:S(2)}) async-start(bf16[4,64,256]{2,1,0:T(8,128)(2,1)} %broadcast_in_dim.80), calls=%async_computation.11 | async-start | bytes 262144 | tf_op jit(solution)/shard_map/all_to_all | solution.py:14
  246.8 2.5 fusion.4
  249.9 1.6 all-to-all-done.11
  252.4 1.5 fusion.18
  (96 shorter events, 24.5 us)
Async XLA Ops:
  0.6 68.9 %copy-start = (bf16[1,128,2048]{2,1,0:T(8,128)(2,1)S(1)}, bf16[1,128,2048]{2,1,0:T(8,128)(2,1)}, u32[]{:S(2)}) copy-start(bf16[1,128,2048]{2,1,0:T(8,128)(2,1)} %param.8) | copy-start | bytes 1572868
  49.5 10.5 %collective-permute-start = (bf16[16,64,768]{2,1,0:T(8,128)(2,1)S(1)}, bf16[16,64,768]{2,1,0:T(8,128)(2,1)}, u32[]{:S(2)}, u32[]{:S(2)}) collective-permute-start(bf16[16,64,768]{2,1,0:T(8,128)(2,1)S(1)} %bitcast.220), channel_id=1, source_target_pairs={{0,16},{16,0},{1,17},{17,1},{2,18},{18,2},{3,19},{19,3},{4,20},{20... | collective-permute-start | bytes 4718600 | tf_op jit(solution)/shard_map/ppermute | solution.py:22
  61.5 1.0 copy-start.6
  61.6 2.0 copy-start.5
  61.9 1.7 copy-start.1
  61.9 6.6 %copy-start.11 = (s32[1,16]{1,0:T(1,128)S(1)}, s32[1,16]{1,0:T(1,128)}, u32[]{:S(2)}) copy-start(s32[1,16]{1,0:T(1,128)} %param.9) | copy-start | bytes 196
  64.6 10.8 %all-to-all-start.2 = ((bf16[4,64,512]{2,1,0:T(8,128)(2,1)}), bf16[4,64,512]{2,1,0:T(8,128)(2,1)S(1)}, u32[]{:S(2)}, u32[]{:S(2)}) async-start(bf16[4,64,512]{2,1,0:T(8,128)(2,1)} %broadcast_in_dim.35), calls=%async_computation.2 | async-start | bytes 524288 | tf_op jit(solution)/shard_map/all_to_all | solution.py:14
  76.1 9.7 %all-to-all-start.1 = ((bf16[4,128,256]{2,1,0:T(8,128)(2,1)}), bf16[4,128,256]{2,1,0:T(8,128)(2,1)S(1)}, u32[]{:S(2)}, u32[]{:S(2)}) async-start(bf16[4,128,256]{2,1,0:T(8,128)(2,1)} %broadcast_in_dim.34), calls=%async_computation.1 | async-start | bytes 524288 | tf_op jit(solution)/shard_map/all_to_all | solution.py:14
  80.3 5.9 %copy-start.9 = (bf16[4,8,2,8,128]{4,3,2,1,0:T(8,128)(2,1)}, bf16[4,8,2,8,128]{4,3,2,1,0:T(8,128)(2,1)S(1)}, u32[]{:S(2)}) copy-start(bf16[4,8,2,8,128]{4,3,2,1,0:T(8,128)(2,1)S(1)} %get-tuple-element.48) | copy-start | bytes 393220
  80.3 6.3 %copy-start.7 = (bf16[4,8,2,8,128]{4,3,2,1,0:T(8,128)(2,1)}, bf16[4,8,2,8,128]{4,3,2,1,0:T(8,128)(2,1)S(1)}, u32[]{:S(2)}) copy-start(bf16[4,8,2,8,128]{4,3,2,1,0:T(8,128)(2,1)S(1)} %get-tuple-element.49) | copy-start | bytes 393220
  86.7 8.4 %copy-start.4 = (f32[512,4,64,2]{0,2,3,1:T(8,128)}, f32[512,4,64,2]{0,2,3,1:T(8,128)S(1)}, u32[]{:S(2)}) copy-start(f32[512,4,64,2]{0,2,3,1:T(8,128)S(1)} %get-tuple-element.55) | copy-start | bytes 3145732
  96.1 9.0 %all-to-all-start.4 = ((bf16[4,64,512]{2,1,0:T(8,128)(2,1)}), bf16[4,64,512]{2,1,0:T(8,128)(2,1)S(1)}, u32[]{:S(2)}, u32[]{:S(2)}) async-start(bf16[4,64,512]{2,1,0:T(8,128)(2,1)} %pad_maximum_fusion.4), calls=%async_computation.4 | async-start | bytes 524288 | tf_op jit(solution)/shard_map/all_to_all | solution.py:18
  99.5 1.8 copy-start.10
  101.1 0.9 copy-start.8
  108.1 10.4 %all-to-all-start.5 = ((bf16[4,256,256]{1,2,0:T(8,128)(2,1)}), bf16[4,256,256]{1,2,0:T(8,128)(2,1)S(1)}, u32[]{:S(2)}, u32[]{:S(2)}) async-start(bf16[4,256,256]{1,2,0:T(8,128)(2,1)} %pad_maximum_fusion.3), calls=%async_computation.5 | async-start | bytes 1048576 | tf_op jit(solution)/shard_map/all_to_all | solution.py:18
  119.5 1.2 copy-start.2
  119.6 1.5 copy-start.3
  121.5 11.5 %collective-permute-start.1 = (bf16[1024,768]{1,0:T(8,128)(2,1)S(1)}, bf16[1024,768]{1,0:T(8,128)(2,1)S(1)}, u32[]{:S(2)}, u32[]{:S(2)}) collective-permute-start(bf16[1024,768]{1,0:T(8,128)(2,1)S(1)} %select_bitcast_fusion), channel_id=1, source_target_pairs={{0,16},{16,0},{1,17},{17,1},{2,18},{18,2},{3,19},{19,3},{4,20},{20... | collective-permute-start | bytes 4718600 | tf_op jit(solution)/shard_map/ppermute | solution.py:22
  214.7 37.5 %collective-permute-start.2 = (bf16[1024,512]{1,0:T(8,128)(2,1)S(1)}, bf16[1024,512]{1,0:T(8,128)(2,1)S(1)}, u32[]{:S(2)}, u32[]{:S(2)}) collective-permute-start(bf16[1024,512]{1,0:T(8,128)(2,1)S(1)} %bitcast.223), channel_id=1, source_target_pairs={{0,16},{16,0},{1,17},{17,1},{2,18},{18,2},{3,19},{19,3},{4,20},{20... | collective-permute-start | bytes 3145736 | tf_op jit(solution)/shard_map/ppermute | solution.py:22
  223.9 8.4 %all-to-all-start.10 = ((bf16[4,64,256]{2,1,0:T(8,128)(2,1)}), bf16[4,64,256]{2,1,0:T(8,128)(2,1)S(1)}, u32[]{:S(2)}, u32[]{:S(2)}) async-start(bf16[4,64,256]{2,1,0:T(8,128)(2,1)} %broadcast_in_dim.79), calls=%async_computation.10 | async-start | bytes 262144 | tf_op jit(solution)/shard_map/all_to_all | solution.py:14
  232.3 10.5 %all-to-all-start.6 = ((bf16[4,64,128]{2,1,0:T(8,128)(2,1)}), bf16[4,64,128]{2,1,0:T(8,128)(2,1)S(1)}, u32[]{:S(2)}, u32[]{:S(2)}) async-start(bf16[4,64,128]{2,1,0:T(8,128)(2,1)} %bitcast.42), calls=%async_computation.6 | async-start | bytes 131072 | tf_op jit(solution)/shard_map/all_to_all | solution.py:18
  243.5 8.1 %all-to-all-start.11 = ((bf16[4,64,256]{2,1,0:T(8,128)(2,1)}), bf16[4,64,256]{2,1,0:T(8,128)(2,1)S(1)}, u32[]{:S(2)}, u32[]{:S(2)}) async-start(bf16[4,64,256]{2,1,0:T(8,128)(2,1)} %broadcast_in_dim.80), calls=%async_computation.11 | async-start | bytes 262144 | tf_op jit(solution)/shard_map/all_to_all | solution.py:14

commit v2 on v1

v2 whole, which is shorter than its diff:
```python
import jax
import jax.numpy as jnp
from jax import lax
from jax.experimental import pallas as pl
from jax.experimental.pallas import tpu as pltpu
from jax.sharding import Mesh, PartitionSpec as P

HD = 128
PT = 128
SCALE = HD ** (-0.5)
f32 = jnp.float32
bf16 = jnp.bfloat16


def spread(block, axis):
    copies = jnp.broadcast_to(block[None], (4,) + block.shape)
    return lax.all_to_all(copies, axis, 0, 0)


def exchange(parts, axis):
    return jnp.sum(lax.all_to_all(parts, axis, 0, 0).astype(f32), 0).astype(bf16)


def swap(block):
    return lax.ppermute(block, "co", [(0, 1), (1, 0)])


def meet(block, axis, bit):
    return lax.ppermute(block, axis, [(i, i ^ bit) for i in range(4)])


def join(keep, moved):
    return (keep.astype(f32) + moved.astype(f32)).astype(bf16)


def halve(parts, axis):
    me = lax.axis_index(axis)
    high, low = me // 2, lax.rem(me, 2)
    keep = lax.dynamic_slice_in_dim(parts, 2 * high, 2, 0)
    send = lax.dynamic_slice_in_dim(parts, 2 - 2 * high, 2, 0)
    two = join(keep, meet(send, axis, 2))
    keep = lax.dynamic_index_in_dim(two, low, 0, keepdims=False)
    send = lax.dynamic_index_in_dim(two, 1 - low, 0, keepdims=False)
    return join(keep, meet(send, axis, 1))


def together(*arrays):
    return lax.optimization_barrier(arrays)


def outer(left, right):
    return lax.dot_general(left, right, (((0,), (0,)), ((), ())), preferred_element_type=f32)


def rows_by_rows(left, right):
    return lax.dot_general(left, right, (((1,), (1,)), ((), ())), preferred_element_type=f32)


def attend(lengths, qa, kv):
    heads = [(z, c) for z in range(4) for c in range(2)]
    q = jnp.concatenate([qa[z, :, c * HD : c * HD + HD] for z, c in heads], 0)
    g = jnp.concatenate([qa[z, :, 256 + c * HD : 256 + c * HD + HD] for z, c in heads], 0)
    token = lax.broadcasted_iota(jnp.int32, (1, 512), 1)
    limit = jnp.full((1, 512), lengths[3], jnp.int32)
    for y in range(2, -1, -1):
        limit = jnp.where(token < PT * (y + 1), lengths[y], limit)
    valid = (token & (PT - 1)) < limit
    scores = rows_by_rows(q, kv[:, :HD]) * SCALE
    weights = jnp.where(valid, jnp.exp(scores), 0.0)
    return q, g, weights, rows_by_rows(g, kv[:, HD:])


def forward_kernel(lengths, qa, kv, out):
    _, _, weights, dprob = attend(lengths, qa, kv)
    total = jnp.sum(weights, -1, keepdims=True)
    probs = weights * (1.0 / jnp.where(total > 0, total, 1.0))
    delta = jnp.sum(probs * dprob, -1, keepdims=True)
    centred = (probs * (dprob - delta)).astype(bf16)
    plain = jnp.dot(probs.astype(bf16), kv[...], preferred_element_type=f32).astype(bf16)
    slope = jnp.dot(centred, kv[:, :HD], preferred_element_type=f32).astype(bf16)
    lane = lax.broadcasted_iota(jnp.int32, (64, 128), 1)
    stats = jnp.zeros((64, 128), f32)
    columns = []
    for h in range(8):
        rows = slice(64 * h, 64 * h + 64)
        for value in (total[rows], delta[rows]):
            high = value.astype(bf16).astype(f32)
            columns += [high, value - high]
    for k, column in enumerate(columns):
        stats = jnp.where(lane == k, column, stats)
    for z in range(4):
        own = stats
        for k in range(8):
            own = jnp.where(lane == 32 + k, columns[8 * z + k], own)
        for c in range(2):
            rows = slice(128 * z + 64 * c, 128 * z + 64 * c + 64)
            out[z, :, c * HD : c * HD + HD] = slope[rows]
            out[z, :, 256 + c * HD : 256 + c * HD + HD] = plain[rows, :HD]
            out[z, :, 512 + c * HD : 512 + c * HD + HD] = plain[rows, HD:]
        out[z, :, 768:] = own.astype(bf16)


def combine(stats, k):
    totals = [s[:, k : k + 1] + s[:, k + 1 : k + 2] for s in stats]
    deltas = [s[:, k + 2 : k + 3] + s[:, k + 3 : k + 4] for s in stats]
    total = totals[0] + totals[1] + totals[2] + totals[3]
    shares = [t / total for t in totals]
    delta = sum(share * d for share, d in zip(shares, deltas))
    return total, delta, shares, deltas


def backward_kernel(lengths, moved, qa, kv, heads, kv_part):
    stats = [moved[i, :, 768:].astype(f32) for i in range(4)]
    for c in range(2):
        _, delta, shares, deltas = combine(stats, 32 + 4 * c)
        mixed = jnp.zeros((64, HD), f32)
        grad = jnp.zeros((64, HD), f32)
        for i in range(4):
            slope, key_mean, value_mean = (
                moved[i, :, at + c * HD : at + c * HD + HD].astype(f32) for at in (0, 256, 512)
            )
            mixed = mixed + shares[i] * value_mean
            grad = grad + shares[i] * (slope + (deltas[i] - delta) * key_mean)
        heads[:64, c * HD : c * HD + HD] = mixed.astype(bf16)
        heads[64:, c * HD : c * HD + HD] = (grad * SCALE).astype(bf16)
    pairs = [combine(stats, 4 * h)[:2] for h in range(8)]
    total = jnp.concatenate([pair[0] for pair in pairs], 0)
    delta = jnp.concatenate([pair[1] for pair in pairs], 0)
    q, g, weights, dprob = attend(lengths, qa, kv)
    probs = weights * (1.0 / total)
    dscore = (probs * (dprob - delta) * SCALE).astype(bf16)
    key_part = outer(dscore, q).astype(bf16)
    value_part = outer(probs.astype(bf16), g).astype(bf16)
    kv_part[:, :HD] = key_part
    kv_part[:, HD:] = value_part


def key_term_kernel(core, kv_part, enc, keep, send):
    term = outer(enc[...], kv_part[...]).astype(bf16).reshape(16, 2, 64, 256)
    at_first = core[0] == 0
    keep[...] = jnp.where(at_first, term[:, 0], term[:, 1])
    send[...] = jnp.where(at_first, term[:, 1], term[:, 0])


def head_term_kernel(sources, moved, own, second, third, fourth, keep, send, kv_sum):
    q_term = o_term = jnp.zeros((512, 256), f32)
    kv_total = jnp.zeros((256, 256), f32)
    for step, rows in enumerate((own, second, third, fourth)):
        block = moved[sources[1 + step]]
        o_term = o_term + outer(rows[:, 512:], block[:64])
        q_term = q_term + outer(rows[:, :512], block[64:128])
        kv_total = kv_total + block[128:].astype(f32)
    term = jnp.concatenate([q_term, o_term], 1).astype(bf16)
    at_first = sources[0] == 0
    keep[...] = jnp.where(at_first, term[:256], term[256:])
    send[...] = jnp.where(at_first, term[256:], term[:256])
    kv_sum[...] = kv_total.astype(bf16)


def place_kernel(core, mine, theirs, q_out, o_out):
    at_first = core[0] == 0
    for half in range(2):
        block = jnp.where(at_first == (half == 0), mine[0], theirs[0])
        q_out[256 * half : 256 * half + 256, :] = block[:, :256].astype(f32)
        o_out[:, 256 * half : 256 * half + 256] = block[:, 256:].T


PARAMS = pltpu.CompilerParams(vmem_limit_bytes=16 * 1024 * 1024)
SCALARS = pl.BlockSpec(memory_space=pltpu.SMEM)


def call(kernel, outs, scalars, *arrays):
    vmem = pl.BlockSpec(memory_space=pltpu.VMEM)
    return pl.pallas_call(
        kernel,
        out_shape=[jax.ShapeDtypeStruct(shape, bf16) for shape in outs],
        in_specs=[SCALARS] + [vmem] * len(arrays),
        out_specs=[vmem] * len(outs),
        compiler_params=PARAMS,
    )(scalars, *arrays)


def place(core, mine, theirs):
    block = pl.BlockSpec((1, 256, 512), lambda i: (i, 0, 0))
    return pl.pallas_call(
        place_kernel,
        grid=(4,),
        out_shape=[
            jax.ShapeDtypeStruct((2048, 256), f32),
            jax.ShapeDtypeStruct((256, 2048), bf16),
        ],
        in_specs=[SCALARS, block, block],
        out_specs=[
            pl.BlockSpec((512, 256), lambda i: (i, 0)),
            pl.BlockSpec((256, 512), lambda i: (0, i)),
        ],
        compiler_params=PARAMS,
    )(core, mine, theirs)


def local(dec_states, enc_states, passage_lengths, q_weight, kv_weight, o_weight, out_grad):
    dec_rows = dec_states[0]
    enc_rows = enc_states[0]
    grad_rows = out_grad[0]
    core = lax.axis_index("co").astype(jnp.int32).reshape(1)
    first_core = lax.axis_index("co") == 0
    zl = lax.axis_index("zl")
    lengths = lax.dynamic_index_in_dim(passage_lengths[0].reshape(4, 4), zl, 1, keepdims=False)

    enc_four = spread(enc_rows, "y").reshape(512, 2048)

    shard = jnp.concatenate([q_weight, kv_weight, o_weight.T], 1)
    own = lax.all_gather(shard, "zh", axis=0, tiled=True)
    own, enc_four = together(own, enc_four)
    own = spread(own, "x").reshape(16, 64, 768)
    other = swap(own)
    weights_all = jnp.stack(
        [jnp.where(first_core, own, other), jnp.where(first_core, other, own)], 1
    ).reshape(2048, 768)
    wq_full = weights_all[:, :256]
    wkv_full = weights_all[:, 256:512]
    wo_t = weights_all[:, 512:]

    queries = jnp.dot(dec_rows, wq_full, preferred_element_type=f32).astype(bf16)
    attn_grad = jnp.dot(grad_rows, wo_t, preferred_element_type=f32).astype(bf16)

    qa_all = spread(jnp.concatenate([queries, attn_grad], 1), "zl")
    kv_all = jnp.dot(enc_four, wkv_full, preferred_element_type=f32).astype(bf16)
    (parts,) = call(forward_kernel, [(4, 64, 896)], lengths, qa_all, kv_all)

    quarters = jnp.stack(
        [
            jnp.concatenate([dec_rows[:, at : at + 512], grad_rows[:, at : at + 512]], 1)
            for at in range(0, 2048, 512)
        ]
    )
    parts, quarters = together(parts, quarters)
    moved = lax.all_to_all(parts, "zl", 0, 0)
    x = lax.axis_index("x")
    rows_x = [lax.dynamic_index_in_dim(quarters, x, 0, keepdims=False)]
    for step in range(1, 4):
        part = lax.dynamic_index_in_dim(quarters, lax.rem(x + step, 4), 0, keepdims=False)
        rows_x.append(lax.ppermute(part, "x", [(i, (i + step) % 4) for i in range(4)]))
    moved, *rows_x = together(moved, *rows_x)
    heads, kv_part = call(backward_kernel, [(128, 256), (512, 256)], lengths, moved, qa_all, kv_all)

    keep, send = call(key_term_kernel, [(16, 64, 256)] * 2, core, kv_part, enc_four)
    kv_chip = join(keep, swap(send)).reshape(4, 256, 256)
    messages = jnp.concatenate([jnp.broadcast_to(heads[None], (4, 128, 256)), kv_chip], 1)
    moved_x = lax.all_to_all(messages, "x", 0, 0)
    sources = jnp.concatenate([core] + [lax.rem(x + 4 - step, 4).reshape(1) for step in range(4)])
    keep, send, kv_sum = call(
        head_term_kernel, [(256, 512), (256, 512), (256, 256)], sources, moved_x, *rows_x
    )
    sum_x = jnp.concatenate([join(keep, swap(send)), kv_sum], 1)
    parts_z = sum_x.reshape(4, 64, 768)

    dec_part = jnp.dot(heads[64:], wq_full.T, preferred_element_type=f32).astype(bf16)
    dec_part = dec_part.reshape(64, 4, 2, 256).transpose(1, 2, 0, 3).reshape(4, 128, 256)
    y_sum = halve(jnp.concatenate([kv_part.reshape(4, PT, 256), dec_part], 1), "y")
    kv_grad = y_sum[:PT]
    dec_y = y_sum[PT:].reshape(2, 64, 2, 128).transpose(0, 2, 1, 3).reshape(4, 64, 128)
    dec_grad = halve(dec_y, "zl")
    enc_grad = jnp.dot(kv_grad, wkv_full.T, preferred_element_type=f32).astype(bf16)

    sum_z = exchange(parts_z, "zh")
    sum_z, dec_grad, enc_grad = together(sum_z, dec_grad, enc_grad)

    kv_y = jnp.sum(spread(sum_z[:, 512:], "y").astype(f32), 0).astype(bf16)
    mine = lax.all_gather(sum_z[:, :512], "zh", axis=0, tiled=True)
    mine, kv_y = together(mine, kv_y)
    mine = spread(mine, "x")
    kv_weight_grad = jnp.sum(lax.all_gather(kv_y, "zl", axis=0).astype(f32), 0)
    mine, kv_weight_grad = together(mine, kv_weight_grad)
    q_weight_grad, o_weight_grad = place(core, mine, swap(mine))
    return (dec_grad[None], enc_grad[None], q_weight_grad, kv_weight_grad, o_weight_grad)


def solution(mesh):
    fine = Mesh(mesh.devices.reshape(4, 4, 2, 4, 4), ("x", "zh", "co", "y", "zl"))
    pb = ("x", "zh", "co")
    row = ("y", "zl")
    placed = (
        P(pb, None, None),
        P(pb, row, None),
        P(pb, None),
        P(pb, row),
        P(pb, None),
        P(row, pb),
        P(pb, None, None),
    )
    return jax.shard_map(
        local,
        mesh=fine,
        in_specs=placed,
        out_specs=(
            P(pb, None, row),
            P(pb, row, None),
            P(None, row),
            P(pb, None),
            P(row, None),
        ),
        check_vma=False,
    )
```

time: 258 us -> 232 us (0.90)
  blocking collectives: 135 us -> 81.6 us
  starting transfers between devices: 51.3 us -> 86.4 us
  Pallas kernels: 0 us -> 9.35 us
  waiting for transfers between devices: 32.4 us -> 27.7 us
  other arithmetic: 11.3 us -> 7.39 us
  local copies, waits for them, and re-layouts: 14 us -> 10.8 us
  matrix products: 9.79 us -> 6.67 us
    all_to_all x2 -> x0, blocking collectives: 50.9 us -> none  [exchange(): return jnp.sum(lax.all_to_all(parts, axis, 0, 0).astype(f32), 0)]
    ppermute x0 -> x7, starting transfers between devices: none -> 24.3 us  [the longest x4 15.9 us: meet(): return lax.ppermute(block, axis, [(i, i ^ bit) for i in range(4)])]
    all_to_all x3 -> x1, blocking collectives: 39.9 us -> 18.8 us  [spread(): return lax.all_to_all(copies, axis, 0, 0)]
    all_gather x1 -> x2, blocking collectives: 16.8 us -> 37.3 us  [the longest x1 25.5 us: local(): mine = lax.all_gather(sum_z[:, :512], 'zh', axis=0, tiled=True)]
    ppermute x0 -> x7, waiting for transfers between devices: none -> 12.4 us  [the longest x4 9.79 us: meet(): return lax.ppermute(block, axis, [(i, i ^ bit) for i in range(4)])]
    all_to_all x4, waiting for transfers between devices: 15.4 us -> 3.1 us  [spread(): return lax.all_to_all(copies, axis, 0, 0)]
    pallas_call x0 -> x5, Pallas kernels: none -> 9.35 us  [the longest x4 7.12 us: call(): pl.pallas_call(kernel, out_shape=[jax.ShapeDtypeStruct(shape, bf16) for s...]
    all_to_all x3, waiting for transfers between devices: 10.8 us -> 4.98 us  [the longest x1 4.98 us: local(): moved_x = lax.all_to_all(messages, 'x', 0, 0)]
  transfers between devices with their start and end apart: 10 -> 18, of which waited for: 9 -> 8; matrix products, arithmetic and copies ran while one was open for 6% -> 5% of each run, Pallas kernels for 0% -> 1%
where the time goes in v2:
time: 232 us; the launch traced here: 231 us
  starting transfers between devices  86.4 us (37%)
  blocking collectives  81.6 us (35%)
  waiting for transfers between devices  27.7 us (12%)
  local copies, waits for them, and re-layouts  10.8 us (5%)
  Pallas kernels  9.35 us (4%)
  other arithmetic  7.39 us (3%)
  matrix products  6.67 us (3%)
    ppermute x4, starting transfers between devices, swap(): return lax.ppermute(block, 'co', [(0, 1), (1, 0)])  26.2 us
    all_gather x1, blocking collectives, local(): own = lax.all_gather(shard, 'zh', axis=0, tiled=True)  25.5 us
    all_gather x1, blocking collectives, local(): mine = lax.all_gather(sum_z[:, :512], 'zh', axis=0, tiled=True)  25.5 us
    all_to_all x1, blocking collectives, spread(): return lax.all_to_all(copies, axis, 0, 0)  18.8 us
    all_to_all x4, starting transfers between devices, spread(): return lax.all_to_all(copies, axis, 0, 0)  17.5 us
    ppermute x4, starting transfers between devices, meet(): return lax.ppermute(block, axis, [(i, i ^ bit) for i in range(4)])  15.9 us
    all_gather x1, blocking collectives, local(): kv_weight_grad = jnp.sum(lax.all_gather(kv_y, 'zl', axis=0).astype(f32), 0)  11.9 us
    all_to_all x1, starting transfers between devices, exchange(): lax.all_to_all(parts, axis, 0, 0).astype(f32)  11.3 us
  transfers between devices with their start and end apart: 18, of which 8 were waited for; matrix products, arithmetic and copies ran while one was open for 5% of the time, Pallas kernels for 1%

profile of v2, /device:TPU:1, one launch (start us, length us, event | category | flops | bytes accessed | tf_op | source)
XLA Modules:
  0.0 231.2 jit_solution(1880039071360694720)
XLA Ops:
  0.6 2.6 %broadcast_in_dim.19 = bf16[4,128,2048]{2,1,0:T(8,128)(2,1)} broadcast(bf16[128,2048]{1,0:T(8,128)(2,1)} %bitcast.78), dimensions={1,2} | broadcast | bytes 2621440 | tf_op jit(solution)/shard_map/broadcast_in_dim | solution.py:16
  3.3 5.1 %all-to-all-start = ((bf16[4,128,2048]{2,1,0:T(8,128)(2,1)}), bf16[4,128,2048]{2,1,0:T(8,128)(2,1)S(1)}, u32[]{:S(2)}, u32[]{:S(2)}) async-start(bf16[4,128,2048]{2,1,0:T(8,128)(2,1)} %broadcast_in_dim.19), calls=%async_computation | async-start | bytes 4194304 | tf_op jit(solution)/shard_map/all_to_all | solution.py:17
  8.4 25.5 %all_gather.12 = bf16[256,768]{1,0:T(8,128)(2,1)S(1)} all-gather(bf16[64,768]{1,0:T(8,128)(2,1)S(1)} %pad_maximum_fusion.4), channel_id=1, replica_groups=mesh['x'=4,'zh'=4,'co'=2,'y'=4,'zl'=4] {'zh'}, dimensions={0}, use_global_device_ids=true | all-gather | bytes 491520 | tf_op jit(solution)/shard_map/all_gather | solution.py:213
  34.0 18.8 %all_to_all.40 = bf16[4,256,768]{2,1,0:T(8,128)(2,1)} all-to-all(bf16[4,256,768]{2,1,0:T(8,128)(2,1)S(1)} %broadcast_in_dim.20), channel_id=1, replica_groups=mesh['x'=4,'zh'=4,'co'=2,'y'=4,'zl'=4] {'x'}, dimensions={0} | all-to-all | bytes 3145728 | tf_op jit(solution)/shard_map/all_to_all | solution.py:17
  52.8 8.7 %collective-permute-start = (bf16[16,64,768]{2,1,0:T(8,128)(2,1)}, bf16[16,64,768]{2,1,0:T(8,128)(2,1)}, u32[]{:S(2)}, u32[]{:S(2)}) collective-permute-start(bf16[16,64,768]{2,1,0:T(8,128)(2,1)} %bitcast.8), channel_id=1, source_target_pairs={{0,16},{16,0},{1,17},{17,1},{2,18},{18,2},{3,19},{19,3},{4,20},{20... | collective-permute-start | bytes 4718600 | tf_op jit(solution)/shard_map/ppermute | solution.py:25
  61.6 3.3 %collective-permute-done = bf16[16,64,768]{2,1,0:T(8,128)(2,1)} collective-permute-done((bf16[16,64,768]{2,1,0:T(8,128)(2,1)}, bf16[16,64,768]{2,1,0:T(8,128)(2,1)}, u32[]{:S(2)}, u32[]{:S(2)}) %collective-permute-start) | collective-permute-done | bytes 1572896 | tf_op jit(solution)/shard_map/ppermute | solution.py:25
  64.9 2.1 select_bitcast_fusion.1
  69.9 5.5 %all-to-all-start.2 = ((bf16[4,64,512]{2,1,0:T(8,128)(2,1)}), bf16[4,64,512]{2,1,0:T(8,128)(2,1)S(1)}, u32[]{:S(2)}, u32[]{:S(2)}) async-start(bf16[4,64,512]{2,1,0:T(8,128)(2,1)} %broadcast_in_dim.21), calls=%async_computation.2 | async-start | bytes 524288 | tf_op jit(solution)/shard_map/all_to_all | solution.py:17
  79.8 3.1 %all-to-all-done.2.qa = bf16[4,64,512]{2,1,0:T(8,128)(2,1)S(1)} async-done(((bf16[4,64,512]{2,1,0:T(8,128)(2,1)}), bf16[4,64,512]{2,1,0:T(8,128)(2,1)S(1)}, u32[]{:S(2)}, u32[]{:S(2)}) %all-to-all-start.2) | async-done | bytes 262176 | tf_op jit(solution)/shard_map/all_to_all | solution.py:17
  82.9 2.3 %shard_map.110 = bf16[4,64,896]{2,1,0:T(8,128)(2,1)} custom-call(s32[4]{0:T(128)S(1)} %fusion.13.lengths, bf16[4,64,512]{2,1,0:T(8,128)(2,1)S(1)} %all-to-all-done.2.qa, bf16[512,256]{1,0:T(8,128)(2,1)S(1)} %convolution_convert_fusion.2.kv), custom_call_target="tpu_custom_call" | custom-call | tf_op jit(solution)/shard_map/pallas_call | solution.py:174
  85.2 3.5 %all-to-all-start.3 = ((bf16[4,64,896]{2,1,0:T(8,128)(2,1)}), bf16[4,64,896]{2,1,0:T(8,128)(2,1)S(1)}, u32[]{:S(2)}, u32[]{:S(2)}) async-start(bf16[4,64,896]{2,1,0:T(8,128)(2,1)} %shard_map.110), calls=%async_computation.3 | async-start | bytes 917504 | tf_op jit(solution)/shard_map/all_to_all | solution.py:238
  89.9 2.2 collective-permute-start.1
  92.1 3.7 %collective-permute-start.2 = (bf16[64,1024]{1,0:T(8,128)(2,1)S(1)}, bf16[64,1024]{1,0:T(8,128)(2,1)S(1)}, u32[]{:S(2)}, u32[]{:S(2)}) collective-permute-start(bf16[64,1024]{1,0:T(8,128)(2,1)S(1)} %get-tuple-element.58), channel_id=1, source_target_pairs={{0,256},{128,384},{256,0},{384,128},{1,257},{129,385},{257,1},{385... | collective-permute-start | bytes 393224 | tf_op jit(solution)/shard_map/ppermute | solution.py:243
  95.8 2.5 %collective-permute-start.3 = (bf16[64,1024]{1,0:T(8,128)(2,1)S(1)}, bf16[64,1024]{1,0:T(8,128)(2,1)S(1)}, u32[]{:S(2)}, u32[]{:S(2)}) collective-permute-start(bf16[64,1024]{1,0:T(8,128)(2,1)S(1)} %get-tuple-element.57), channel_id=1, source_target_pairs={{0,384},{128,0},{256,128},{384,256},{1,385},{129,1},{257,129},{385... | collective-permute-start | bytes 393224 | tf_op jit(solution)/shard_map/ppermute | solution.py:243
  106.3 5.3 %collective-permute-start.4 = (bf16[16,64,256]{2,1,0:T(8,128)(2,1)}, bf16[16,64,256]{2,1,0:T(8,128)(2,1)S(1)}, u32[]{:S(2)}, u32[]{:S(2)}) collective-permute-start(bf16[16,64,256]{2,1,0:T(8,128)(2,1)} %get-tuple-element.38), channel_id=1, source_target_pairs={{0,16},{16,0},{1,17},{17,1},{2,18},{18,2},{3,19},{19,3},{4,20},{20... | collective-permute-start | bytes 1572872 | tf_op jit(solution)/shard_map/ppermute | solution.py:25
  114.5 3.6 %all-to-all-start.4 = ((bf16[4,384,256]{2,1,0:T(8,128)(2,1)}), bf16[4,384,256]{2,1,0:T(8,128)(2,1)S(1)}, u32[]{:S(2)}, u32[]{:S(2)}) async-start(bf16[4,384,256]{2,1,0:T(8,128)(2,1)} %pad_maximum_fusion.1), calls=%async_computation.4 | async-start | bytes 1572864 | tf_op jit(solution)/shard_map/all_to_all | solution.py:250
  120.1 4.9 %collective-permute-start.6 = (bf16[2,256,256]{2,1,0:T(8,128)(2,1)S(1)}, bf16[2,256,256]{2,1,0:T(8,128)(2,1)S(1)}, u32[]{:S(2)}, u32[]{:S(2)}) collective-permute-start(bf16[2,256,256]{2,1,0:T(8,128)(2,1)S(1)} %fusion.7), channel_id=1, source_target_pairs={{0,8},{4,12},{8,0},{12,4},{1,9},{5,13},{9,1},{13,5},{2,10},{6,14},... | collective-permute-start | bytes 786440 | tf_op jit(solution)/shard_map/ppermute | solution.py:29
  125.2 5.0 %all-to-all-done.4.moved = bf16[4,384,256]{2,1,0:T(8,128)(2,1)S(1)} async-done(((bf16[4,384,256]{2,1,0:T(8,128)(2,1)}), bf16[4,384,256]{2,1,0:T(8,128)(2,1)S(1)}, u32[]{:S(2)}, u32[]{:S(2)}) %all-to-all-start.4) | async-done | bytes 786464 | tf_op jit(solution)/shard_map/all_to_all | solution.py:250
  131.5 3.1 %collective-permute-start.5 = (bf16[256,512]{1,0:T(8,128)(2,1)S(1)}, bf16[256,512]{1,0:T(8,128)(2,1)S(1)}, u32[]{:S(2)}, u32[]{:S(2)}) collective-permute-start(bf16[256,512]{1,0:T(8,128)(2,1)S(1)} %get-tuple-element.44), channel_id=1, source_target_pairs={{0,16},{16,0},{1,17},{17,1},{2,18},{18,2},{3,19},{19,3},{4,20},{20... | collective-permute-start | bytes 786440 | tf_op jit(solution)/shard_map/ppermute | solution.py:25
  134.7 3.4 %collective-permute-start.7 = (bf16[256,256]{1,0:T(8,128)(2,1)S(1)}, bf16[256,256]{1,0:T(8,128)(2,1)S(1)}, u32[]{:S(2)}, u32[]{:S(2)}) collective-permute-start(bf16[256,256]{1,0:T(8,128)(2,1)S(1)} %dynamic-slice_bitcast_fusion), channel_id=1, source_target_pairs={{0,4},{4,0},{8,12},{12,8},{1,5},{5,1},{9,13},{13,9},{2,6},{6,2},{1... | collective-permute-start | bytes 393224 | tf_op jit(solution)/shard_map/ppermute | solution.py:29
  139.0 11.3 %all-to-all-start.5 = ((bf16[4,64,768]{2,1,0:T(8,128)(2,1)}), bf16[4,64,768]{2,1,0:T(8,128)(2,1)S(1)}, u32[]{:S(2)}, u32[]{:S(2)}) async-start(bf16[4,64,768]{2,1,0:T(8,128)(2,1)} %bitcast.26), calls=%async_computation.5 | async-start | bytes 786432 | tf_op jit(solution)/shard_map/all_to_all | solution.py:21
  150.4 4.5 %collective-permute-start.8 = (bf16[2,64,128]{2,1,0:T(8,128)(2,1)S(1)}, bf16[2,64,128]{2,1,0:T(8,128)(2,1)S(1)}, u32[]{:S(2)}, u32[]{:S(2)}) collective-permute-start(bf16[2,64,128]{2,1,0:T(8,128)(2,1)S(1)} %constant_dynamic-slice_fusion), channel_id=1, source_target_pairs={{0,2},{1,3},{2,0},{3,1},{4,6},{5,7},{6,4},{7,5},{8,10},{9,11},{10,... | collective-permute-start | bytes 98312 | tf_op jit(solution)/shard_map/ppermute | solution.py:29
  154.9 9.8 %collective-permute-done.8 = bf16[2,64,128]{2,1,0:T(8,128)(2,1)S(1)} collective-permute-done((bf16[2,64,128]{2,1,0:T(8,128)(2,1)S(1)}, bf16[2,64,128]{2,1,0:T(8,128)(2,1)S(1)}, u32[]{:S(2)}, u32[]{:S(2)}) %collective-permute-start.8) | collective-permute-done | bytes 32800 | tf_op jit(solution)/shard_map/ppermute | solution.py:29
  164.8 3.1 %collective-permute-start.9 = (bf16[64,128]{1,0:T(8,128)(2,1)S(1)}, bf16[64,128]{1,0:T(8,128)(2,1)S(1)}, u32[]{:S(2)}, u32[]{:S(2)}) collective-permute-start(bf16[64,128]{1,0:T(8,128)(2,1)S(1)} %dynamic-slice_bitcast_fusion.5), channel_id=1, source_target_pairs={{0,1},{1,0},{2,3},{3,2},{4,5},{5,4},{6,7},{7,6},{8,9},{9,8},{10,11... | collective-permute-start | bytes 49160 | tf_op jit(solution)/shard_map/ppermute | solution.py:29
  167.8 2.5 %convolution_convert_fusion = bf16[128,2048]{1,0:T(8,128)(2,1)} fusion(bf16[2048,768]{1,0:T(8,128)(2,1)} %bitcast.73, bf16[256,256]{1,0:T(8,128)(2,1)S(1)} %fusion.9), kind=kOutput, calls=%fused_computation.1 | convolution fusion | flops 134479872 | bytes 1638400 | tf_op jit(solution)/shard_map/dot_general | solution.py:264
  171.7 3.3 %all-to-all-start.6 = ((bf16[4,64,256]{2,1,0:T(8,128)(2,1)}), bf16[4,64,256]{2,1,0:T(8,128)(2,1)S(1)}, u32[]{:S(2)}, u32[]{:S(2)}) async-start(bf16[4,64,256]{2,1,0:T(8,128)(2,1)} %broadcast_in_dim.50), calls=%async_computation.6 | async-start | bytes 262144 | tf_op jit(solution)/shard_map/all_to_all | solution.py:17
  175.0 25.5 %all_gather.13 = bf16[256,512]{1,0:T(8,128)(2,1)S(1)} all-gather(bf16[64,512]{1,0:T(8,128)(2,1)S(1)} %slice.62), channel_id=1, replica_groups=mesh['x'=4,'zh'=4,'co'=2,'y'=4,'zl'=4] {'zh'}, dimensions={0}, use_global_device_ids=true | all-gather | bytes 327680 | tf_op jit(solution)/shard_map/all_gather | solution.py:270
  201.6 3.5 %all-to-all-start.7 = ((bf16[4,256,512]{2,1,0:T(8,128)(2,1)}), bf16[4,256,512]{2,1,0:T(8,128)(2,1)S(1)}, u32[]{:S(2)}, u32[]{:S(2)}) async-start(bf16[4,256,512]{2,1,0:T(8,128)(2,1)} %broadcast_in_dim.51), calls=%async_computation.7 | async-start | bytes 2097152 | tf_op jit(solution)/shard_map/all_to_all | solution.py:17
  205.1 11.9 %all-gather = bf16[256,256]{1,0:T(8,128)(2,1)S(1)} all-gather(bf16[64,256]{1,0:T(8,128)(2,1)S(1)} %reduce_sum.34), channel_id=2, replica_groups=mesh['x'=4,'zh'=4,'co'=2,'y'=4,'zl'=4] {'zl'}, dimensions={0}, use_global_device_ids=true | all-gather | bytes 163840 | tf_op jit(solution)/shard_map/all_gather | solution.py:273
  217.6 9.0 %collective-permute-start.10 = (bf16[4,256,512]{2,1,0:T(8,128)(2,1)S(1)}, bf16[4,256,512]{2,1,0:T(8,128)(2,1)S(1)}, u32[]{:S(2)}, u32[]{:S(2)}) collective-permute-start(bf16[4,256,512]{2,1,0:T(8,128)(2,1)S(1)} %all-to-all-done.7.mine), channel_id=1, source_target_pairs={{0,16},{16,0},{1,17},{17,1},{2,18},{18,2},{3,19},{19,3},{4,20},{20... | collective-permute-start | bytes 3145736 | tf_op jit(solution)/shard_map/ppermute | solution.py:25
  226.7 2.3 collective-permute-done.10.theirs
  228.9 2.2 shard_map.114
  (87 shorter events, 26.8 us)
Async XLA Ops:
  3.2 5.2 %copy-start.9 = (bf16[256,64]{0,1:T(8,128)(2,1)S(1)}, bf16[256,64]{0,1:T(8,128)(2,1)}, u32[]{:S(2)}) copy-start(bf16[256,64]{0,1:T(8,128)(2,1)} %param.12) | copy-start | bytes 98308
  3.3 5.2 %copy-start.10 = (bf16[64,256]{1,0:T(8,128)(2,1)S(1)}, bf16[64,256]{1,0:T(8,128)(2,1)}, u32[]{:S(2)}) copy-start(bf16[64,256]{1,0:T(8,128)(2,1)} %param.11) | copy-start | bytes 98308
  3.3 5.2 %copy-start.11 = (bf16[64,256]{1,0:T(8,128)(2,1)S(1)}, bf16[64,256]{1,0:T(8,128)(2,1)}, u32[]{:S(2)}) copy-start(bf16[64,256]{1,0:T(8,128)(2,1)} %param.10) | copy-start | bytes 98308
  3.3 30.7 %all-to-all-start = ((bf16[4,128,2048]{2,1,0:T(8,128)(2,1)}), bf16[4,128,2048]{2,1,0:T(8,128)(2,1)S(1)}, u32[]{:S(2)}, u32[]{:S(2)}) async-start(bf16[4,128,2048]{2,1,0:T(8,128)(2,1)} %broadcast_in_dim.19), calls=%async_computation | async-start | bytes 4194304 | tf_op jit(solution)/shard_map/all_to_all | solution.py:17
  33.9 27.6 %copy-start.7 = (bf16[1,64,2048]{2,1,0:T(8,128)(2,1)S(1)}, bf16[1,64,2048]{2,1,0:T(8,128)(2,1)}, u32[]{:S(2)}) copy-start(bf16[1,64,2048]{2,1,0:T(8,128)(2,1)} %param.7) | copy-start | bytes 786436
  52.8 12.1 %collective-permute-start = (bf16[16,64,768]{2,1,0:T(8,128)(2,1)}, bf16[16,64,768]{2,1,0:T(8,128)(2,1)}, u32[]{:S(2)}, u32[]{:S(2)}) collective-permute-start(bf16[16,64,768]{2,1,0:T(8,128)(2,1)} %bitcast.8), channel_id=1, source_target_pairs={{0,16},{16,0},{1,17},{17,1},{2,18},{18,2},{3,19},{19,3},{4,20},{20... | collective-permute-start | bytes 4718600 | tf_op jit(solution)/shard_map/ppermute | solution.py:25
  67.0 1.9 copy-start.8
  67.3 1.6 copy-start.6
  67.3 8.7 %copy-start.12 = (s32[1,16]{1,0:T(1,128)S(1)}, s32[1,16]{1,0:T(1,128)}, u32[]{:S(2)}) copy-start(s32[1,16]{1,0:T(1,128)} %param.9) | copy-start | bytes 196
  69.9 12.9 %all-to-all-start.2 = ((bf16[4,64,512]{2,1,0:T(8,128)(2,1)}), bf16[4,64,512]{2,1,0:T(8,128)(2,1)S(1)}, u32[]{:S(2)}, u32[]{:S(2)}) async-start(bf16[4,64,512]{2,1,0:T(8,128)(2,1)} %broadcast_in_dim.21), calls=%async_computation.2 | async-start | bytes 524288 | tf_op jit(solution)/shard_map/all_to_all | solution.py:17
  85.2 17.6 %all-to-all-start.3 = ((bf16[4,64,896]{2,1,0:T(8,128)(2,1)}), bf16[4,64,896]{2,1,0:T(8,128)(2,1)S(1)}, u32[]{:S(2)}, u32[]{:S(2)}) async-start(bf16[4,64,896]{2,1,0:T(8,128)(2,1)} %shard_map.110), calls=%async_computation.3 | async-start | bytes 917504 | tf_op jit(solution)/shard_map/all_to_all | solution.py:238
  89.9 8.4 %collective-permute-start.1 = (bf16[64,1024]{1,0:T(8,128)(2,1)S(1)}, bf16[64,1024]{1,0:T(8,128)(2,1)S(1)}, u32[]{:S(2)}, u32[]{:S(2)}) collective-permute-start(bf16[64,1024]{1,0:T(8,128)(2,1)S(1)} %get-tuple-element.59), channel_id=1, source_target_pairs={{0,128},{128,256},{256,384},{384,0},{1,129},{129,257},{257,385},{3... | collective-permute-start | bytes 393224 | tf_op jit(solution)/shard_map/ppermute | solution.py:243
  92.1 8.5 %collective-permute-start.2 = (bf16[64,1024]{1,0:T(8,128)(2,1)S(1)}, bf16[64,1024]{1,0:T(8,128)(2,1)S(1)}, u32[]{:S(2)}, u32[]{:S(2)}) collective-permute-start(bf16[64,1024]{1,0:T(8,128)(2,1)S(1)} %get-tuple-element.58), channel_id=1, source_target_pairs={{0,256},{128,384},{256,0},{384,128},{1,257},{129,385},{257,1},{385... | collective-permute-start | bytes 393224 | tf_op jit(solution)/shard_map/ppermute | solution.py:243
  95.8 6.4 %collective-permute-start.3 = (bf16[64,1024]{1,0:T(8,128)(2,1)S(1)}, bf16[64,1024]{1,0:T(8,128)(2,1)S(1)}, u32[]{:S(2)}, u32[]{:S(2)}) collective-permute-start(bf16[64,1024]{1,0:T(8,128)(2,1)S(1)} %get-tuple-element.57), channel_id=1, source_target_pairs={{0,384},{128,0},{256,128},{384,256},{1,385},{129,1},{257,129},{385... | collective-permute-start | bytes 393224 | tf_op jit(solution)/shard_map/ppermute | solution.py:243
  98.3 0.7 copy-start
  100.6 0.6 copy-start.2
  102.2 0.6 copy-start.4
  106.3 7.1 %collective-permute-start.4 = (bf16[16,64,256]{2,1,0:T(8,128)(2,1)}, bf16[16,64,256]{2,1,0:T(8,128)(2,1)S(1)}, u32[]{:S(2)}, u32[]{:S(2)}) collective-permute-start(bf16[16,64,256]{2,1,0:T(8,128)(2,1)} %get-tuple-element.38), channel_id=1, source_target_pairs={{0,16},{16,0},{1,17},{17,1},{2,18},{18,2},{3,19},{19,3},{4,20},{20... | collective-permute-start | bytes 1572872 | tf_op jit(solution)/shard_map/ppermute | solution.py:25
  114.5 15.6 %copy-start.1 = (bf16[64,1024]{1,0:T(8,128)(2,1)S(1)}, bf16[64,1024]{1,0:T(8,128)(2,1)}, u32[]{:S(2)}) copy-start(bf16[64,1024]{1,0:T(8,128)(2,1)} %copy-done) | copy-start | bytes 393220
  114.5 15.6 %copy-start.3 = (bf16[64,1024]{1,0:T(8,128)(2,1)S(1)}, bf16[64,1024]{1,0:T(8,128)(2,1)}, u32[]{:S(2)}) copy-start(bf16[64,1024]{1,0:T(8,128)(2,1)} %copy-done.2) | copy-start | bytes 393220
  114.5 15.6 %copy-start.5 = (bf16[64,1024]{1,0:T(8,128)(2,1)S(1)}, bf16[64,1024]{1,0:T(8,128)(2,1)}, u32[]{:S(2)}) copy-start(bf16[64,1024]{1,0:T(8,128)(2,1)} %copy-done.4) | copy-start | bytes 393220
  114.5 15.6 %all-to-all-start.4 = ((bf16[4,384,256]{2,1,0:T(8,128)(2,1)}), bf16[4,384,256]{2,1,0:T(8,128)(2,1)S(1)}, u32[]{:S(2)}, u32[]{:S(2)}) async-start(bf16[4,384,256]{2,1,0:T(8,128)(2,1)} %pad_maximum_fusion.1), calls=%async_computation.4 | async-start | bytes 1572864 | tf_op jit(solution)/shard_map/all_to_all | solution.py:250
  120.1 14.5 %collective-permute-start.6 = (bf16[2,256,256]{2,1,0:T(8,128)(2,1)S(1)}, bf16[2,256,256]{2,1,0:T(8,128)(2,1)S(1)}, u32[]{:S(2)}, u32[]{:S(2)}) collective-permute-start(bf16[2,256,256]{2,1,0:T(8,128)(2,1)S(1)} %fusion.7), channel_id=1, source_target_pairs={{0,8},{4,12},{8,0},{12,4},{1,9},{5,13},{9,1},{13,5},{2,10},{6,14},... | collective-permute-start | bytes 786440 | tf_op jit(solution)/shard_map/ppermute | solution.py:29
  131.5 6.7 %collective-permute-start.5 = (bf16[256,512]{1,0:T(8,128)(2,1)S(1)}, bf16[256,512]{1,0:T(8,128)(2,1)S(1)}, u32[]{:S(2)}, u32[]{:S(2)}) collective-permute-start(bf16[256,512]{1,0:T(8,128)(2,1)S(1)} %get-tuple-element.44), channel_id=1, source_target_pairs={{0,16},{16,0},{1,17},{17,1},{2,18},{18,2},{3,19},{19,3},{4,20},{20... | collective-permute-start | bytes 786440 | tf_op jit(solution)/shard_map/ppermute | solution.py:25
  134.7 15.6 %collective-permute-start.7 = (bf16[256,256]{1,0:T(8,128)(2,1)S(1)}, bf16[256,256]{1,0:T(8,128)(2,1)S(1)}, u32[]{:S(2)}, u32[]{:S(2)}) collective-permute-start(bf16[256,256]{1,0:T(8,128)(2,1)S(1)} %dynamic-slice_bitcast_fusion), channel_id=1, source_target_pairs={{0,4},{4,0},{8,12},{12,8},{1,5},{5,1},{9,13},{13,9},{2,6},{6,2},{1... | collective-permute-start | bytes 393224 | tf_op jit(solution)/shard_map/ppermute | solution.py:29
  139.0 31.9 %all-to-all-start.5 = ((bf16[4,64,768]{2,1,0:T(8,128)(2,1)}), bf16[4,64,768]{2,1,0:T(8,128)(2,1)S(1)}, u32[]{:S(2)}, u32[]{:S(2)}) async-start(bf16[4,64,768]{2,1,0:T(8,128)(2,1)} %bitcast.26), calls=%async_computation.5 | async-start | bytes 786432 | tf_op jit(solution)/shard_map/all_to_all | solution.py:21
  150.4 14.3 %collective-permute-start.8 = (bf16[2,64,128]{2,1,0:T(8,128)(2,1)S(1)}, bf16[2,64,128]{2,1,0:T(8,128)(2,1)S(1)}, u32[]{:S(2)}, u32[]{:S(2)}) collective-permute-start(bf16[2,64,128]{2,1,0:T(8,128)(2,1)S(1)} %constant_dynamic-slice_fusion), channel_id=1, source_target_pairs={{0,2},{1,3},{2,0},{3,1},{4,6},{5,7},{6,4},{7,5},{8,10},{9,11},{10,... | collective-permute-start | bytes 98312 | tf_op jit(solution)/shard_map/ppermute | solution.py:29
  164.8 5.6 %collective-permute-start.9 = (bf16[64,128]{1,0:T(8,128)(2,1)S(1)}, bf16[64,128]{1,0:T(8,128)(2,1)S(1)}, u32[]{:S(2)}, u32[]{:S(2)}) collective-permute-start(bf16[64,128]{1,0:T(8,128)(2,1)S(1)} %dynamic-slice_bitcast_fusion.5), channel_id=1, source_target_pairs={{0,1},{1,0},{2,3},{3,2},{4,5},{5,4},{6,7},{7,6},{8,9},{9,8},{10,11... | collective-permute-start | bytes 49160 | tf_op jit(solution)/shard_map/ppermute | solution.py:29
  171.7 28.8 %all-to-all-start.6 = ((bf16[4,64,256]{2,1,0:T(8,128)(2,1)}), bf16[4,64,256]{2,1,0:T(8,128)(2,1)S(1)}, u32[]{:S(2)}, u32[]{:S(2)}) async-start(bf16[4,64,256]{2,1,0:T(8,128)(2,1)} %broadcast_in_dim.50), calls=%async_computation.6 | async-start | bytes 262144 | tf_op jit(solution)/shard_map/all_to_all | solution.py:17
  201.6 16.0 %all-to-all-start.7 = ((bf16[4,256,512]{2,1,0:T(8,128)(2,1)}), bf16[4,256,512]{2,1,0:T(8,128)(2,1)S(1)}, u32[]{:S(2)}, u32[]{:S(2)}) async-start(bf16[4,256,512]{2,1,0:T(8,128)(2,1)} %broadcast_in_dim.51), calls=%async_computation.7 | async-start | bytes 2097152 | tf_op jit(solution)/shard_map/all_to_all | solution.py:17
  217.6 11.3 %collective-permute-start.10 = (bf16[4,256,512]{2,1,0:T(8,128)(2,1)S(1)}, bf16[4,256,512]{2,1,0:T(8,128)(2,1)S(1)}, u32[]{:S(2)}, u32[]{:S(2)}) collective-permute-start(bf16[4,256,512]{2,1,0:T(8,128)(2,1)S(1)} %all-to-all-done.7.mine), channel_id=1, source_target_pairs={{0,16},{16,0},{1,17},{17,1},{2,18},{18,2},{3,19},{19,3},{4,20},{20... | collective-permute-start | bytes 3145736 | tf_op jit(solution)/shard_map/ppermute | solution.py:25

commit v3 on v2

--- a/solution.py
+++ b/solution.py
@@ -34,11 +34,14 @@
 
 
 def halve(parts, axis):
-    me = lax.axis_index(axis)
-    high, low = me // 2, lax.rem(me, 2)
+    high = lax.axis_index(axis) // 2
     keep = lax.dynamic_slice_in_dim(parts, 2 * high, 2, 0)
     send = lax.dynamic_slice_in_dim(parts, 2 - 2 * high, 2, 0)
-    two = join(keep, meet(send, axis, 2))
+    return join(keep, meet(send, axis, 2))
+
+
+def halve_again(two, axis):
+    low = lax.rem(lax.axis_index(axis), 2)
     keep = lax.dynamic_index_in_dim(two, low, 0, keepdims=False)
     send = lax.dynamic_index_in_dim(two, 1 - low, 0, keepdims=False)
     return join(keep, meet(send, axis, 1))
@@ -70,10 +73,20 @@
     return q, g, weights, rows_by_rows(g, kv[:, HD:])
 
 
+def projection_kernel(core, even, odd, own, other, out):
+    at_first = core[0] == 0
+    for i, at in enumerate((0, 512)):
+        kept = jnp.where(at_first, even[i], odd[i])
+        rest = jnp.where(at_first, odd[i], even[i])
+        total = jnp.dot(kept, own[:, at : at + 256], preferred_element_type=f32)
+        total = total + jnp.dot(rest, other[:, at : at + 256], preferred_element_type=f32)
+        out[:, 256 * i : 256 * i + 256] = total.astype(bf16)
+
+
 def forward_kernel(lengths, qa, kv, out):
     _, _, weights, dprob = attend(lengths, qa, kv)
     total = jnp.sum(weights, -1, keepdims=True)
-    probs = weights * (1.0 / jnp.where(total > 0, total, 1.0))
+    probs = weights / jnp.where(total > 0, total, 1.0)
     delta = jnp.sum(probs * dprob, -1, keepdims=True)
     centred = (probs * (dprob - delta)).astype(bf16)
     plain = jnp.dot(probs.astype(bf16), kv[...], preferred_element_type=f32).astype(bf16)
@@ -127,7 +140,7 @@
     total = jnp.concatenate([pair[0] for pair in pairs], 0)
     delta = jnp.concatenate([pair[1] for pair in pairs], 0)
     q, g, weights, dprob = attend(lengths, qa, kv)
-    probs = weights * (1.0 / total)
+    probs = weights / total
     dscore = (probs * (dprob - delta) * SCALE).astype(bf16)
     key_part = outer(dscore, q).astype(bf16)
     value_part = outer(probs.astype(bf16), g).astype(bf16)
@@ -211,20 +224,21 @@
 
     shard = jnp.concatenate([q_weight, kv_weight, o_weight.T], 1)
     own = lax.all_gather(shard, "zh", axis=0, tiled=True)
-    own, enc_four = together(own, enc_four)
-    own = spread(own, "x").reshape(16, 64, 768)
+    own, enc_four, dec_rows, grad_rows = together(own, enc_four, dec_rows, grad_rows)
+    own = spread(own, "x").reshape(1024, 768)
+    halves = jnp.stack([dec_rows, grad_rows]).reshape(2, 64, 16, 2, 64)
+    even, odd = halves[:, :, :, 0].reshape(2, 64, 1024), halves[:, :, :, 1].reshape(2, 64, 1024)
+    own, even, odd = together(own, even, odd)
     other = swap(own)
+    (qa_own,) = call(projection_kernel, [(64, 512)], core, even, odd, own, other)
+    own, other, qa_own = together(own, other, qa_own)
+    own, other = own.reshape(16, 64, 768), other.reshape(16, 64, 768)
     weights_all = jnp.stack(
         [jnp.where(first_core, own, other), jnp.where(first_core, other, own)], 1
     ).reshape(2048, 768)
     wq_full = weights_all[:, :256]
     wkv_full = weights_all[:, 256:512]
-    wo_t = weights_all[:, 512:]
-
-    queries = jnp.dot(dec_rows, wq_full, preferred_element_type=f32).astype(bf16)
-    attn_grad = jnp.dot(grad_rows, wo_t, preferred_element_type=f32).astype(bf16)
-
-    qa_all = spread(jnp.concatenate([queries, attn_grad], 1), "zl")
+    qa_all = spread(qa_own, "zl")
     kv_all = jnp.dot(enc_four, wkv_full, preferred_element_type=f32).astype(bf16)
     (parts,) = call(forward_kernel, [(4, 64, 896)], lengths, qa_all, kv_all)
 
@@ -247,31 +261,43 @@
     keep, send = call(key_term_kernel, [(16, 64, 256)] * 2, core, kv_part, enc_four)
     kv_chip = join(keep, swap(send)).reshape(4, 256, 256)
     messages = jnp.concatenate([jnp.broadcast_to(heads[None], (4, 128, 256)), kv_chip], 1)
+    messages, kv_part = together(messages, kv_part)
     moved_x = lax.all_to_all(messages, "x", 0, 0)
+    kv_two = halve(kv_part.reshape(4, PT, 256), "y")
+    moved_x, kv_two = together(moved_x, kv_two)
     sources = jnp.concatenate([core] + [lax.rem(x + 4 - step, 4).reshape(1) for step in range(4)])
     keep, send, kv_sum = call(
         head_term_kernel, [(256, 512), (256, 512), (256, 256)], sources, moved_x, *rows_x
     )
     sum_x = jnp.concatenate([join(keep, swap(send)), kv_sum], 1)
-    parts_z = sum_x.reshape(4, 64, 768)
-
+    sum_x, kv_two, heads = together(sum_x, kv_two, heads)
+
+    sum_z = exchange(sum_x.reshape(4, 64, 768), "zh")
+    kv_grad = halve_again(kv_two, "y")
+    enc_grad = jnp.dot(kv_grad, wkv_full.T, preferred_element_type=f32).astype(bf16)
     dec_part = jnp.dot(heads[64:], wq_full.T, preferred_element_type=f32).astype(bf16)
-    dec_part = dec_part.reshape(64, 4, 2, 256).transpose(1, 2, 0, 3).reshape(4, 128, 256)
-    y_sum = halve(jnp.concatenate([kv_part.reshape(4, PT, 256), dec_part], 1), "y")
-    kv_grad = y_sum[:PT]
-    dec_y = y_sum[PT:].reshape(2, 64, 2, 128).transpose(0, 2, 1, 3).reshape(4, 64, 128)
-    dec_grad = halve(dec_y, "zl")
-    enc_grad = jnp.dot(kv_grad, wkv_full.T, preferred_element_type=f32).astype(bf16)
-
-    sum_z = exchange(parts_z, "zh")
-    sum_z, dec_grad, enc_grad = together(sum_z, dec_grad, enc_grad)
-
-    kv_y = jnp.sum(spread(sum_z[:, 512:], "y").astype(f32), 0).astype(bf16)
+    dec_part = dec_part.reshape(64, 4, 512).transpose(1, 0, 2)
+    sum_z, dec_part, enc_grad = together(sum_z, dec_part, enc_grad)
+
+    last = jnp.concatenate([jnp.broadcast_to(sum_z[None, :, 512:], (4, 64, 256)), dec_part], 2)
+    last = exchange(last, "y")
     mine = lax.all_gather(sum_z[:, :512], "zh", axis=0, tiled=True)
-    mine, kv_y = together(mine, kv_y)
-    mine = spread(mine, "x")
-    kv_weight_grad = jnp.sum(lax.all_gather(kv_y, "zl", axis=0).astype(f32), 0)
-    mine, kv_weight_grad = together(mine, kv_weight_grad)
+    copies = jnp.broadcast_to(mine[None], (4, 256, 512))
+    copies, last = together(copies, last)
+    mine = lax.all_to_all(copies, "x", 0, 0)
+    high, low = zl // 2, lax.rem(zl, 2)
+    parts = last[:, 256:].reshape(64, 2, 256)
+    ahead = lax.dynamic_index_in_dim(parts, 1 - high, 1, keepdims=False)
+    back = meet(jnp.concatenate([last[:, :256], ahead], 1), "zl", 2)
+    here = lax.dynamic_index_in_dim(parts, high, 1, keepdims=False)
+    last = join(jnp.concatenate([last[:, :256], here], 1), back)
+    mine, last = together(mine, last)
+    parts = last[:, 256:].reshape(64, 2, 128)
+    ahead = lax.dynamic_index_in_dim(parts, 1 - low, 1, keepdims=False)
+    back = meet(jnp.concatenate([last[:, :256], ahead], 1), "zl", 1).astype(f32)
+    here = lax.dynamic_index_in_dim(parts, low, 1, keepdims=False)
+    kv_weight_grad = last[:, :256].astype(f32) + back[:, :256]
+    dec_grad = (here.astype(f32) + back[:, 256:]).astype(bf16)
     q_weight_grad, o_weight_grad = place(core, mine, swap(mine))
     return (dec_grad[None], enc_grad[None], q_weight_grad, kv_weight_grad, o_weight_grad)
 

time: 232 us -> 224 us (0.966)
  blocking collectives: 81.6 us -> 42.1 us
  starting transfers between devices: 86.4 us -> 102 us
  waiting for transfers between devices: 27.7 us -> 39.9 us
  local copies, waits for them, and re-layouts: 10.8 us -> 14.9 us
    all_to_all x1 -> x0, blocking collectives: 18.8 us -> none  [spread(): return lax.all_to_all(copies, axis, 0, 0)]
    all_gather x1 -> x0, blocking collectives: 11.9 us -> none  [local(): kv_weight_grad = jnp.sum(lax.all_gather(kv_y, 'zl', axis=0).astype(f32), 0)]
    all_to_all x4 -> x3, waiting for transfers between devices: 3.1 us -> 14.9 us  [spread(): return lax.all_to_all(copies, axis, 0, 0)]
    ppermute x4, starting transfers between devices: 15.9 us -> 25.5 us  [meet(): return lax.ppermute(block, axis, [(i, i ^ bit) for i in range(4)])]
    all_gather x1, blocking collectives: 25.5 us -> 16.7 us  [local(): mine = lax.all_gather(sum_z[:, :512], 'zh', axis=0, tiled=True)]
    all_to_all x1 -> x2, waiting for transfers between devices: 0.01 us -> 8.02 us  [exchange(): lax.all_to_all(parts, axis, 0, 0).astype(f32)]
    all_to_all x1 -> x2, starting transfers between devices: 11.3 us -> 16 us  [exchange(): lax.all_to_all(parts, axis, 0, 0).astype(f32)]
    ppermute x4, waiting for transfers between devices: 7.28 us -> 2.66 us  [swap(): return lax.ppermute(block, 'co', [(0, 1), (1, 0)])]
  transfers between devices with their start and end apart: 18 -> 19, of which waited for: 8 -> 12; matrix products, arithmetic and copies ran while one was open for 5% -> 8% of each run, Pallas kernels for 1% -> 0%
where the time goes in v3:
time: 224 us; the launch traced here: 223 us
  starting transfers between devices  102 us (46%)
  blocking collectives  42.1 us (19%)
  waiting for transfers between devices  39.9 us (18%)
  local copies, waits for them, and re-layouts  14.9 us (7%)
  Pallas kernels  9 us (4%)
  other arithmetic  7.94 us (4%)
  matrix products  6.09 us (3%)
    ppermute x4, starting transfers between devices, swap(): return lax.ppermute(block, 'co', [(0, 1), (1, 0)])  26.5 us
    ppermute x4, starting transfers between devices, meet(): return lax.ppermute(block, axis, [(i, i ^ bit) for i in range(4)])  25.5 us
    all_gather x1, blocking collectives, local(): own = lax.all_gather(shard, 'zh', axis=0, tiled=True)  25.5 us
    all_gather x1, blocking collectives, local(): mine = lax.all_gather(sum_z[:, :512], 'zh', axis=0, tiled=True)  16.7 us
    all_to_all x2, starting transfers between devices, exchange(): lax.all_to_all(parts, axis, 0, 0).astype(f32)  16 us
    all_to_all x3, waiting for transfers between devices, spread(): return lax.all_to_all(copies, axis, 0, 0)  14.9 us
    all_to_all x3, starting transfers between devices, spread(): return lax.all_to_all(copies, axis, 0, 0)  14.7 us
    ppermute x3, starting transfers between devices, local(): lax.ppermute(part, 'x', [(i, (i + step) % 4) for i in range(4)])  8.42 us
  transfers between devices with their start and end apart: 19, of which 12 were waited for; matrix products, arithmetic and copies ran while one was open for 8% of the time, Pallas kernels for 0%

profile of v3, /device:TPU:1, one launch (start us, length us, event | category | flops | bytes accessed | tf_op | source)
XLA Modules:
  0.0 222.9 jit_solution(1036784963479658231)
XLA Ops:
  0.6 2.6 %broadcast_in_dim.19 = bf16[4,128,2048]{2,1,0:T(8,128)(2,1)} broadcast(bf16[128,2048]{1,0:T(8,128)(2,1)} %bitcast.90), dimensions={1,2} | broadcast | bytes 2621440 | tf_op jit(solution)/shard_map/broadcast_in_dim | solution.py:16
  3.3 5.1 %all-to-all-start = ((bf16[4,128,2048]{2,1,0:T(8,128)(2,1)}), bf16[4,128,2048]{2,1,0:T(8,128)(2,1)S(1)}, u32[]{:S(2)}, u32[]{:S(2)}) async-start(bf16[4,128,2048]{2,1,0:T(8,128)(2,1)} %broadcast_in_dim.19), calls=%async_computation | async-start | bytes 4194304 | tf_op jit(solution)/shard_map/all_to_all | solution.py:17
  8.4 25.5 %all_gather.6 = bf16[256,768]{1,0:T(8,128)(2,1)S(1)} all-gather(bf16[64,768]{1,0:T(8,128)(2,1)S(1)} %pad_maximum_fusion.5), channel_id=1, replica_groups=mesh['x'=4,'zh'=4,'co'=2,'y'=4,'zl'=4] {'zh'}, dimensions={0}, use_global_device_ids=true | all-gather | bytes 491520 | tf_op jit(solution)/shard_map/all_gather | solution.py:226
  35.8 4.0 %all-to-all-start.1 = ((bf16[4,256,768]{2,1,0:T(8,128)(2,1)}), bf16[4,256,768]{2,1,0:T(8,128)(2,1)S(1)}, u32[]{:S(2)}, u32[]{:S(2)}) async-start(bf16[4,256,768]{2,1,0:T(8,128)(2,1)} %broadcast_in_dim.20), calls=%async_computation.1 | async-start | bytes 3145728 | tf_op jit(solution)/shard_map/all_to_all | solution.py:17
  42.6 11.9 %all-to-all-done.1 = bf16[4,256,768]{2,1,0:T(8,128)(2,1)S(1)} async-done(((bf16[4,256,768]{2,1,0:T(8,128)(2,1)}), bf16[4,256,768]{2,1,0:T(8,128)(2,1)S(1)}, u32[]{:S(2)}, u32[]{:S(2)}) %all-to-all-start.1) | async-done | bytes 1572896 | tf_op jit(solution)/shard_map/all_to_all | solution.py:17
  54.5 8.8 %collective-permute-start = (bf16[1024,768]{1,0:T(8,128)(2,1)S(1)}, bf16[1024,768]{1,0:T(8,128)(2,1)S(1)}, u32[]{:S(2)}, u32[]{:S(2)}) collective-permute-start(bf16[1024,768]{1,0:T(8,128)(2,1)S(1)} %bitcast.74), channel_id=1, source_target_pairs={{0,16},{16,0},{1,17},{17,1},{2,18},{18,2},{3,19},{19,3},{4,20},{20... | collective-permute-start | bytes 4718600 | tf_op jit(solution)/shard_map/ppermute | solution.py:25
  68.1 5.5 %all-to-all-start.2 = ((bf16[4,64,512]{2,1,0:T(8,128)(2,1)}), bf16[4,64,512]{2,1,0:T(8,128)(2,1)S(1)}, u32[]{:S(2)}, u32[]{:S(2)}) async-start(bf16[4,64,512]{2,1,0:T(8,128)(2,1)} %broadcast_in_dim.21), calls=%async_computation.2 | async-start | bytes 524288 | tf_op jit(solution)/shard_map/all_to_all | solution.py:17
  76.2 1.9 convolution_convert_fusion.2.kv
  78.1 3.0 %all-to-all-done.2.qa = bf16[4,64,512]{2,1,0:T(8,128)(2,1)S(1)} async-done(((bf16[4,64,512]{2,1,0:T(8,128)(2,1)}), bf16[4,64,512]{2,1,0:T(8,128)(2,1)S(1)}, u32[]{:S(2)}, u32[]{:S(2)}) %all-to-all-start.2) | async-done | bytes 262176 | tf_op jit(solution)/shard_map/all_to_all | solution.py:17
  81.1 2.3 %shard_map.111 = bf16[4,64,896]{2,1,0:T(8,128)(2,1)} custom-call(s32[4]{0:T(128)S(1)} %fusion.11.lengths, bf16[4,64,512]{2,1,0:T(8,128)(2,1)S(1)} %all-to-all-done.2.qa, bf16[512,256]{1,0:T(8,128)(2,1)S(1)} %convolution_convert_fusion.2.kv), custom_call_target="tpu_custom_call" | custom-call | tf_op jit(solution)/shard_map/pallas_call | solution.py:187
  83.4 3.5 %all-to-all-start.3 = ((bf16[4,64,896]{2,1,0:T(8,128)(2,1)}), bf16[4,64,896]{2,1,0:T(8,128)(2,1)S(1)}, u32[]{:S(2)}, u32[]{:S(2)}) async-start(bf16[4,64,896]{2,1,0:T(8,128)(2,1)} %shard_map.111), calls=%async_computation.3 | async-start | bytes 917504 | tf_op jit(solution)/shard_map/all_to_all | solution.py:252
  88.1 2.2 collective-permute-start.1
  90.3 3.7 %collective-permute-start.2 = (bf16[64,1024]{1,0:T(8,128)(2,1)S(1)}, bf16[64,1024]{1,0:T(8,128)(2,1)S(1)}, u32[]{:S(2)}, u32[]{:S(2)}) collective-permute-start(bf16[64,1024]{1,0:T(8,128)(2,1)S(1)} %get-tuple-element.90), channel_id=1, source_target_pairs={{0,256},{128,384},{256,0},{384,128},{1,257},{129,385},{257,1},{385... | collective-permute-start | bytes 393224 | tf_op jit(solution)/shard_map/ppermute | solution.py:257
  94.0 2.5 %collective-permute-start.3 = (bf16[64,1024]{1,0:T(8,128)(2,1)S(1)}, bf16[64,1024]{1,0:T(8,128)(2,1)S(1)}, u32[]{:S(2)}, u32[]{:S(2)}) collective-permute-start(bf16[64,1024]{1,0:T(8,128)(2,1)S(1)} %get-tuple-element.89), channel_id=1, source_target_pairs={{0,384},{128,0},{256,128},{384,256},{1,385},{129,1},{257,129},{385... | collective-permute-start | bytes 393224 | tf_op jit(solution)/shard_map/ppermute | solution.py:257
  103.8 5.1 %collective-permute-start.4 = (bf16[16,64,256]{2,1,0:T(8,128)(2,1)S(1)}, bf16[16,64,256]{2,1,0:T(8,128)(2,1)S(1)}, u32[]{:S(2)}, u32[]{:S(2)}) collective-permute-start(bf16[16,64,256]{2,1,0:T(8,128)(2,1)S(1)} %get-tuple-element.61), channel_id=1, source_target_pairs={{0,16},{16,0},{1,17},{17,1},{2,18},{18,2},{3,19},{19,3},{4,20},{20... | collective-permute-start | bytes 1572872 | tf_op jit(solution)/shard_map/ppermute | solution.py:25
  111.6 3.5 %all-to-all-start.4 = ((bf16[4,384,256]{2,1,0:T(8,128)(2,1)}), bf16[4,384,256]{2,1,0:T(8,128)(2,1)S(1)}, u32[]{:S(2)}, u32[]{:S(2)}) async-start(bf16[4,384,256]{2,1,0:T(8,128)(2,1)} %pad_maximum_fusion.1), calls=%async_computation.4 | async-start | bytes 1572864 | tf_op jit(solution)/shard_map/all_to_all | solution.py:265
  115.1 4.9 %collective-permute-start.5 = (bf16[2,128,256]{2,1,0:T(8,128)(2,1)S(1)}, bf16[2,128,256]{2,1,0:T(8,128)(2,1)S(1)}, u32[]{:S(2)}, u32[]{:S(2)}) collective-permute-start(bf16[2,128,256]{2,1,0:T(8,128)(2,1)S(1)} %constant_dynamic-slice_fusion.3), channel_id=1, source_target_pairs={{0,8},{4,12},{8,0},{12,4},{1,9},{5,13},{9,1},{13,5},{2,10},{6,14},... | collective-permute-start | bytes 393224 | tf_op jit(solution)/shard_map/ppermute | solution.py:29
  120.2 3.2 %collective-permute-done.5 = bf16[2,128,256]{2,1,0:T(8,128)(2,1)S(1)} collective-permute-done((bf16[2,128,256]{2,1,0:T(8,128)(2,1)S(1)}, bf16[2,128,256]{2,1,0:T(8,128)(2,1)S(1)}, u32[]{:S(2)}, u32[]{:S(2)}) %collective-permute-start.5) | collective-permute-done | bytes 131104 | tf_op jit(solution)/shard_map/ppermute | solution.py:29
  123.5 3.6 %all-to-all-done.4.moved = bf16[4,384,256]{2,1,0:T(8,128)(2,1)S(1)} async-done(((bf16[4,384,256]{2,1,0:T(8,128)(2,1)}), bf16[4,384,256]{2,1,0:T(8,128)(2,1)S(1)}, u32[]{:S(2)}, u32[]{:S(2)}) %all-to-all-start.4) | async-done | bytes 786464 | tf_op jit(solution)/shard_map/all_to_all | solution.py:265
  128.4 3.1 %collective-permute-start.6 = (bf16[256,512]{1,0:T(8,128)(2,1)S(1)}, bf16[256,512]{1,0:T(8,128)(2,1)S(1)}, u32[]{:S(2)}, u32[]{:S(2)}) collective-permute-start(bf16[256,512]{1,0:T(8,128)(2,1)S(1)} %get-tuple-element.70), channel_id=1, source_target_pairs={{0,16},{16,0},{1,17},{17,1},{2,18},{18,2},{3,19},{19,3},{4,20},{20... | collective-permute-start | bytes 786440 | tf_op jit(solution)/shard_map/ppermute | solution.py:25
  133.5 12.6 %all-to-all-start.5 = ((bf16[4,64,768]{2,1,0:T(8,128)(2,1)}), bf16[4,64,768]{2,1,0:T(8,128)(2,1)S(1)}, u32[]{:S(2)}, u32[]{:S(2)}) async-start(bf16[4,64,768]{2,1,0:T(8,128)(2,1)} %bitcast.26), calls=%async_computation.5 | async-start | bytes 786432 | tf_op jit(solution)/shard_map/all_to_all | solution.py:21
  146.1 2.2 collective-permute-start.7
  151.1 2.5 %convolution_convert_fusion = bf16[128,2048]{1,0:T(8,128)(2,1)} fusion(bf16[2048,768]{1,0:T(8,128)(2,1)} %bitcast.15, bf16[128,256]{1,0:T(8,128)(2,1)S(1)} %collective-permute-done.7, bf16[2,128,256]{2,1,0:T(8,128)(2,1)S(1)} %add_convert_fusion.2, s32[]{:T(128)S(6)} %select_n.97), kind=kOutput, calls=%fused_computation.1 | convolution fusion | flops 134610944 | bytes 1703940 | tf_op jit(solution)/shard_map/dot_general | solution.py:277
  153.6 8.0 %all-to-all-done.5 = bf16[4,64,768]{2,1,0:T(8,128)(2,1)S(1)} async-done(((bf16[4,64,768]{2,1,0:T(8,128)(2,1)}), bf16[4,64,768]{2,1,0:T(8,128)(2,1)S(1)}, u32[]{:S(2)}, u32[]{:S(2)}) %all-to-all-start.5) | async-done | bytes 393248 | tf_op jit(solution)/shard_map/all_to_all | solution.py:21
  162.5 3.5 %all-to-all-start.6 = ((bf16[4,64,768]{2,1,0:T(8,128)(2,1)}), bf16[4,64,768]{2,1,0:T(8,128)(2,1)S(1)}, u32[]{:S(2)}, u32[]{:S(2)}) async-start(bf16[4,64,768]{2,1,0:T(8,128)(2,1)} %pad_maximum_fusion.4), calls=%async_computation.6 | async-start | bytes 786432 | tf_op jit(solution)/shard_map/all_to_all | solution.py:21
  166.0 16.7 %all_gather.7 = bf16[256,512]{1,0:T(8,128)(2,1)S(1)} all-gather(bf16[64,512]{1,0:T(8,128)(2,1)S(1)} %slice.78), channel_id=1, replica_groups=mesh['x'=4,'zh'=4,'co'=2,'y'=4,'zl'=4] {'zh'}, dimensions={0}, use_global_device_ids=true | all-gather | bytes 327680 | tf_op jit(solution)/shard_map/all_gather | solution.py:284
  183.8 3.5 %all-to-all-start.7 = ((bf16[4,256,512]{2,1,0:T(8,128)(2,1)}), bf16[4,256,512]{2,1,0:T(8,128)(2,1)S(1)}, u32[]{:S(2)}, u32[]{:S(2)}) async-start(bf16[4,256,512]{2,1,0:T(8,128)(2,1)} %broadcast_in_dim.23), calls=%async_computation.7 | async-start | bytes 2097152 | tf_op jit(solution)/shard_map/all_to_all | solution.py:287
  187.6 12.6 %collective-permute-start.8 = (bf16[64,512]{1,0:T(8,128)(2,1)S(1)}, bf16[64,512]{1,0:T(8,128)(2,1)S(1)}, u32[]{:S(2)}, u32[]{:S(2)}) collective-permute-start(bf16[64,512]{1,0:T(8,128)(2,1)S(1)} %pad_maximum_fusion.6), channel_id=1, source_target_pairs={{0,2},{1,3},{2,0},{3,1},{4,6},{5,7},{6,4},{7,5},{8,10},{9,11},{10,... | collective-permute-start | bytes 196616 | tf_op jit(solution)/shard_map/ppermute | solution.py:29
  201.8 9.5 %collective-permute-start.10 = (bf16[4,256,512]{2,1,0:T(8,128)(2,1)S(1)}, bf16[4,256,512]{2,1,0:T(8,128)(2,1)S(1)}, u32[]{:S(2)}, u32[]{:S(2)}) collective-permute-start(bf16[4,256,512]{2,1,0:T(8,128)(2,1)S(1)} %all-to-all-done.7.mine), channel_id=1, source_target_pairs={{0,16},{16,0},{1,17},{17,1},{2,18},{18,2},{3,19},{19,3},{4,20},{20... | collective-permute-start | bytes 3145736 | tf_op jit(solution)/shard_map/ppermute | solution.py:25
  211.5 5.8 %collective-permute-start.9 = (bf16[64,384]{1,0:T(8,128)(2,1)S(1)}, bf16[64,384]{1,0:T(8,128)(2,1)S(1)}, u32[]{:S(2)}, u32[]{:S(2)}) collective-permute-start(bf16[64,384]{1,0:T(8,128)(2,1)S(1)} %pad_maximum_fusion.8), channel_id=1, source_target_pairs={{0,1},{1,0},{2,3},{3,2},{4,5},{5,4},{6,7},{7,6},{8,9},{9,8},{10,11... | collective-permute-start | bytes 147464 | tf_op jit(solution)/shard_map/ppermute | solution.py:29
  217.3 2.1 collective-permute-done.9
  220.6 2.2 %shard_map.115 = (f32[2048,256]{1,0:T(8,128)}, bf16[256,2048]{1,0:T(8,128)(2,1)}) custom-call(s32[1]{0:T(128)} %bitcast.core, bf16[4,256,512]{2,1,0:T(8,128)(2,1)S(1)} %all-to-all-done.7.mine, bf16[4,256,512]{2,1,0:T(8,128)(2,1)S(1)} %collective-permute-done.10.theirs), custom_call_target="tpu_custom_call" | custom-call | tf_op jit(solution)/shard_map/pallas_call | solution.py:198
  (104 shorter events, 34.4 us)
Async XLA Ops:
  3.2 5.2 %copy-start.11 = (bf16[256,64]{0,1:T(8,128)(2,1)S(1)}, bf16[256,64]{0,1:T(8,128)(2,1)}, u32[]{:S(2)}) copy-start(bf16[256,64]{0,1:T(8,128)(2,1)} %param.12) | copy-start | bytes 98308
  3.3 5.2 %copy-start.12 = (bf16[64,256]{1,0:T(8,128)(2,1)S(1)}, bf16[64,256]{1,0:T(8,128)(2,1)}, u32[]{:S(2)}) copy-start(bf16[64,256]{1,0:T(8,128)(2,1)} %param.11) | copy-start | bytes 98308
  3.3 5.2 %copy-start.13 = (bf16[64,256]{1,0:T(8,128)(2,1)S(1)}, bf16[64,256]{1,0:T(8,128)(2,1)}, u32[]{:S(2)}) copy-start(bf16[64,256]{1,0:T(8,128)(2,1)} %param.10) | copy-start | bytes 98308
  3.3 30.7 %all-to-all-start = ((bf16[4,128,2048]{2,1,0:T(8,128)(2,1)}), bf16[4,128,2048]{2,1,0:T(8,128)(2,1)S(1)}, u32[]{:S(2)}, u32[]{:S(2)}) async-start(bf16[4,128,2048]{2,1,0:T(8,128)(2,1)} %broadcast_in_dim.19), calls=%async_computation | async-start | bytes 4194304 | tf_op jit(solution)/shard_map/all_to_all | solution.py:17
  33.9 1.8 copy-start
  33.9 5.9 %copy-start.9 = (bf16[1,64,2048]{2,1,0:T(8,128)(2,1)S(1)}, bf16[1,64,2048]{2,1,0:T(8,128)(2,1)}, u32[]{:S(2)}) copy-start(bf16[1,64,2048]{2,1,0:T(8,128)(2,1)} %param.7) | copy-start | bytes 786436
  35.2 5.1 %copy-start.10 = (bf16[1,64,2048]{2,1,0:T(8,128)(2,1)S(1)}, bf16[1,64,2048]{2,1,0:T(8,128)(2,1)}, u32[]{:S(2)}) copy-start(bf16[1,64,2048]{2,1,0:T(8,128)(2,1)} %param.13) | copy-start | bytes 786436
  35.8 18.7 %all-to-all-start.1 = ((bf16[4,256,768]{2,1,0:T(8,128)(2,1)}), bf16[4,256,768]{2,1,0:T(8,128)(2,1)S(1)}, u32[]{:S(2)}, u32[]{:S(2)}) async-start(bf16[4,256,768]{2,1,0:T(8,128)(2,1)} %broadcast_in_dim.20), calls=%async_computation.1 | async-start | bytes 3145728 | tf_op jit(solution)/shard_map/all_to_all | solution.py:17
  41.0 22.8 %copy-start.14 = (s32[1,16]{1,0:T(1,128)S(1)}, s32[1,16]{1,0:T(1,128)}, u32[]{:S(2)}) copy-start(s32[1,16]{1,0:T(1,128)} %param.9) | copy-start | bytes 196
  54.5 12.4 %collective-permute-start = (bf16[1024,768]{1,0:T(8,128)(2,1)S(1)}, bf16[1024,768]{1,0:T(8,128)(2,1)S(1)}, u32[]{:S(2)}, u32[]{:S(2)}) collective-permute-start(bf16[1024,768]{1,0:T(8,128)(2,1)S(1)} %bitcast.74), channel_id=1, source_target_pairs={{0,16},{16,0},{1,17},{17,1},{2,18},{18,2},{3,19},{19,3},{4,20},{20... | collective-permute-start | bytes 4718600 | tf_op jit(solution)/shard_map/ppermute | solution.py:25
  64.6 2.2 %copy-start.2 = (bf16[2,64,1024]{2,1,0:T(8,128)(2,1)S(1)}, bf16[2,64,1024]{2,1,0:T(8,128)(2,1)}, u32[]{:S(2)}) copy-start(bf16[2,64,1024]{2,1,0:T(8,128)(2,1)} %reshape_squeeze.11.odd) | copy-start | bytes 786436
  68.1 13.0 %all-to-all-start.2 = ((bf16[4,64,512]{2,1,0:T(8,128)(2,1)}), bf16[4,64,512]{2,1,0:T(8,128)(2,1)S(1)}, u32[]{:S(2)}, u32[]{:S(2)}) async-start(bf16[4,64,512]{2,1,0:T(8,128)(2,1)} %broadcast_in_dim.21), calls=%async_computation.2 | async-start | bytes 524288 | tf_op jit(solution)/shard_map/all_to_all | solution.py:17
  73.8 2.4 %copy-start.1 = (bf16[4,128,2048]{2,1,0:T(8,128)(2,1)S(1)}, bf16[4,128,2048]{2,1,0:T(8,128)(2,1)}, u32[]{:S(2)}) copy-start(bf16[4,128,2048]{2,1,0:T(8,128)(2,1)} %copy-done) | copy-start | bytes 6291460
  83.4 17.8 %all-to-all-start.3 = ((bf16[4,64,896]{2,1,0:T(8,128)(2,1)}), bf16[4,64,896]{2,1,0:T(8,128)(2,1)S(1)}, u32[]{:S(2)}, u32[]{:S(2)}) async-start(bf16[4,64,896]{2,1,0:T(8,128)(2,1)} %shard_map.111), calls=%async_computation.3 | async-start | bytes 917504 | tf_op jit(solution)/shard_map/all_to_all | solution.py:252
  88.1 8.4 %collective-permute-start.1 = (bf16[64,1024]{1,0:T(8,128)(2,1)S(1)}, bf16[64,1024]{1,0:T(8,128)(2,1)S(1)}, u32[]{:S(2)}, u32[]{:S(2)}) collective-permute-start(bf16[64,1024]{1,0:T(8,128)(2,1)S(1)} %get-tuple-element.91), channel_id=1, source_target_pairs={{0,128},{128,256},{256,384},{384,0},{1,129},{129,257},{257,385},{3... | collective-permute-start | bytes 393224 | tf_op jit(solution)/shard_map/ppermute | solution.py:257
  90.3 8.4 %collective-permute-start.2 = (bf16[64,1024]{1,0:T(8,128)(2,1)S(1)}, bf16[64,1024]{1,0:T(8,128)(2,1)S(1)}, u32[]{:S(2)}, u32[]{:S(2)}) collective-permute-start(bf16[64,1024]{1,0:T(8,128)(2,1)S(1)} %get-tuple-element.90), channel_id=1, source_target_pairs={{0,256},{128,384},{256,0},{384,128},{1,257},{129,385},{257,1},{385... | collective-permute-start | bytes 393224 | tf_op jit(solution)/shard_map/ppermute | solution.py:257
  94.0 6.6 %collective-permute-start.3 = (bf16[64,1024]{1,0:T(8,128)(2,1)S(1)}, bf16[64,1024]{1,0:T(8,128)(2,1)S(1)}, u32[]{:S(2)}, u32[]{:S(2)}) collective-permute-start(bf16[64,1024]{1,0:T(8,128)(2,1)S(1)} %get-tuple-element.89), channel_id=1, source_target_pairs={{0,384},{128,0},{256,128},{384,256},{1,385},{129,1},{257,129},{385... | collective-permute-start | bytes 393224 | tf_op jit(solution)/shard_map/ppermute | solution.py:257
  96.5 0.7 copy-start.3
  103.8 6.6 %collective-permute-start.4 = (bf16[16,64,256]{2,1,0:T(8,128)(2,1)S(1)}, bf16[16,64,256]{2,1,0:T(8,128)(2,1)S(1)}, u32[]{:S(2)}, u32[]{:S(2)}) collective-permute-start(bf16[16,64,256]{2,1,0:T(8,128)(2,1)S(1)} %get-tuple-element.61), channel_id=1, source_target_pairs={{0,16},{16,0},{1,17},{17,1},{2,18},{18,2},{3,19},{19,3},{4,20},{20... | collective-permute-start | bytes 1572872 | tf_op jit(solution)/shard_map/ppermute | solution.py:25
  110.6 16.5 %copy-start.4 = (bf16[64,1024]{1,0:T(8,128)(2,1)S(1)}, bf16[64,1024]{1,0:T(8,128)(2,1)}, u32[]{:S(2)}) copy-start(bf16[64,1024]{1,0:T(8,128)(2,1)} %copy-done.3) | copy-start | bytes 393220
  110.6 16.5 %copy-start.6 = (bf16[64,1024]{1,0:T(8,128)(2,1)S(1)}, bf16[64,1024]{1,0:T(8,128)(2,1)}, u32[]{:S(2)}) copy-start(bf16[64,1024]{1,0:T(8,128)(2,1)} %copy-done.5) | copy-start | bytes 393220
  110.6 16.5 %copy-start.8 = (bf16[64,1024]{1,0:T(8,128)(2,1)S(1)}, bf16[64,1024]{1,0:T(8,128)(2,1)}, u32[]{:S(2)}) copy-start(bf16[64,1024]{1,0:T(8,128)(2,1)} %copy-done.7) | copy-start | bytes 393220
  111.6 15.5 %all-to-all-start.4 = ((bf16[4,384,256]{2,1,0:T(8,128)(2,1)}), bf16[4,384,256]{2,1,0:T(8,128)(2,1)S(1)}, u32[]{:S(2)}, u32[]{:S(2)}) async-start(bf16[4,384,256]{2,1,0:T(8,128)(2,1)} %pad_maximum_fusion.1), calls=%async_computation.4 | async-start | bytes 1572864 | tf_op jit(solution)/shard_map/all_to_all | solution.py:265
  115.1 8.3 %collective-permute-start.5 = (bf16[2,128,256]{2,1,0:T(8,128)(2,1)S(1)}, bf16[2,128,256]{2,1,0:T(8,128)(2,1)S(1)}, u32[]{:S(2)}, u32[]{:S(2)}) collective-permute-start(bf16[2,128,256]{2,1,0:T(8,128)(2,1)S(1)} %constant_dynamic-slice_fusion.3), channel_id=1, source_target_pairs={{0,8},{4,12},{8,0},{12,4},{1,9},{5,13},{9,1},{13,5},{2,10},{6,14},... | collective-permute-start | bytes 393224 | tf_op jit(solution)/shard_map/ppermute | solution.py:29
  128.4 4.3 %collective-permute-start.6 = (bf16[256,512]{1,0:T(8,128)(2,1)S(1)}, bf16[256,512]{1,0:T(8,128)(2,1)S(1)}, u32[]{:S(2)}, u32[]{:S(2)}) collective-permute-start(bf16[256,512]{1,0:T(8,128)(2,1)S(1)} %get-tuple-element.70), channel_id=1, source_target_pairs={{0,16},{16,0},{1,17},{17,1},{2,18},{18,2},{3,19},{19,3},{4,20},{20... | collective-permute-start | bytes 786440 | tf_op jit(solution)/shard_map/ppermute | solution.py:25
  133.5 28.1 %all-to-all-start.5 = ((bf16[4,64,768]{2,1,0:T(8,128)(2,1)}), bf16[4,64,768]{2,1,0:T(8,128)(2,1)S(1)}, u32[]{:S(2)}, u32[]{:S(2)}) async-start(bf16[4,64,768]{2,1,0:T(8,128)(2,1)} %bitcast.26), calls=%async_computation.5 | async-start | bytes 786432 | tf_op jit(solution)/shard_map/all_to_all | solution.py:21
  146.1 5.0 %collective-permute-start.7 = (bf16[128,256]{1,0:T(8,128)(2,1)S(1)}, bf16[128,256]{1,0:T(8,128)(2,1)S(1)}, u32[]{:S(2)}, u32[]{:S(2)}) collective-permute-start(bf16[128,256]{1,0:T(8,128)(2,1)S(1)} %dynamic-slice_bitcast_fusion.4), channel_id=1, source_target_pairs={{0,4},{4,0},{8,12},{12,8},{1,5},{5,1},{9,13},{13,9},{2,6},{6,2},{1... | collective-permute-start | bytes 196616 | tf_op jit(solution)/shard_map/ppermute | solution.py:29
  162.5 20.2 %all-to-all-start.6 = ((bf16[4,64,768]{2,1,0:T(8,128)(2,1)}), bf16[4,64,768]{2,1,0:T(8,128)(2,1)S(1)}, u32[]{:S(2)}, u32[]{:S(2)}) async-start(bf16[4,64,768]{2,1,0:T(8,128)(2,1)} %pad_maximum_fusion.4), calls=%async_computation.6 | async-start | bytes 786432 | tf_op jit(solution)/shard_map/all_to_all | solution.py:21
  183.8 18.0 %all-to-all-start.7 = ((bf16[4,256,512]{2,1,0:T(8,128)(2,1)}), bf16[4,256,512]{2,1,0:T(8,128)(2,1)S(1)}, u32[]{:S(2)}, u32[]{:S(2)}) async-start(bf16[4,256,512]{2,1,0:T(8,128)(2,1)} %broadcast_in_dim.23), calls=%async_computation.7 | async-start | bytes 2097152 | tf_op jit(solution)/shard_map/all_to_all | solution.py:287
  187.6 14.2 %collective-permute-start.8 = (bf16[64,512]{1,0:T(8,128)(2,1)S(1)}, bf16[64,512]{1,0:T(8,128)(2,1)S(1)}, u32[]{:S(2)}, u32[]{:S(2)}) collective-permute-start(bf16[64,512]{1,0:T(8,128)(2,1)S(1)} %pad_maximum_fusion.6), channel_id=1, source_target_pairs={{0,2},{1,3},{2,0},{3,1},{4,6},{5,7},{6,4},{7,5},{8,10},{9,11},{10,... | collective-permute-start | bytes 196616 | tf_op jit(solution)/shard_map/ppermute | solution.py:29
  201.8 18.8 %collective-permute-start.10 = (bf16[4,256,512]{2,1,0:T(8,128)(2,1)S(1)}, bf16[4,256,512]{2,1,0:T(8,128)(2,1)S(1)}, u32[]{:S(2)}, u32[]{:S(2)}) collective-permute-start(bf16[4,256,512]{2,1,0:T(8,128)(2,1)S(1)} %all-to-all-done.7.mine), channel_id=1, source_target_pairs={{0,16},{16,0},{1,17},{17,1},{2,18},{18,2},{3,19},{19,3},{4,20},{20... | collective-permute-start | bytes 3145736 | tf_op jit(solution)/shard_map/ppermute | solution.py:25
  211.5 7.9 %collective-permute-start.9 = (bf16[64,384]{1,0:T(8,128)(2,1)S(1)}, bf16[64,384]{1,0:T(8,128)(2,1)S(1)}, u32[]{:S(2)}, u32[]{:S(2)}) collective-permute-start(bf16[64,384]{1,0:T(8,128)(2,1)S(1)} %pad_maximum_fusion.8), channel_id=1, source_target_pairs={{0,1},{1,0},{2,3},{3,2},{4,5},{5,4},{6,7},{7,6},{8,9},{9,8},{10,11... | collective-permute-start | bytes 147464 | tf_op jit(solution)/shard_map/ppermute | solution.py:29
  (2 other events, 1.3 us)

commit v4 on v3

--- a/solution.py
+++ b/solution.py
@@ -261,43 +261,36 @@
     keep, send = call(key_term_kernel, [(16, 64, 256)] * 2, core, kv_part, enc_four)
     kv_chip = join(keep, swap(send)).reshape(4, 256, 256)
     messages = jnp.concatenate([jnp.broadcast_to(heads[None], (4, 128, 256)), kv_chip], 1)
-    messages, kv_part = together(messages, kv_part)
+    messages, heads = together(messages, heads)
     moved_x = lax.all_to_all(messages, "x", 0, 0)
-    kv_two = halve(kv_part.reshape(4, PT, 256), "y")
-    moved_x, kv_two = together(moved_x, kv_two)
+    dec_part = jnp.dot(heads[64:], wq_full.T, preferred_element_type=f32).astype(bf16)
+    dec_two = halve(dec_part.reshape(64, 4, 4, 128).transpose(2, 0, 1, 3).reshape(4, 64, 512), "zl")
+    moved_x, dec_two = together(moved_x, dec_two)
     sources = jnp.concatenate([core] + [lax.rem(x + 4 - step, 4).reshape(1) for step in range(4)])
     keep, send, kv_sum = call(
         head_term_kernel, [(256, 512), (256, 512), (256, 256)], sources, moved_x, *rows_x
     )
     sum_x = jnp.concatenate([join(keep, swap(send)), kv_sum], 1)
-    sum_x, kv_two, heads = together(sum_x, kv_two, heads)
+    sum_x, kv_part, dec_two = together(sum_x, kv_part, dec_two)
 
     sum_z = exchange(sum_x.reshape(4, 64, 768), "zh")
-    kv_grad = halve_again(kv_two, "y")
-    enc_grad = jnp.dot(kv_grad, wkv_full.T, preferred_element_type=f32).astype(bf16)
-    dec_part = jnp.dot(heads[64:], wq_full.T, preferred_element_type=f32).astype(bf16)
-    dec_part = dec_part.reshape(64, 4, 512).transpose(1, 0, 2)
-    sum_z, dec_part, enc_grad = together(sum_z, dec_part, enc_grad)
-
-    last = jnp.concatenate([jnp.broadcast_to(sum_z[None, :, 512:], (4, 64, 256)), dec_part], 2)
+    rest = [
+        halve_again(dec_two, "zl").reshape(64, 4, 128).transpose(1, 0, 2),
+        kv_part.reshape(4, 2, 64, 256).transpose(0, 2, 1, 3).reshape(4, 64, 512),
+    ]
+    sum_z, *rest = together(sum_z, *rest)
+
+    last = jnp.concatenate([jnp.broadcast_to(sum_z[None, :, 512:], (4, 64, 256)), *rest], 2)
     last = exchange(last, "y")
     mine = lax.all_gather(sum_z[:, :512], "zh", axis=0, tiled=True)
     copies = jnp.broadcast_to(mine[None], (4, 256, 512))
     copies, last = together(copies, last)
     mine = lax.all_to_all(copies, "x", 0, 0)
-    high, low = zl // 2, lax.rem(zl, 2)
-    parts = last[:, 256:].reshape(64, 2, 256)
-    ahead = lax.dynamic_index_in_dim(parts, 1 - high, 1, keepdims=False)
-    back = meet(jnp.concatenate([last[:, :256], ahead], 1), "zl", 2)
-    here = lax.dynamic_index_in_dim(parts, high, 1, keepdims=False)
-    last = join(jnp.concatenate([last[:, :256], here], 1), back)
-    mine, last = together(mine, last)
-    parts = last[:, 256:].reshape(64, 2, 128)
-    ahead = lax.dynamic_index_in_dim(parts, 1 - low, 1, keepdims=False)
-    back = meet(jnp.concatenate([last[:, :256], ahead], 1), "zl", 1).astype(f32)
-    here = lax.dynamic_index_in_dim(parts, low, 1, keepdims=False)
-    kv_weight_grad = last[:, :256].astype(f32) + back[:, :256]
-    dec_grad = (here.astype(f32) + back[:, 256:]).astype(bf16)
+    dec_grad = last[:, 256:384]
+    kv_grad = jnp.concatenate([last[:, 384:640], last[:, 640:]], 0)
+    enc_grad = jnp.dot(kv_grad, wkv_full.T, preferred_element_type=f32).astype(bf16)
+    kv_weight_grad = jnp.sum(lax.all_gather(last[:, :256], "zl", axis=0).astype(f32), 0)
+    mine, kv_weight_grad, enc_grad = together(mine, kv_weight_grad, enc_grad)
     q_weight_grad, o_weight_grad = place(core, mine, swap(mine))
     return (dec_grad[None], enc_grad[None], q_weight_grad, kv_weight_grad, o_weight_grad)
 

time: 224 us -> 230 us (1.027)
  blocking collectives: 42.1 us -> 58.4 us
  starting transfers between devices: 102 us -> 87.6 us
    ppermute x4 -> x2, starting transfers between devices: 25.5 us -> 7.29 us  [meet(): return lax.ppermute(block, axis, [(i, i ^ bit) for i in range(4)])]
    ppermute x4 -> x2, waiting for transfers between devices: 8.05 us -> 19.5 us  [meet(): return lax.ppermute(block, axis, [(i, i ^ bit) for i in range(4)])]
    all_gather x0 -> x1, blocking collectives: none -> 10.5 us  [local(): lax.all_gather(last[:, :256], 'zl', axis=0).astype(f32)]
    all_to_all x2, waiting for transfers between devices: 8.02 us -> 0.01 us  [exchange(): lax.all_to_all(parts, axis, 0, 0).astype(f32)]
    all_gather x1, blocking collectives: 16.7 us -> 22.4 us  [local(): mine = lax.all_gather(sum_z[:, :512], 'zh', axis=0, tiled=True)]
    all_to_all x1, waiting for transfers between devices: 3.64 us -> 0.01 us  [local(): moved_x = lax.all_to_all(messages, 'x', 0, 0)]
    all_to_all x1, starting transfers between devices: 3.52 us -> 6.39 us  [local(): mine = lax.all_to_all(copies, 'x', 0, 0)]
  transfers between devices with their start and end apart: 19 -> 17, of which waited for: 12 -> 9; matrix products, arithmetic and copies ran while one was open for 8% -> 8% of each run, Pallas kernels for 0% -> 0%
where the time goes in v4:
time: 230 us; the launch traced here: 228 us
  starting transfers between devices  87.6 us (38%)
  blocking collectives  58.4 us (25%)
  waiting for transfers between devices  41.6 us (18%)
  local copies, waits for them, and re-layouts  16.1 us (7%)
  Pallas kernels  9.79 us (4%)
  other arithmetic  7.28 us (3%)
  matrix products  6.13 us (3%)
    ppermute x4, starting transfers between devices, swap(): return lax.ppermute(block, 'co', [(0, 1), (1, 0)])  27.8 us
    all_gather x1, blocking collectives, local(): own = lax.all_gather(shard, 'zh', axis=0, tiled=True)  25.5 us
    all_gather x1, blocking collectives, local(): mine = lax.all_gather(sum_z[:, :512], 'zh', axis=0, tiled=True)  22.4 us
    ppermute x2, waiting for transfers between devices, meet(): return lax.ppermute(block, axis, [(i, i ^ bit) for i in range(4)])  19.5 us
    all_to_all x2, starting transfers between devices, exchange(): lax.all_to_all(parts, axis, 0, 0).astype(f32)  16 us
    all_to_all x3, waiting for transfers between devices, spread(): return lax.all_to_all(copies, axis, 0, 0)  14.9 us
    all_to_all x3, starting transfers between devices, spread(): return lax.all_to_all(copies, axis, 0, 0)  14.7 us
    all_gather x1, blocking collectives, local(): lax.all_gather(last[:, :256], 'zl', axis=0).astype(f32)  10.5 us
  transfers between devices with their start and end apart: 17, of which 9 were waited for; matrix products, arithmetic and copies ran while one was open for 8% of the time, Pallas kernels for 0%

profile of v4, /device:TPU:1, one launch (start us, length us, event | category | flops | bytes accessed | tf_op | source)
XLA Modules:
  0.0 228.0 jit_solution(11626740210580950866)
XLA Ops:
  0.6 2.6 %broadcast_in_dim.19 = bf16[4,128,2048]{2,1,0:T(8,128)(2,1)} broadcast(bf16[128,2048]{1,0:T(8,128)(2,1)} %bitcast.85), dimensions={1,2} | broadcast | bytes 2621440 | tf_op jit(solution)/shard_map/broadcast_in_dim | solution.py:16
  3.3 5.1 %all-to-all-start = ((bf16[4,128,2048]{2,1,0:T(8,128)(2,1)}), bf16[4,128,2048]{2,1,0:T(8,128)(2,1)S(1)}, u32[]{:S(2)}, u32[]{:S(2)}) async-start(bf16[4,128,2048]{2,1,0:T(8,128)(2,1)} %broadcast_in_dim.19), calls=%async_computation | async-start | bytes 4194304 | tf_op jit(solution)/shard_map/all_to_all | solution.py:17
  8.4 25.5 %all_gather.12 = bf16[256,768]{1,0:T(8,128)(2,1)S(1)} all-gather(bf16[64,768]{1,0:T(8,128)(2,1)S(1)} %pad_maximum_fusion.5), channel_id=1, replica_groups=mesh['x'=4,'zh'=4,'co'=2,'y'=4,'zl'=4] {'zh'}, dimensions={0}, use_global_device_ids=true | all-gather | bytes 491520 | tf_op jit(solution)/shard_map/all_gather | solution.py:226
  35.8 4.0 %all-to-all-start.1 = ((bf16[4,256,768]{2,1,0:T(8,128)(2,1)}), bf16[4,256,768]{2,1,0:T(8,128)(2,1)S(1)}, u32[]{:S(2)}, u32[]{:S(2)}) async-start(bf16[4,256,768]{2,1,0:T(8,128)(2,1)} %broadcast_in_dim.20), calls=%async_computation.1 | async-start | bytes 3145728 | tf_op jit(solution)/shard_map/all_to_all | solution.py:17
  42.6 11.9 %all-to-all-done.1 = bf16[4,256,768]{2,1,0:T(8,128)(2,1)S(1)} async-done(((bf16[4,256,768]{2,1,0:T(8,128)(2,1)}), bf16[4,256,768]{2,1,0:T(8,128)(2,1)S(1)}, u32[]{:S(2)}, u32[]{:S(2)}) %all-to-all-start.1) | async-done | bytes 1572896 | tf_op jit(solution)/shard_map/all_to_all | solution.py:17
  54.5 8.8 %collective-permute-start = (bf16[1024,768]{1,0:T(8,128)(2,1)S(1)}, bf16[1024,768]{1,0:T(8,128)(2,1)S(1)}, u32[]{:S(2)}, u32[]{:S(2)}) collective-permute-start(bf16[1024,768]{1,0:T(8,128)(2,1)S(1)} %bitcast.70), channel_id=1, source_target_pairs={{0,16},{16,0},{1,17},{17,1},{2,18},{18,2},{3,19},{19,3},{4,20},{20... | collective-permute-start | bytes 4718600 | tf_op jit(solution)/shard_map/ppermute | solution.py:25
  68.1 5.5 %all-to-all-start.2 = ((bf16[4,64,512]{2,1,0:T(8,128)(2,1)}), bf16[4,64,512]{2,1,0:T(8,128)(2,1)S(1)}, u32[]{:S(2)}, u32[]{:S(2)}) async-start(bf16[4,64,512]{2,1,0:T(8,128)(2,1)} %broadcast_in_dim.21), calls=%async_computation.2 | async-start | bytes 524288 | tf_op jit(solution)/shard_map/all_to_all | solution.py:17
  73.8 1.9 pad_maximum_fusion
  76.2 1.9 convolution_convert_fusion.2.kv
  78.1 3.0 %all-to-all-done.2.qa = bf16[4,64,512]{2,1,0:T(8,128)(2,1)S(1)} async-done(((bf16[4,64,512]{2,1,0:T(8,128)(2,1)}), bf16[4,64,512]{2,1,0:T(8,128)(2,1)S(1)}, u32[]{:S(2)}, u32[]{:S(2)}) %all-to-all-start.2) | async-done | bytes 262176 | tf_op jit(solution)/shard_map/all_to_all | solution.py:17
  81.1 2.3 %shard_map.111 = bf16[4,64,896]{2,1,0:T(8,128)(2,1)} custom-call(s32[4]{0:T(128)S(1)} %fusion.9.lengths, bf16[4,64,512]{2,1,0:T(8,128)(2,1)S(1)} %all-to-all-done.2.qa, bf16[512,256]{1,0:T(8,128)(2,1)S(1)} %convolution_convert_fusion.2.kv), custom_call_target="tpu_custom_call" | custom-call | tf_op jit(solution)/shard_map/pallas_call | solution.py:187
  83.4 3.5 %all-to-all-start.3 = ((bf16[4,64,896]{2,1,0:T(8,128)(2,1)}), bf16[4,64,896]{2,1,0:T(8,128)(2,1)S(1)}, u32[]{:S(2)}, u32[]{:S(2)}) async-start(bf16[4,64,896]{2,1,0:T(8,128)(2,1)} %shard_map.111), calls=%async_computation.3 | async-start | bytes 917504 | tf_op jit(solution)/shard_map/all_to_all | solution.py:252
  88.1 2.2 collective-permute-start.1
  90.3 3.7 %collective-permute-start.2 = (bf16[64,1024]{1,0:T(8,128)(2,1)S(1)}, bf16[64,1024]{1,0:T(8,128)(2,1)S(1)}, u32[]{:S(2)}, u32[]{:S(2)}) collective-permute-start(bf16[64,1024]{1,0:T(8,128)(2,1)S(1)} %get-tuple-element.92), channel_id=1, source_target_pairs={{0,256},{128,384},{256,0},{384,128},{1,257},{129,385},{257,1},{385... | collective-permute-start | bytes 393224 | tf_op jit(solution)/shard_map/ppermute | solution.py:257
  94.0 2.5 %collective-permute-start.3 = (bf16[64,1024]{1,0:T(8,128)(2,1)S(1)}, bf16[64,1024]{1,0:T(8,128)(2,1)S(1)}, u32[]{:S(2)}, u32[]{:S(2)}) collective-permute-start(bf16[64,1024]{1,0:T(8,128)(2,1)S(1)} %get-tuple-element.91), channel_id=1, source_target_pairs={{0,384},{128,0},{256,128},{384,256},{1,385},{129,1},{257,129},{385... | collective-permute-start | bytes 393224 | tf_op jit(solution)/shard_map/ppermute | solution.py:257
  101.2 1.8 shard_map.112
  104.6 5.1 %collective-permute-start.4 = (bf16[16,64,256]{2,1,0:T(8,128)(2,1)}, bf16[16,64,256]{2,1,0:T(8,128)(2,1)S(1)}, u32[]{:S(2)}, u32[]{:S(2)}) collective-permute-start(bf16[16,64,256]{2,1,0:T(8,128)(2,1)} %get-tuple-element.62), channel_id=1, source_target_pairs={{0,16},{16,0},{1,17},{17,1},{2,18},{18,2},{3,19},{19,3},{4,20},{20... | collective-permute-start | bytes 1572872 | tf_op jit(solution)/shard_map/ppermute | solution.py:25
  112.5 3.5 %all-to-all-start.4 = ((bf16[4,384,256]{2,1,0:T(8,128)(2,1)}), bf16[4,384,256]{2,1,0:T(8,128)(2,1)S(1)}, u32[]{:S(2)}, u32[]{:S(2)}) async-start(bf16[4,384,256]{2,1,0:T(8,128)(2,1)} %pad_maximum_fusion.1), calls=%async_computation.4 | async-start | bytes 1572864 | tf_op jit(solution)/shard_map/all_to_all | solution.py:265
  116.1 1.7 convolution_convert_fusion.1
  118.2 4.5 %collective-permute-start.5 = (bf16[2,64,512]{2,1,0:T(8,128)(2,1)S(1)}, bf16[2,64,512]{2,1,0:T(8,128)(2,1)S(1)}, u32[]{:S(2)}, u32[]{:S(2)}) collective-permute-start(bf16[2,64,512]{2,1,0:T(8,128)(2,1)S(1)} %constant_dynamic-slice_fusion), channel_id=1, source_target_pairs={{0,2},{1,3},{2,0},{3,1},{4,6},{5,7},{6,4},{7,5},{8,10},{9,11},{10,... | collective-permute-start | bytes 393224 | tf_op jit(solution)/shard_map/ppermute | solution.py:29
  122.8 6.2 %collective-permute-done.5 = bf16[2,64,512]{2,1,0:T(8,128)(2,1)S(1)} collective-permute-done((bf16[2,64,512]{2,1,0:T(8,128)(2,1)S(1)}, bf16[2,64,512]{2,1,0:T(8,128)(2,1)S(1)}, u32[]{:S(2)}, u32[]{:S(2)}) %collective-permute-start.5) | collective-permute-done | bytes 131104 | tf_op jit(solution)/shard_map/ppermute | solution.py:29
  130.4 2.9 %collective-permute-start.6 = (bf16[256,512]{1,0:T(8,128)(2,1)S(1)}, bf16[256,512]{1,0:T(8,128)(2,1)S(1)}, u32[]{:S(2)}, u32[]{:S(2)}) collective-permute-start(bf16[256,512]{1,0:T(8,128)(2,1)S(1)} %get-tuple-element.71), channel_id=1, source_target_pairs={{0,16},{16,0},{1,17},{17,1},{2,18},{18,2},{3,19},{19,3},{4,20},{20... | collective-permute-start | bytes 786440 | tf_op jit(solution)/shard_map/ppermute | solution.py:25
  135.3 12.6 %all-to-all-start.5 = ((bf16[4,64,768]{2,1,0:T(8,128)(2,1)}), bf16[4,64,768]{2,1,0:T(8,128)(2,1)S(1)}, u32[]{:S(2)}, u32[]{:S(2)}) async-start(bf16[4,64,768]{2,1,0:T(8,128)(2,1)} %bitcast.26), calls=%async_computation.5 | async-start | bytes 786432 | tf_op jit(solution)/shard_map/all_to_all | solution.py:21
  147.8 2.8 %collective-permute-start.7 = (bf16[64,512]{1,0:T(8,128)(2,1)S(1)}, bf16[64,512]{1,0:T(8,128)(2,1)S(1)}, u32[]{:S(2)}, u32[]{:S(2)}) collective-permute-start(bf16[64,512]{1,0:T(8,128)(2,1)S(1)} %dynamic-slice_bitcast_fusion.4), channel_id=1, source_target_pairs={{0,1},{1,0},{2,3},{3,2},{4,5},{5,4},{6,7},{7,6},{8,9},{9,8},{10,11... | collective-permute-start | bytes 196616 | tf_op jit(solution)/shard_map/ppermute | solution.py:29
  151.1 13.3 %collective-permute-done.7 = bf16[64,512]{1,0:T(8,128)(2,1)S(1)} collective-permute-done((bf16[64,512]{1,0:T(8,128)(2,1)S(1)}, bf16[64,512]{1,0:T(8,128)(2,1)S(1)}, u32[]{:S(2)}, u32[]{:S(2)}) %collective-permute-start.7) | collective-permute-done | bytes 65568 | tf_op jit(solution)/shard_map/ppermute | solution.py:29
  165.4 3.5 %all-to-all-start.6 = ((bf16[4,64,896]{2,1,0:T(8,128)(2,1)}), bf16[4,64,896]{2,1,0:T(8,128)(2,1)S(1)}, u32[]{:S(2)}, u32[]{:S(2)}) async-start(bf16[4,64,896]{2,1,0:T(8,128)(2,1)} %pad_maximum_fusion.3), calls=%async_computation.6 | async-start | bytes 917504 | tf_op jit(solution)/shard_map/all_to_all | solution.py:21
  168.9 22.4 %all_gather.13 = bf16[256,512]{1,0:T(8,128)(2,1)S(1)} all-gather(bf16[64,512]{1,0:T(8,128)(2,1)S(1)} %slice.70), channel_id=1, replica_groups=mesh['x'=4,'zh'=4,'co'=2,'y'=4,'zl'=4] {'zh'}, dimensions={0}, use_global_device_ids=true | all-gather | bytes 327680 | tf_op jit(solution)/shard_map/all_gather | solution.py:285
  192.4 6.4 %all-to-all-start.7 = ((bf16[4,256,512]{2,1,0:T(8,128)(2,1)}), bf16[4,256,512]{2,1,0:T(8,128)(2,1)S(1)}, u32[]{:S(2)}, u32[]{:S(2)}) async-start(bf16[4,256,512]{2,1,0:T(8,128)(2,1)} %broadcast_in_dim.23), calls=%async_computation.7 | async-start | bytes 2097152 | tf_op jit(solution)/shard_map/all_to_all | solution.py:288
  198.8 10.5 %all-gather = bf16[256,256]{1,0:T(8,128)(2,1)S(1)} all-gather(bf16[64,256]{1,0:T(8,128)(2,1)S(1)} %get-tuple-element.105), channel_id=2, replica_groups=mesh['x'=4,'zh'=4,'co'=2,'y'=4,'zl'=4] {'zl'}, dimensions={0}, use_global_device_ids=true | all-gather | bytes 163840 | tf_op jit(solution)/shard_map/all_gather | solution.py:292
  209.9 2.5 %convolution_convert_fusion = bf16[128,2048]{1,0:T(8,128)(2,1)} fusion(bf16[2048,768]{1,0:T(8,128)(2,1)} %bitcast.15, bf16[64,256]{1,0:T(8,128)(2,1)S(1)} %get-tuple-element.104, bf16[64,256]{1,0:T(8,128)(2,1)S(1)} %get-tuple-element.103), kind=kOutput, calls=%fused_computation.1 | convolution fusion | flops 134610944 | bytes 1638400 | tf_op jit(solution)/shard_map/dot_general | solution.py:291
  212.4 11.1 %collective-permute-start.8 = (bf16[4,256,512]{2,1,0:T(8,128)(2,1)S(1)}, bf16[4,256,512]{2,1,0:T(8,128)(2,1)S(1)}, u32[]{:S(2)}, u32[]{:S(2)}) collective-permute-start(bf16[4,256,512]{2,1,0:T(8,128)(2,1)S(1)} %all-to-all-done.7.mine), channel_id=1, source_target_pairs={{0,16},{16,0},{1,17},{17,1},{2,18},{18,2},{3,19},{19,3},{4,20},{20... | collective-permute-start | bytes 3145736 | tf_op jit(solution)/shard_map/ppermute | solution.py:25
  225.8 2.2 shard_map.115
  (93 shorter events, 29.5 us)
Async XLA Ops:
  3.2 5.2 %copy-start.11 = (bf16[256,64]{0,1:T(8,128)(2,1)S(1)}, bf16[256,64]{0,1:T(8,128)(2,1)}, u32[]{:S(2)}) copy-start(bf16[256,64]{0,1:T(8,128)(2,1)} %param.12) | copy-start | bytes 98308
  3.3 5.2 %copy-start.12 = (bf16[64,256]{1,0:T(8,128)(2,1)S(1)}, bf16[64,256]{1,0:T(8,128)(2,1)}, u32[]{:S(2)}) copy-start(bf16[64,256]{1,0:T(8,128)(2,1)} %param.11) | copy-start | bytes 98308
  3.3 5.2 %copy-start.13 = (bf16[64,256]{1,0:T(8,128)(2,1)S(1)}, bf16[64,256]{1,0:T(8,128)(2,1)}, u32[]{:S(2)}) copy-start(bf16[64,256]{1,0:T(8,128)(2,1)} %param.10) | copy-start | bytes 98308
  3.3 30.7 %all-to-all-start = ((bf16[4,128,2048]{2,1,0:T(8,128)(2,1)}), bf16[4,128,2048]{2,1,0:T(8,128)(2,1)S(1)}, u32[]{:S(2)}, u32[]{:S(2)}) async-start(bf16[4,128,2048]{2,1,0:T(8,128)(2,1)} %broadcast_in_dim.19), calls=%async_computation | async-start | bytes 4194304 | tf_op jit(solution)/shard_map/all_to_all | solution.py:17
  33.9 1.8 copy-start
  33.9 5.9 %copy-start.9 = (bf16[1,64,2048]{2,1,0:T(8,128)(2,1)S(1)}, bf16[1,64,2048]{2,1,0:T(8,128)(2,1)}, u32[]{:S(2)}) copy-start(bf16[1,64,2048]{2,1,0:T(8,128)(2,1)} %param.7) | copy-start | bytes 786436
  35.2 5.1 %copy-start.10 = (bf16[1,64,2048]{2,1,0:T(8,128)(2,1)S(1)}, bf16[1,64,2048]{2,1,0:T(8,128)(2,1)}, u32[]{:S(2)}) copy-start(bf16[1,64,2048]{2,1,0:T(8,128)(2,1)} %param.13) | copy-start | bytes 786436
  35.8 18.7 %all-to-all-start.1 = ((bf16[4,256,768]{2,1,0:T(8,128)(2,1)}), bf16[4,256,768]{2,1,0:T(8,128)(2,1)S(1)}, u32[]{:S(2)}, u32[]{:S(2)}) async-start(bf16[4,256,768]{2,1,0:T(8,128)(2,1)} %broadcast_in_dim.20), calls=%async_computation.1 | async-start | bytes 3145728 | tf_op jit(solution)/shard_map/all_to_all | solution.py:17
  41.0 22.8 %copy-start.14 = (s32[1,16]{1,0:T(1,128)S(1)}, s32[1,16]{1,0:T(1,128)}, u32[]{:S(2)}) copy-start(s32[1,16]{1,0:T(1,128)} %param.9) | copy-start | bytes 196
  54.5 12.4 %collective-permute-start = (bf16[1024,768]{1,0:T(8,128)(2,1)S(1)}, bf16[1024,768]{1,0:T(8,128)(2,1)S(1)}, u32[]{:S(2)}, u32[]{:S(2)}) collective-permute-start(bf16[1024,768]{1,0:T(8,128)(2,1)S(1)} %bitcast.70), channel_id=1, source_target_pairs={{0,16},{16,0},{1,17},{17,1},{2,18},{18,2},{3,19},{19,3},{4,20},{20... | collective-permute-start | bytes 4718600 | tf_op jit(solution)/shard_map/ppermute | solution.py:25
  64.6 2.2 copy-start.2
  68.1 13.0 %all-to-all-start.2 = ((bf16[4,64,512]{2,1,0:T(8,128)(2,1)}), bf16[4,64,512]{2,1,0:T(8,128)(2,1)S(1)}, u32[]{:S(2)}, u32[]{:S(2)}) async-start(bf16[4,64,512]{2,1,0:T(8,128)(2,1)} %broadcast_in_dim.21), calls=%async_computation.2 | async-start | bytes 524288 | tf_op jit(solution)/shard_map/all_to_all | solution.py:17
  73.8 2.4 %copy-start.1 = (bf16[4,128,2048]{2,1,0:T(8,128)(2,1)S(1)}, bf16[4,128,2048]{2,1,0:T(8,128)(2,1)}, u32[]{:S(2)}) copy-start(bf16[4,128,2048]{2,1,0:T(8,128)(2,1)} %copy-done) | copy-start | bytes 6291460
  83.4 17.8 %all-to-all-start.3 = ((bf16[4,64,896]{2,1,0:T(8,128)(2,1)}), bf16[4,64,896]{2,1,0:T(8,128)(2,1)S(1)}, u32[]{:S(2)}, u32[]{:S(2)}) async-start(bf16[4,64,896]{2,1,0:T(8,128)(2,1)} %shard_map.111), calls=%async_computation.3 | async-start | bytes 917504 | tf_op jit(solution)/shard_map/all_to_all | solution.py:252
  88.1 8.4 %collective-permute-start.1 = (bf16[64,1024]{1,0:T(8,128)(2,1)S(1)}, bf16[64,1024]{1,0:T(8,128)(2,1)S(1)}, u32[]{:S(2)}, u32[]{:S(2)}) collective-permute-start(bf16[64,1024]{1,0:T(8,128)(2,1)S(1)} %get-tuple-element.93), channel_id=1, source_target_pairs={{0,128},{128,256},{256,384},{384,0},{1,129},{129,257},{257,385},{3... | collective-permute-start | bytes 393224 | tf_op jit(solution)/shard_map/ppermute | solution.py:257
  90.3 8.4 %collective-permute-start.2 = (bf16[64,1024]{1,0:T(8,128)(2,1)S(1)}, bf16[64,1024]{1,0:T(8,128)(2,1)S(1)}, u32[]{:S(2)}, u32[]{:S(2)}) collective-permute-start(bf16[64,1024]{1,0:T(8,128)(2,1)S(1)} %get-tuple-element.92), channel_id=1, source_target_pairs={{0,256},{128,384},{256,0},{384,128},{1,257},{129,385},{257,1},{385... | collective-permute-start | bytes 393224 | tf_op jit(solution)/shard_map/ppermute | solution.py:257
  94.0 6.6 %collective-permute-start.3 = (bf16[64,1024]{1,0:T(8,128)(2,1)S(1)}, bf16[64,1024]{1,0:T(8,128)(2,1)S(1)}, u32[]{:S(2)}, u32[]{:S(2)}) collective-permute-start(bf16[64,1024]{1,0:T(8,128)(2,1)S(1)} %get-tuple-element.91), channel_id=1, source_target_pairs={{0,384},{128,0},{256,128},{384,256},{1,385},{129,1},{257,129},{385... | collective-permute-start | bytes 393224 | tf_op jit(solution)/shard_map/ppermute | solution.py:257
  96.5 0.7 copy-start.3
  98.7 0.7 copy-start.5
  100.5 0.7 copy-start.7
  104.6 6.8 %collective-permute-start.4 = (bf16[16,64,256]{2,1,0:T(8,128)(2,1)}, bf16[16,64,256]{2,1,0:T(8,128)(2,1)S(1)}, u32[]{:S(2)}, u32[]{:S(2)}) collective-permute-start(bf16[16,64,256]{2,1,0:T(8,128)(2,1)} %get-tuple-element.62), channel_id=1, source_target_pairs={{0,16},{16,0},{1,17},{17,1},{2,18},{18,2},{3,19},{19,3},{4,20},{20... | collective-permute-start | bytes 1572872 | tf_op jit(solution)/shard_map/ppermute | solution.py:25
  112.5 16.5 %all-to-all-start.4 = ((bf16[4,384,256]{2,1,0:T(8,128)(2,1)}), bf16[4,384,256]{2,1,0:T(8,128)(2,1)S(1)}, u32[]{:S(2)}, u32[]{:S(2)}) async-start(bf16[4,384,256]{2,1,0:T(8,128)(2,1)} %pad_maximum_fusion.1), calls=%async_computation.4 | async-start | bytes 1572864 | tf_op jit(solution)/shard_map/all_to_all | solution.py:265
  116.0 13.0 %copy-start.4 = (bf16[64,1024]{1,0:T(8,128)(2,1)S(1)}, bf16[64,1024]{1,0:T(8,128)(2,1)}, u32[]{:S(2)}) copy-start(bf16[64,1024]{1,0:T(8,128)(2,1)} %copy-done.3) | copy-start | bytes 393220
  116.1 13.0 %copy-start.6 = (bf16[64,1024]{1,0:T(8,128)(2,1)S(1)}, bf16[64,1024]{1,0:T(8,128)(2,1)}, u32[]{:S(2)}) copy-start(bf16[64,1024]{1,0:T(8,128)(2,1)} %copy-done.5) | copy-start | bytes 393220
  116.1 13.0 %copy-start.8 = (bf16[64,1024]{1,0:T(8,128)(2,1)S(1)}, bf16[64,1024]{1,0:T(8,128)(2,1)}, u32[]{:S(2)}) copy-start(bf16[64,1024]{1,0:T(8,128)(2,1)} %copy-done.7) | copy-start | bytes 393220
  118.2 10.8 %collective-permute-start.5 = (bf16[2,64,512]{2,1,0:T(8,128)(2,1)S(1)}, bf16[2,64,512]{2,1,0:T(8,128)(2,1)S(1)}, u32[]{:S(2)}, u32[]{:S(2)}) collective-permute-start(bf16[2,64,512]{2,1,0:T(8,128)(2,1)S(1)} %constant_dynamic-slice_fusion), channel_id=1, source_target_pairs={{0,2},{1,3},{2,0},{3,1},{4,6},{5,7},{6,4},{7,5},{8,10},{9,11},{10,... | collective-permute-start | bytes 393224 | tf_op jit(solution)/shard_map/ppermute | solution.py:29
  130.4 4.0 %collective-permute-start.6 = (bf16[256,512]{1,0:T(8,128)(2,1)S(1)}, bf16[256,512]{1,0:T(8,128)(2,1)S(1)}, u32[]{:S(2)}, u32[]{:S(2)}) collective-permute-start(bf16[256,512]{1,0:T(8,128)(2,1)S(1)} %get-tuple-element.71), channel_id=1, source_target_pairs={{0,16},{16,0},{1,17},{17,1},{2,18},{18,2},{3,19},{19,3},{4,20},{20... | collective-permute-start | bytes 786440 | tf_op jit(solution)/shard_map/ppermute | solution.py:25
  135.3 29.2 %all-to-all-start.5 = ((bf16[4,64,768]{2,1,0:T(8,128)(2,1)}), bf16[4,64,768]{2,1,0:T(8,128)(2,1)S(1)}, u32[]{:S(2)}, u32[]{:S(2)}) async-start(bf16[4,64,768]{2,1,0:T(8,128)(2,1)} %bitcast.26), calls=%async_computation.5 | async-start | bytes 786432 | tf_op jit(solution)/shard_map/all_to_all | solution.py:21
  147.8 16.6 %collective-permute-start.7 = (bf16[64,512]{1,0:T(8,128)(2,1)S(1)}, bf16[64,512]{1,0:T(8,128)(2,1)S(1)}, u32[]{:S(2)}, u32[]{:S(2)}) collective-permute-start(bf16[64,512]{1,0:T(8,128)(2,1)S(1)} %dynamic-slice_bitcast_fusion.4), channel_id=1, source_target_pairs={{0,1},{1,0},{2,3},{3,2},{4,5},{5,4},{6,7},{7,6},{8,9},{9,8},{10,11... | collective-permute-start | bytes 196616 | tf_op jit(solution)/shard_map/ppermute | solution.py:29
  165.4 25.9 %all-to-all-start.6 = ((bf16[4,64,896]{2,1,0:T(8,128)(2,1)}), bf16[4,64,896]{2,1,0:T(8,128)(2,1)S(1)}, u32[]{:S(2)}, u32[]{:S(2)}) async-start(bf16[4,64,896]{2,1,0:T(8,128)(2,1)} %pad_maximum_fusion.3), calls=%async_computation.6 | async-start | bytes 917504 | tf_op jit(solution)/shard_map/all_to_all | solution.py:21
  192.4 20.0 %all-to-all-start.7 = ((bf16[4,256,512]{2,1,0:T(8,128)(2,1)}), bf16[4,256,512]{2,1,0:T(8,128)(2,1)S(1)}, u32[]{:S(2)}, u32[]{:S(2)}) async-start(bf16[4,256,512]{2,1,0:T(8,128)(2,1)} %broadcast_in_dim.23), calls=%async_computation.7 | async-start | bytes 2097152 | tf_op jit(solution)/shard_map/all_to_all | solution.py:288
  212.4 13.4 %collective-permute-start.8 = (bf16[4,256,512]{2,1,0:T(8,128)(2,1)S(1)}, bf16[4,256,512]{2,1,0:T(8,128)(2,1)S(1)}, u32[]{:S(2)}, u32[]{:S(2)}) collective-permute-start(bf16[4,256,512]{2,1,0:T(8,128)(2,1)S(1)} %all-to-all-done.7.mine), channel_id=1, source_target_pairs={{0,16},{16,0},{1,17},{17,1},{2,18},{18,2},{3,19},{19,3},{4,20},{20... | collective-permute-start | bytes 3145736 | tf_op jit(solution)/shard_map/ppermute | solution.py:25

commit v5 on v4

--- a/solution.py
+++ b/solution.py
@@ -265,17 +265,18 @@
     moved_x = lax.all_to_all(messages, "x", 0, 0)
     dec_part = jnp.dot(heads[64:], wq_full.T, preferred_element_type=f32).astype(bf16)
     dec_two = halve(dec_part.reshape(64, 4, 4, 128).transpose(2, 0, 1, 3).reshape(4, 64, 512), "zl")
-    moved_x, dec_two = together(moved_x, dec_two)
+    dec_zl = halve_again(dec_two, "zl")
+    moved_x, dec_zl = together(moved_x, dec_zl)
     sources = jnp.concatenate([core] + [lax.rem(x + 4 - step, 4).reshape(1) for step in range(4)])
     keep, send, kv_sum = call(
         head_term_kernel, [(256, 512), (256, 512), (256, 256)], sources, moved_x, *rows_x
     )
     sum_x = jnp.concatenate([join(keep, swap(send)), kv_sum], 1)
-    sum_x, kv_part, dec_two = together(sum_x, kv_part, dec_two)
+    sum_x, kv_part, dec_zl = together(sum_x, kv_part, dec_zl)
 
     sum_z = exchange(sum_x.reshape(4, 64, 768), "zh")
     rest = [
-        halve_again(dec_two, "zl").reshape(64, 4, 128).transpose(1, 0, 2),
+        dec_zl.reshape(64, 4, 128).transpose(1, 0, 2),
         kv_part.reshape(4, 2, 64, 256).transpose(0, 2, 1, 3).reshape(4, 64, 512),
     ]
     sum_z, *rest = together(sum_z, *rest)

time: 230 us -> 232 us (level)
  waiting for transfers between devices: 41.6 us -> 51.5 us
  starting transfers between devices: 87.6 us -> 82.9 us
  blocking collectives: 58.4 us -> 55 us
    all_to_all x2, waiting for transfers between devices: 0.01 us -> 20.7 us  [exchange(): lax.all_to_all(parts, axis, 0, 0).astype(f32)]
    ppermute x2, waiting for transfers between devices: 19.5 us -> 5.13 us  [meet(): return lax.ppermute(block, axis, [(i, i ^ bit) for i in range(4)])]
    all_gather x1, blocking collectives: 22.4 us -> 17.4 us  [local(): mine = lax.all_gather(sum_z[:, :512], 'zh', axis=0, tiled=True)]
    all_to_all x1, waiting for transfers between devices: 0.01 us -> 3.53 us  [local(): moved_x = lax.all_to_all(messages, 'x', 0, 0)]
    all_to_all x1, starting transfers between devices: 6.39 us -> 3.52 us  [local(): mine = lax.all_to_all(copies, 'x', 0, 0)]
  transfers between devices with their start and end apart: 17 -> 17, of which waited for: 9 -> 11; matrix products, arithmetic and copies ran while one was open for 8% -> 7% of each run, Pallas kernels for 0% -> 0%
where the time goes in v5:
time: 232 us; the launch traced here: 230 us
  starting transfers between devices  82.9 us (36%)
  blocking collectives  55 us (24%)
  waiting for transfers between devices  51.5 us (22%)
  local copies, waits for them, and re-layouts  16.1 us (7%)
  Pallas kernels  9.79 us (4%)
  other arithmetic  7.28 us (3%)
  matrix products  6.08 us (3%)
    ppermute x4, starting transfers between devices, swap(): return lax.ppermute(block, 'co', [(0, 1), (1, 0)])  26 us
    all_gather x1, blocking collectives, local(): own = lax.all_gather(shard, 'zh', axis=0, tiled=True)  25.5 us
    all_to_all x2, waiting for transfers between devices, exchange(): lax.all_to_all(parts, axis, 0, 0).astype(f32)  20.7 us
    all_gather x1, blocking collectives, local(): mine = lax.all_gather(sum_z[:, :512], 'zh', axis=0, tiled=True)  17.4 us
    all_to_all x2, starting transfers between devices, exchange(): lax.all_to_all(parts, axis, 0, 0).astype(f32)  16 us
    all_to_all x3, waiting for transfers between devices, spread(): return lax.all_to_all(copies, axis, 0, 0)  14.9 us
    all_to_all x3, starting transfers between devices, spread(): return lax.all_to_all(copies, axis, 0, 0)  14.7 us
    all_gather x1, blocking collectives, local(): lax.all_gather(last[:, :256], 'zl', axis=0).astype(f32)  12.2 us
  transfers between devices with their start and end apart: 17, of which 11 were waited for; matrix products, arithmetic and copies ran while one was open for 7% of the time, Pallas kernels for 0%

profile of v5, /device:TPU:1, one launch (start us, length us, event | category | flops | bytes accessed | tf_op | source)
XLA Modules:
  0.0 229.9 jit_solution(13265432246700062141)
XLA Ops:
  0.6 2.6 %broadcast_in_dim.19 = bf16[4,128,2048]{2,1,0:T(8,128)(2,1)} broadcast(bf16[128,2048]{1,0:T(8,128)(2,1)} %bitcast.84), dimensions={1,2} | broadcast | bytes 2621440 | tf_op jit(solution)/shard_map/broadcast_in_dim | solution.py:16
  3.3 5.1 %all-to-all-start = ((bf16[4,128,2048]{2,1,0:T(8,128)(2,1)}), bf16[4,128,2048]{2,1,0:T(8,128)(2,1)S(1)}, u32[]{:S(2)}, u32[]{:S(2)}) async-start(bf16[4,128,2048]{2,1,0:T(8,128)(2,1)} %broadcast_in_dim.19), calls=%async_computation | async-start | bytes 4194304 | tf_op jit(solution)/shard_map/all_to_all | solution.py:17
  8.4 25.5 %all_gather.12 = bf16[256,768]{1,0:T(8,128)(2,1)S(1)} all-gather(bf16[64,768]{1,0:T(8,128)(2,1)S(1)} %pad_maximum_fusion.5), channel_id=1, replica_groups=mesh['x'=4,'zh'=4,'co'=2,'y'=4,'zl'=4] {'zh'}, dimensions={0}, use_global_device_ids=true | all-gather | bytes 491520 | tf_op jit(solution)/shard_map/all_gather | solution.py:226
  35.8 4.0 %all-to-all-start.1 = ((bf16[4,256,768]{2,1,0:T(8,128)(2,1)}), bf16[4,256,768]{2,1,0:T(8,128)(2,1)S(1)}, u32[]{:S(2)}, u32[]{:S(2)}) async-start(bf16[4,256,768]{2,1,0:T(8,128)(2,1)} %broadcast_in_dim.20), calls=%async_computation.1 | async-start | bytes 3145728 | tf_op jit(solution)/shard_map/all_to_all | solution.py:17
  42.6 11.9 %all-to-all-done.1 = bf16[4,256,768]{2,1,0:T(8,128)(2,1)S(1)} async-done(((bf16[4,256,768]{2,1,0:T(8,128)(2,1)}), bf16[4,256,768]{2,1,0:T(8,128)(2,1)S(1)}, u32[]{:S(2)}, u32[]{:S(2)}) %all-to-all-start.1) | async-done | bytes 1572896 | tf_op jit(solution)/shard_map/all_to_all | solution.py:17
  54.5 8.8 %collective-permute-start = (bf16[1024,768]{1,0:T(8,128)(2,1)S(1)}, bf16[1024,768]{1,0:T(8,128)(2,1)S(1)}, u32[]{:S(2)}, u32[]{:S(2)}) collective-permute-start(bf16[1024,768]{1,0:T(8,128)(2,1)S(1)} %bitcast.69), channel_id=1, source_target_pairs={{0,16},{16,0},{1,17},{17,1},{2,18},{18,2},{3,19},{19,3},{4,20},{20... | collective-permute-start | bytes 4718600 | tf_op jit(solution)/shard_map/ppermute | solution.py:25
  68.1 5.5 %all-to-all-start.2 = ((bf16[4,64,512]{2,1,0:T(8,128)(2,1)}), bf16[4,64,512]{2,1,0:T(8,128)(2,1)S(1)}, u32[]{:S(2)}, u32[]{:S(2)}) async-start(bf16[4,64,512]{2,1,0:T(8,128)(2,1)} %broadcast_in_dim.21), calls=%async_computation.2 | async-start | bytes 524288 | tf_op jit(solution)/shard_map/all_to_all | solution.py:17
  73.8 1.9 pad_maximum_fusion
  76.2 1.9 convolution_convert_fusion.2.kv
  78.1 3.0 %all-to-all-done.2.qa = bf16[4,64,512]{2,1,0:T(8,128)(2,1)S(1)} async-done(((bf16[4,64,512]{2,1,0:T(8,128)(2,1)}), bf16[4,64,512]{2,1,0:T(8,128)(2,1)S(1)}, u32[]{:S(2)}, u32[]{:S(2)}) %all-to-all-start.2) | async-done | bytes 262176 | tf_op jit(solution)/shard_map/all_to_all | solution.py:17
  81.1 2.3 %shard_map.111 = bf16[4,64,896]{2,1,0:T(8,128)(2,1)} custom-call(s32[4]{0:T(128)S(1)} %fusion.8.lengths, bf16[4,64,512]{2,1,0:T(8,128)(2,1)S(1)} %all-to-all-done.2.qa, bf16[512,256]{1,0:T(8,128)(2,1)S(1)} %convolution_convert_fusion.2.kv), custom_call_target="tpu_custom_call" | custom-call | tf_op jit(solution)/shard_map/pallas_call | solution.py:187
  83.4 3.5 %all-to-all-start.3 = ((bf16[4,64,896]{2,1,0:T(8,128)(2,1)}), bf16[4,64,896]{2,1,0:T(8,128)(2,1)S(1)}, u32[]{:S(2)}, u32[]{:S(2)}) async-start(bf16[4,64,896]{2,1,0:T(8,128)(2,1)} %shard_map.111), calls=%async_computation.3 | async-start | bytes 917504 | tf_op jit(solution)/shard_map/all_to_all | solution.py:252
  88.1 2.2 collective-permute-start.1
  90.3 3.7 %collective-permute-start.2 = (bf16[64,1024]{1,0:T(8,128)(2,1)S(1)}, bf16[64,1024]{1,0:T(8,128)(2,1)S(1)}, u32[]{:S(2)}, u32[]{:S(2)}) collective-permute-start(bf16[64,1024]{1,0:T(8,128)(2,1)S(1)} %get-tuple-element.92), channel_id=1, source_target_pairs={{0,256},{128,384},{256,0},{384,128},{1,257},{129,385},{257,1},{385... | collective-permute-start | bytes 393224 | tf_op jit(solution)/shard_map/ppermute | solution.py:257
  94.0 2.5 %collective-permute-start.3 = (bf16[64,1024]{1,0:T(8,128)(2,1)S(1)}, bf16[64,1024]{1,0:T(8,128)(2,1)S(1)}, u32[]{:S(2)}, u32[]{:S(2)}) collective-permute-start(bf16[64,1024]{1,0:T(8,128)(2,1)S(1)} %get-tuple-element.91), channel_id=1, source_target_pairs={{0,384},{128,0},{256,128},{384,256},{1,385},{129,1},{257,129},{385... | collective-permute-start | bytes 393224 | tf_op jit(solution)/shard_map/ppermute | solution.py:257
  104.6 5.1 %collective-permute-start.4 = (bf16[16,64,256]{2,1,0:T(8,128)(2,1)}, bf16[16,64,256]{2,1,0:T(8,128)(2,1)S(1)}, u32[]{:S(2)}, u32[]{:S(2)}) collective-permute-start(bf16[16,64,256]{2,1,0:T(8,128)(2,1)} %get-tuple-element.62), channel_id=1, source_target_pairs={{0,16},{16,0},{1,17},{17,1},{2,18},{18,2},{3,19},{19,3},{4,20},{20... | collective-permute-start | bytes 1572872 | tf_op jit(solution)/shard_map/ppermute | solution.py:25
  114.6 4.5 %collective-permute-start.5 = (bf16[2,64,512]{2,1,0:T(8,128)(2,1)S(1)}, bf16[2,64,512]{2,1,0:T(8,128)(2,1)S(1)}, u32[]{:S(2)}, u32[]{:S(2)}) collective-permute-start(bf16[2,64,512]{2,1,0:T(8,128)(2,1)S(1)} %constant_dynamic-slice_fusion), channel_id=1, source_target_pairs={{0,2},{1,3},{2,0},{3,1},{4,6},{5,7},{6,4},{7,5},{8,10},{9,11},{10,... | collective-permute-start | bytes 393224 | tf_op jit(solution)/shard_map/ppermute | solution.py:29
  119.1 3.5 %all-to-all-start.4 = ((bf16[4,384,256]{2,1,0:T(8,128)(2,1)}), bf16[4,384,256]{2,1,0:T(8,128)(2,1)S(1)}, u32[]{:S(2)}, u32[]{:S(2)}) async-start(bf16[4,384,256]{2,1,0:T(8,128)(2,1)} %pad_maximum_fusion.1), calls=%async_computation.4 | async-start | bytes 1572864 | tf_op jit(solution)/shard_map/all_to_all | solution.py:265
  122.7 2.8 %collective-permute-done.5 = bf16[2,64,512]{2,1,0:T(8,128)(2,1)S(1)} collective-permute-done((bf16[2,64,512]{2,1,0:T(8,128)(2,1)S(1)}, bf16[2,64,512]{2,1,0:T(8,128)(2,1)S(1)}, u32[]{:S(2)}, u32[]{:S(2)}) %collective-permute-start.5) | collective-permute-done | bytes 131104 | tf_op jit(solution)/shard_map/ppermute | solution.py:29
  125.5 2.8 %collective-permute-start.6 = (bf16[64,512]{1,0:T(8,128)(2,1)S(1)}, bf16[64,512]{1,0:T(8,128)(2,1)S(1)}, u32[]{:S(2)}, u32[]{:S(2)}) collective-permute-start(bf16[64,512]{1,0:T(8,128)(2,1)S(1)} %dynamic-slice_bitcast_fusion.4), channel_id=1, source_target_pairs={{0,1},{1,0},{2,3},{3,2},{4,5},{5,4},{6,7},{7,6},{8,9},{9,8},{10,11... | collective-permute-start | bytes 196616 | tf_op jit(solution)/shard_map/ppermute | solution.py:29
  128.4 2.4 %collective-permute-done.6 = bf16[64,512]{1,0:T(8,128)(2,1)S(1)} collective-permute-done((bf16[64,512]{1,0:T(8,128)(2,1)S(1)}, bf16[64,512]{1,0:T(8,128)(2,1)S(1)}, u32[]{:S(2)}, u32[]{:S(2)}) %collective-permute-start.6) | collective-permute-done | bytes 65568 | tf_op jit(solution)/shard_map/ppermute | solution.py:29
  130.8 3.5 %all-to-all-done.4.moved = bf16[4,384,256]{2,1,0:T(8,128)(2,1)S(1)} async-done(((bf16[4,384,256]{2,1,0:T(8,128)(2,1)}), bf16[4,384,256]{2,1,0:T(8,128)(2,1)S(1)}, u32[]{:S(2)}, u32[]{:S(2)}) %all-to-all-start.4) | async-done | bytes 786464 | tf_op jit(solution)/shard_map/all_to_all | solution.py:265
  135.7 3.4 %collective-permute-start.7 = (bf16[256,512]{1,0:T(8,128)(2,1)S(1)}, bf16[256,512]{1,0:T(8,128)(2,1)S(1)}, u32[]{:S(2)}, u32[]{:S(2)}) collective-permute-start(bf16[256,512]{1,0:T(8,128)(2,1)S(1)} %get-tuple-element.71), channel_id=1, source_target_pairs={{0,16},{16,0},{1,17},{17,1},{2,18},{18,2},{3,19},{19,3},{4,20},{20... | collective-permute-start | bytes 786440 | tf_op jit(solution)/shard_map/ppermute | solution.py:25
  141.1 12.6 %all-to-all-start.5 = ((bf16[4,64,768]{2,1,0:T(8,128)(2,1)}), bf16[4,64,768]{2,1,0:T(8,128)(2,1)S(1)}, u32[]{:S(2)}, u32[]{:S(2)}) async-start(bf16[4,64,768]{2,1,0:T(8,128)(2,1)} %bitcast.28), calls=%async_computation.5 | async-start | bytes 786432 | tf_op jit(solution)/shard_map/all_to_all | solution.py:21
  154.2 20.7 %all-to-all-done.5 = bf16[4,64,768]{2,1,0:T(8,128)(2,1)S(1)} async-done(((bf16[4,64,768]{2,1,0:T(8,128)(2,1)}), bf16[4,64,768]{2,1,0:T(8,128)(2,1)S(1)}, u32[]{:S(2)}, u32[]{:S(2)}) %all-to-all-start.5) | async-done | bytes 393248 | tf_op jit(solution)/shard_map/all_to_all | solution.py:21
  175.8 3.5 %all-to-all-start.6 = ((bf16[4,64,896]{2,1,0:T(8,128)(2,1)}), bf16[4,64,896]{2,1,0:T(8,128)(2,1)S(1)}, u32[]{:S(2)}, u32[]{:S(2)}) async-start(bf16[4,64,896]{2,1,0:T(8,128)(2,1)} %pad_maximum_fusion.3), calls=%async_computation.6 | async-start | bytes 917504 | tf_op jit(solution)/shard_map/all_to_all | solution.py:21
  179.3 17.4 %all_gather.13 = bf16[256,512]{1,0:T(8,128)(2,1)S(1)} all-gather(bf16[64,512]{1,0:T(8,128)(2,1)S(1)} %slice.70), channel_id=1, replica_groups=mesh['x'=4,'zh'=4,'co'=2,'y'=4,'zl'=4] {'zh'}, dimensions={0}, use_global_device_ids=true | all-gather | bytes 327680 | tf_op jit(solution)/shard_map/all_gather | solution.py:286
  197.8 3.5 %all-to-all-start.7 = ((bf16[4,256,512]{2,1,0:T(8,128)(2,1)}), bf16[4,256,512]{2,1,0:T(8,128)(2,1)S(1)}, u32[]{:S(2)}, u32[]{:S(2)}) async-start(bf16[4,256,512]{2,1,0:T(8,128)(2,1)} %broadcast_in_dim.23), calls=%async_computation.7 | async-start | bytes 2097152 | tf_op jit(solution)/shard_map/all_to_all | solution.py:289
  201.3 12.2 %all-gather = bf16[256,256]{1,0:T(8,128)(2,1)S(1)} all-gather(bf16[64,256]{1,0:T(8,128)(2,1)S(1)} %get-tuple-element.105), channel_id=2, replica_groups=mesh['x'=4,'zh'=4,'co'=2,'y'=4,'zl'=4] {'zl'}, dimensions={0}, use_global_device_ids=true | all-gather | bytes 163840 | tf_op jit(solution)/shard_map/all_gather | solution.py:293
  214.2 2.5 %convolution_convert_fusion = bf16[128,2048]{1,0:T(8,128)(2,1)} fusion(bf16[2048,768]{1,0:T(8,128)(2,1)} %bitcast.15, bf16[64,256]{1,0:T(8,128)(2,1)S(1)} %get-tuple-element.104, bf16[64,256]{1,0:T(8,128)(2,1)S(1)} %get-tuple-element.103), kind=kOutput, calls=%fused_computation.1 | convolution fusion | flops 134610944 | bytes 1638400 | tf_op jit(solution)/shard_map/dot_general | solution.py:292
  216.7 8.7 %collective-permute-start.8 = (bf16[4,256,512]{2,1,0:T(8,128)(2,1)S(1)}, bf16[4,256,512]{2,1,0:T(8,128)(2,1)S(1)}, u32[]{:S(2)}, u32[]{:S(2)}) collective-permute-start(bf16[4,256,512]{2,1,0:T(8,128)(2,1)S(1)} %all-to-all-done.7.mine), channel_id=1, source_target_pairs={{0,16},{16,0},{1,17},{17,1},{2,18},{18,2},{3,19},{19,3},{4,20},{20... | collective-permute-start | bytes 3145736 | tf_op jit(solution)/shard_map/ppermute | solution.py:25
  227.6 2.2 shard_map.115
  (94 shorter events, 33.0 us)
Async XLA Ops:
  3.2 5.2 %copy-start.11 = (bf16[256,64]{0,1:T(8,128)(2,1)S(1)}, bf16[256,64]{0,1:T(8,128)(2,1)}, u32[]{:S(2)}) copy-start(bf16[256,64]{0,1:T(8,128)(2,1)} %param.12) | copy-start | bytes 98308
  3.3 5.2 %copy-start.12 = (bf16[64,256]{1,0:T(8,128)(2,1)S(1)}, bf16[64,256]{1,0:T(8,128)(2,1)}, u32[]{:S(2)}) copy-start(bf16[64,256]{1,0:T(8,128)(2,1)} %param.11) | copy-start | bytes 98308
  3.3 5.2 %copy-start.13 = (bf16[64,256]{1,0:T(8,128)(2,1)S(1)}, bf16[64,256]{1,0:T(8,128)(2,1)}, u32[]{:S(2)}) copy-start(bf16[64,256]{1,0:T(8,128)(2,1)} %param.10) | copy-start | bytes 98308
  3.3 30.7 %all-to-all-start = ((bf16[4,128,2048]{2,1,0:T(8,128)(2,1)}), bf16[4,128,2048]{2,1,0:T(8,128)(2,1)S(1)}, u32[]{:S(2)}, u32[]{:S(2)}) async-start(bf16[4,128,2048]{2,1,0:T(8,128)(2,1)} %broadcast_in_dim.19), calls=%async_computation | async-start | bytes 4194304 | tf_op jit(solution)/shard_map/all_to_all | solution.py:17
  33.9 1.8 copy-start
  33.9 5.9 %copy-start.9 = (bf16[1,64,2048]{2,1,0:T(8,128)(2,1)S(1)}, bf16[1,64,2048]{2,1,0:T(8,128)(2,1)}, u32[]{:S(2)}) copy-start(bf16[1,64,2048]{2,1,0:T(8,128)(2,1)} %param.7) | copy-start | bytes 786436
  35.2 5.1 %copy-start.10 = (bf16[1,64,2048]{2,1,0:T(8,128)(2,1)S(1)}, bf16[1,64,2048]{2,1,0:T(8,128)(2,1)}, u32[]{:S(2)}) copy-start(bf16[1,64,2048]{2,1,0:T(8,128)(2,1)} %param.13) | copy-start | bytes 786436
  35.8 18.7 %all-to-all-start.1 = ((bf16[4,256,768]{2,1,0:T(8,128)(2,1)}), bf16[4,256,768]{2,1,0:T(8,128)(2,1)S(1)}, u32[]{:S(2)}, u32[]{:S(2)}) async-start(bf16[4,256,768]{2,1,0:T(8,128)(2,1)} %broadcast_in_dim.20), calls=%async_computation.1 | async-start | bytes 3145728 | tf_op jit(solution)/shard_map/all_to_all | solution.py:17
  41.0 22.8 %copy-start.14 = (s32[1,16]{1,0:T(1,128)S(1)}, s32[1,16]{1,0:T(1,128)}, u32[]{:S(2)}) copy-start(s32[1,16]{1,0:T(1,128)} %param.9) | copy-start | bytes 196
  54.5 12.4 %collective-permute-start = (bf16[1024,768]{1,0:T(8,128)(2,1)S(1)}, bf16[1024,768]{1,0:T(8,128)(2,1)S(1)}, u32[]{:S(2)}, u32[]{:S(2)}) collective-permute-start(bf16[1024,768]{1,0:T(8,128)(2,1)S(1)} %bitcast.69), channel_id=1, source_target_pairs={{0,16},{16,0},{1,17},{17,1},{2,18},{18,2},{3,19},{19,3},{4,20},{20... | collective-permute-start | bytes 4718600 | tf_op jit(solution)/shard_map/ppermute | solution.py:25
  64.6 2.2 copy-start.2
  68.1 13.0 %all-to-all-start.2 = ((bf16[4,64,512]{2,1,0:T(8,128)(2,1)}), bf16[4,64,512]{2,1,0:T(8,128)(2,1)S(1)}, u32[]{:S(2)}, u32[]{:S(2)}) async-start(bf16[4,64,512]{2,1,0:T(8,128)(2,1)} %broadcast_in_dim.21), calls=%async_computation.2 | async-start | bytes 524288 | tf_op jit(solution)/shard_map/all_to_all | solution.py:17
  73.8 2.4 %copy-start.1 = (bf16[4,128,2048]{2,1,0:T(8,128)(2,1)S(1)}, bf16[4,128,2048]{2,1,0:T(8,128)(2,1)}, u32[]{:S(2)}) copy-start(bf16[4,128,2048]{2,1,0:T(8,128)(2,1)} %copy-done) | copy-start | bytes 6291460
  83.4 17.8 %all-to-all-start.3 = ((bf16[4,64,896]{2,1,0:T(8,128)(2,1)}), bf16[4,64,896]{2,1,0:T(8,128)(2,1)S(1)}, u32[]{:S(2)}, u32[]{:S(2)}) async-start(bf16[4,64,896]{2,1,0:T(8,128)(2,1)} %shard_map.111), calls=%async_computation.3 | async-start | bytes 917504 | tf_op jit(solution)/shard_map/all_to_all | solution.py:252
  88.1 8.4 %collective-permute-start.1 = (bf16[64,1024]{1,0:T(8,128)(2,1)S(1)}, bf16[64,1024]{1,0:T(8,128)(2,1)S(1)}, u32[]{:S(2)}, u32[]{:S(2)}) collective-permute-start(bf16[64,1024]{1,0:T(8,128)(2,1)S(1)} %get-tuple-element.93), channel_id=1, source_target_pairs={{0,128},{128,256},{256,384},{384,0},{1,129},{129,257},{257,385},{3... | collective-permute-start | bytes 393224 | tf_op jit(solution)/shard_map/ppermute | solution.py:257
  90.3 8.4 %collective-permute-start.2 = (bf16[64,1024]{1,0:T(8,128)(2,1)S(1)}, bf16[64,1024]{1,0:T(8,128)(2,1)S(1)}, u32[]{:S(2)}, u32[]{:S(2)}) collective-permute-start(bf16[64,1024]{1,0:T(8,128)(2,1)S(1)} %get-tuple-element.92), channel_id=1, source_target_pairs={{0,256},{128,384},{256,0},{384,128},{1,257},{129,385},{257,1},{385... | collective-permute-start | bytes 393224 | tf_op jit(solution)/shard_map/ppermute | solution.py:257
  94.0 6.6 %collective-permute-start.3 = (bf16[64,1024]{1,0:T(8,128)(2,1)S(1)}, bf16[64,1024]{1,0:T(8,128)(2,1)S(1)}, u32[]{:S(2)}, u32[]{:S(2)}) collective-permute-start(bf16[64,1024]{1,0:T(8,128)(2,1)S(1)} %get-tuple-element.91), channel_id=1, source_target_pairs={{0,384},{128,0},{256,128},{384,256},{1,385},{129,1},{257,129},{385... | collective-permute-start | bytes 393224 | tf_op jit(solution)/shard_map/ppermute | solution.py:257
  96.5 0.7 copy-start.3
  98.7 0.7 copy-start.5
  100.5 0.7 copy-start.7
  104.6 6.8 %collective-permute-start.4 = (bf16[16,64,256]{2,1,0:T(8,128)(2,1)}, bf16[16,64,256]{2,1,0:T(8,128)(2,1)S(1)}, u32[]{:S(2)}, u32[]{:S(2)}) collective-permute-start(bf16[16,64,256]{2,1,0:T(8,128)(2,1)} %get-tuple-element.62), channel_id=1, source_target_pairs={{0,16},{16,0},{1,17},{17,1},{2,18},{18,2},{3,19},{19,3},{4,20},{20... | collective-permute-start | bytes 1572872 | tf_op jit(solution)/shard_map/ppermute | solution.py:25
  114.2 20.1 %copy-start.4 = (bf16[64,1024]{1,0:T(8,128)(2,1)S(1)}, bf16[64,1024]{1,0:T(8,128)(2,1)}, u32[]{:S(2)}) copy-start(bf16[64,1024]{1,0:T(8,128)(2,1)} %copy-done.3) | copy-start | bytes 393220
  114.2 20.1 %copy-start.6 = (bf16[64,1024]{1,0:T(8,128)(2,1)S(1)}, bf16[64,1024]{1,0:T(8,128)(2,1)}, u32[]{:S(2)}) copy-start(bf16[64,1024]{1,0:T(8,128)(2,1)} %copy-done.5) | copy-start | bytes 393220
  114.2 20.1 %copy-start.8 = (bf16[64,1024]{1,0:T(8,128)(2,1)S(1)}, bf16[64,1024]{1,0:T(8,128)(2,1)}, u32[]{:S(2)}) copy-start(bf16[64,1024]{1,0:T(8,128)(2,1)} %copy-done.7) | copy-start | bytes 393220
  114.6 10.8 %collective-permute-start.5 = (bf16[2,64,512]{2,1,0:T(8,128)(2,1)S(1)}, bf16[2,64,512]{2,1,0:T(8,128)(2,1)S(1)}, u32[]{:S(2)}, u32[]{:S(2)}) collective-permute-start(bf16[2,64,512]{2,1,0:T(8,128)(2,1)S(1)} %constant_dynamic-slice_fusion), channel_id=1, source_target_pairs={{0,2},{1,3},{2,0},{3,1},{4,6},{5,7},{6,4},{7,5},{8,10},{9,11},{10,... | collective-permute-start | bytes 393224 | tf_op jit(solution)/shard_map/ppermute | solution.py:29
  119.1 15.2 %all-to-all-start.4 = ((bf16[4,384,256]{2,1,0:T(8,128)(2,1)}), bf16[4,384,256]{2,1,0:T(8,128)(2,1)S(1)}, u32[]{:S(2)}, u32[]{:S(2)}) async-start(bf16[4,384,256]{2,1,0:T(8,128)(2,1)} %pad_maximum_fusion.1), calls=%async_computation.4 | async-start | bytes 1572864 | tf_op jit(solution)/shard_map/all_to_all | solution.py:265
  125.5 5.3 %collective-permute-start.6 = (bf16[64,512]{1,0:T(8,128)(2,1)S(1)}, bf16[64,512]{1,0:T(8,128)(2,1)S(1)}, u32[]{:S(2)}, u32[]{:S(2)}) collective-permute-start(bf16[64,512]{1,0:T(8,128)(2,1)S(1)} %dynamic-slice_bitcast_fusion.4), channel_id=1, source_target_pairs={{0,1},{1,0},{2,3},{3,2},{4,5},{5,4},{6,7},{7,6},{8,9},{9,8},{10,11... | collective-permute-start | bytes 196616 | tf_op jit(solution)/shard_map/ppermute | solution.py:29
  135.7 4.6 %collective-permute-start.7 = (bf16[256,512]{1,0:T(8,128)(2,1)S(1)}, bf16[256,512]{1,0:T(8,128)(2,1)S(1)}, u32[]{:S(2)}, u32[]{:S(2)}) collective-permute-start(bf16[256,512]{1,0:T(8,128)(2,1)S(1)} %get-tuple-element.71), channel_id=1, source_target_pairs={{0,16},{16,0},{1,17},{17,1},{2,18},{18,2},{3,19},{19,3},{4,20},{20... | collective-permute-start | bytes 786440 | tf_op jit(solution)/shard_map/ppermute | solution.py:25
  141.1 33.8 %all-to-all-start.5 = ((bf16[4,64,768]{2,1,0:T(8,128)(2,1)}), bf16[4,64,768]{2,1,0:T(8,128)(2,1)S(1)}, u32[]{:S(2)}, u32[]{:S(2)}) async-start(bf16[4,64,768]{2,1,0:T(8,128)(2,1)} %bitcast.28), calls=%async_computation.5 | async-start | bytes 786432 | tf_op jit(solution)/shard_map/all_to_all | solution.py:21
  175.8 20.9 %all-to-all-start.6 = ((bf16[4,64,896]{2,1,0:T(8,128)(2,1)}), bf16[4,64,896]{2,1,0:T(8,128)(2,1)S(1)}, u32[]{:S(2)}, u32[]{:S(2)}) async-start(bf16[4,64,896]{2,1,0:T(8,128)(2,1)} %pad_maximum_fusion.3), calls=%async_computation.6 | async-start | bytes 917504 | tf_op jit(solution)/shard_map/all_to_all | solution.py:21
  197.8 18.9 %all-to-all-start.7 = ((bf16[4,256,512]{2,1,0:T(8,128)(2,1)}), bf16[4,256,512]{2,1,0:T(8,128)(2,1)S(1)}, u32[]{:S(2)}, u32[]{:S(2)}) async-start(bf16[4,256,512]{2,1,0:T(8,128)(2,1)} %broadcast_in_dim.23), calls=%async_computation.7 | async-start | bytes 2097152 | tf_op jit(solution)/shard_map/all_to_all | solution.py:289
  216.7 11.0 %collective-permute-start.8 = (bf16[4,256,512]{2,1,0:T(8,128)(2,1)S(1)}, bf16[4,256,512]{2,1,0:T(8,128)(2,1)S(1)}, u32[]{:S(2)}, u32[]{:S(2)}) collective-permute-start(bf16[4,256,512]{2,1,0:T(8,128)(2,1)S(1)} %all-to-all-done.7.mine), channel_id=1, source_target_pairs={{0,16},{16,0},{1,17},{17,1},{2,18},{18,2},{3,19},{19,3},{4,20},{20... | collective-permute-start | bytes 3145736 | tf_op jit(solution)/shard_map/ppermute | solution.py:25

commit v6 on v4

--- a/solution.py
+++ b/solution.py
@@ -31,20 +31,6 @@
 
 def join(keep, moved):
     return (keep.astype(f32) + moved.astype(f32)).astype(bf16)
-
-
-def halve(parts, axis):
-    high = lax.axis_index(axis) // 2
-    keep = lax.dynamic_slice_in_dim(parts, 2 * high, 2, 0)
-    send = lax.dynamic_slice_in_dim(parts, 2 - 2 * high, 2, 0)
-    return join(keep, meet(send, axis, 2))
-
-
-def halve_again(two, axis):
-    low = lax.rem(lax.axis_index(axis), 2)
-    keep = lax.dynamic_index_in_dim(two, low, 0, keepdims=False)
-    send = lax.dynamic_index_in_dim(two, 1 - low, 0, keepdims=False)
-    return join(keep, meet(send, axis, 1))
 
 
 def together(*arrays):
@@ -261,21 +247,18 @@
     keep, send = call(key_term_kernel, [(16, 64, 256)] * 2, core, kv_part, enc_four)
     kv_chip = join(keep, swap(send)).reshape(4, 256, 256)
     messages = jnp.concatenate([jnp.broadcast_to(heads[None], (4, 128, 256)), kv_chip], 1)
-    messages, heads = together(messages, heads)
     moved_x = lax.all_to_all(messages, "x", 0, 0)
-    dec_part = jnp.dot(heads[64:], wq_full.T, preferred_element_type=f32).astype(bf16)
-    dec_two = halve(dec_part.reshape(64, 4, 4, 128).transpose(2, 0, 1, 3).reshape(4, 64, 512), "zl")
-    moved_x, dec_two = together(moved_x, dec_two)
     sources = jnp.concatenate([core] + [lax.rem(x + 4 - step, 4).reshape(1) for step in range(4)])
     keep, send, kv_sum = call(
         head_term_kernel, [(256, 512), (256, 512), (256, 256)], sources, moved_x, *rows_x
     )
     sum_x = jnp.concatenate([join(keep, swap(send)), kv_sum], 1)
-    sum_x, kv_part, dec_two = together(sum_x, kv_part, dec_two)
+    sum_x, kv_part, heads = together(sum_x, kv_part, heads)
 
     sum_z = exchange(sum_x.reshape(4, 64, 768), "zh")
+    dec_part = jnp.dot(heads[64:], wq_full.T, preferred_element_type=f32).astype(bf16)
     rest = [
-        halve_again(dec_two, "zl").reshape(64, 4, 128).transpose(1, 0, 2),
+        dec_part.reshape(64, 4, 512).transpose(1, 0, 2),
         kv_part.reshape(4, 2, 64, 256).transpose(0, 2, 1, 3).reshape(4, 64, 512),
     ]
     sum_z, *rest = together(sum_z, *rest)
@@ -286,11 +269,14 @@
     copies = jnp.broadcast_to(mine[None], (4, 256, 512))
     copies, last = together(copies, last)
     mine = lax.all_to_all(copies, "x", 0, 0)
-    dec_grad = last[:, 256:384]
-    kv_grad = jnp.concatenate([last[:, 384:640], last[:, 640:]], 0)
+    kv_grad = jnp.concatenate([last[:, 768:1024], last[:, 1024:]], 0)
     enc_grad = jnp.dot(kv_grad, wkv_full.T, preferred_element_type=f32).astype(bf16)
-    kv_weight_grad = jnp.sum(lax.all_gather(last[:, :256], "zl", axis=0).astype(f32), 0)
-    mine, kv_weight_grad, enc_grad = together(mine, kv_weight_grad, enc_grad)
+    rows_zl = lax.all_gather(last[:, :768], "zl", axis=0)
+    kv_weight_grad = jnp.sum(rows_zl[:, :, :256].astype(f32), 0)
+    dec_zl = rows_zl[:, :, 256:].reshape(4, 64, 4, 128)
+    dec_zl = lax.dynamic_index_in_dim(dec_zl, zl, 2, keepdims=False)
+    dec_grad = jnp.sum(dec_zl.astype(f32), 0).astype(bf16)
+    mine, rows_zl = together(mine, rows_zl)
     q_weight_grad, o_weight_grad = place(core, mine, swap(mine))
     return (dec_grad[None], enc_grad[None], q_weight_grad, kv_weight_grad, o_weight_grad)
 

time: 230 us -> 223 us (0.970)
  starting transfers between devices: 87.6 us -> 74.1 us
  waiting for transfers between devices: 41.6 us -> 46.8 us
  blocking collectives: 58.4 us -> 62.7 us
    ppermute x2 -> x0, waiting for transfers between devices: 19.5 us -> none  [meet(): return lax.ppermute(block, axis, [(i, i ^ bit) for i in range(4)])]
    all_to_all x2, waiting for transfers between devices: 0.01 us -> 13.4 us  [exchange(): lax.all_to_all(parts, axis, 0, 0).astype(f32)]
    all_to_all x1, waiting for transfers between devices: 0.01 us -> 11.9 us  [local(): moved_x = lax.all_to_all(messages, 'x', 0, 0)]
    all_gather x1, blocking collectives: 10.5 us -> 20.6 us  [local(): rows_zl = lax.all_gather(last[:, :768], 'zl', axis=0)]
    ppermute x2 -> x0, starting transfers between devices: 7.29 us -> none  [meet(): return lax.ppermute(block, axis, [(i, i ^ bit) for i in range(4)])]
    all_gather x1, blocking collectives: 22.4 us -> 16.7 us  [local(): mine = lax.all_gather(sum_z[:, :512], 'zh', axis=0, tiled=True)]
    ppermute x4, starting transfers between devices: 27.8 us -> 24.5 us  [swap(): return lax.ppermute(block, 'co', [(0, 1), (1, 0)])]
    all_to_all x1, starting transfers between devices: 6.39 us -> 3.52 us  [local(): mine = lax.all_to_all(copies, 'x', 0, 0)]
  transfers between devices with their start and end apart: 17 -> 15, of which waited for: 9 -> 8; matrix products, arithmetic and copies ran while one was open for 8% -> 7% of each run, Pallas kernels for 0% -> 0%
where the time goes in v6:
time: 223 us; the launch traced here: 222 us
  starting transfers between devices  74.1 us (33%)
  blocking collectives  62.7 us (28%)
  waiting for transfers between devices  46.8 us (21%)
  local copies, waits for them, and re-layouts  16.8 us (8%)
  Pallas kernels  9.06 us (4%)
  other arithmetic  6.54 us (3%)
  matrix products  4.87 us (2%)
    all_gather x1, blocking collectives, local(): own = lax.all_gather(shard, 'zh', axis=0, tiled=True)  25.5 us
    ppermute x4, starting transfers between devices, swap(): return lax.ppermute(block, 'co', [(0, 1), (1, 0)])  24.5 us
    all_gather x1, blocking collectives, local(): rows_zl = lax.all_gather(last[:, :768], 'zl', axis=0)  20.6 us
    all_gather x1, blocking collectives, local(): mine = lax.all_gather(sum_z[:, :512], 'zh', axis=0, tiled=True)  16.7 us
    all_to_all x3, waiting for transfers between devices, spread(): return lax.all_to_all(copies, axis, 0, 0)  16.1 us
    all_to_all x2, starting transfers between devices, exchange(): lax.all_to_all(parts, axis, 0, 0).astype(f32)  16.1 us
    all_to_all x3, starting transfers between devices, spread(): return lax.all_to_all(copies, axis, 0, 0)  14.7 us
    all_to_all x2, waiting for transfers between devices, exchange(): lax.all_to_all(parts, axis, 0, 0).astype(f32)  13.4 us
  transfers between devices with their start and end apart: 15, of which 8 were waited for; matrix products, arithmetic and copies ran while one was open for 7% of the time, Pallas kernels for 0%

profile of v6, /device:TPU:1, one launch (start us, length us, event | category | flops | bytes accessed | tf_op | source)
XLA Modules:
  0.0 222.0 jit_solution(11832747675413020944)
XLA Ops:
  0.6 2.6 %broadcast_in_dim.19 = bf16[4,128,2048]{2,1,0:T(8,128)(2,1)} broadcast(bf16[128,2048]{1,0:T(8,128)(2,1)} %bitcast.81), dimensions={1,2} | broadcast | bytes 2621440 | tf_op jit(solution)/shard_map/broadcast_in_dim | solution.py:16
  3.3 5.1 %all-to-all-start = ((bf16[4,128,2048]{2,1,0:T(8,128)(2,1)}), bf16[4,128,2048]{2,1,0:T(8,128)(2,1)S(1)}, u32[]{:S(2)}, u32[]{:S(2)}) async-start(bf16[4,128,2048]{2,1,0:T(8,128)(2,1)} %broadcast_in_dim.19), calls=%async_computation | async-start | bytes 4194304 | tf_op jit(solution)/shard_map/all_to_all | solution.py:17
  8.4 25.5 %all_gather.12 = bf16[256,768]{1,0:T(8,128)(2,1)S(1)} all-gather(bf16[64,768]{1,0:T(8,128)(2,1)S(1)} %pad_maximum_fusion.5), channel_id=1, replica_groups=mesh['x'=4,'zh'=4,'co'=2,'y'=4,'zl'=4] {'zh'}, dimensions={0}, use_global_device_ids=true | all-gather | bytes 491520 | tf_op jit(solution)/shard_map/all_gather | solution.py:212
  33.9 1.4 broadcast_in_dim.20
  35.8 4.0 %all-to-all-start.1 = ((bf16[4,256,768]{2,1,0:T(8,128)(2,1)}), bf16[4,256,768]{2,1,0:T(8,128)(2,1)S(1)}, u32[]{:S(2)}, u32[]{:S(2)}) async-start(bf16[4,256,768]{2,1,0:T(8,128)(2,1)} %broadcast_in_dim.20), calls=%async_computation.1 | async-start | bytes 3145728 | tf_op jit(solution)/shard_map/all_to_all | solution.py:17
  42.6 11.9 %all-to-all-done.1 = bf16[4,256,768]{2,1,0:T(8,128)(2,1)S(1)} async-done(((bf16[4,256,768]{2,1,0:T(8,128)(2,1)}), bf16[4,256,768]{2,1,0:T(8,128)(2,1)S(1)}, u32[]{:S(2)}, u32[]{:S(2)}) %all-to-all-start.1) | async-done | bytes 1572896 | tf_op jit(solution)/shard_map/all_to_all | solution.py:17
  54.5 8.8 %collective-permute-start = (bf16[1024,768]{1,0:T(8,128)(2,1)S(1)}, bf16[1024,768]{1,0:T(8,128)(2,1)S(1)}, u32[]{:S(2)}, u32[]{:S(2)}) collective-permute-start(bf16[1024,768]{1,0:T(8,128)(2,1)S(1)} %bitcast.60), channel_id=1, source_target_pairs={{0,16},{16,0},{1,17},{17,1},{2,18},{18,2},{3,19},{19,3},{4,20},{20... | collective-permute-start | bytes 4718600 | tf_op jit(solution)/shard_map/ppermute | solution.py:25
  68.1 5.5 %all-to-all-start.2 = ((bf16[4,64,512]{2,1,0:T(8,128)(2,1)}), bf16[4,64,512]{2,1,0:T(8,128)(2,1)S(1)}, u32[]{:S(2)}, u32[]{:S(2)}) async-start(bf16[4,64,512]{2,1,0:T(8,128)(2,1)} %broadcast_in_dim.21), calls=%async_computation.2 | async-start | bytes 524288 | tf_op jit(solution)/shard_map/all_to_all | solution.py:17
  74.2 1.6 copy-done.9
  76.9 4.2 %all-to-all-done.2.qa = bf16[4,64,512]{2,1,0:T(8,128)(2,1)S(1)} async-done(((bf16[4,64,512]{2,1,0:T(8,128)(2,1)}), bf16[4,64,512]{2,1,0:T(8,128)(2,1)S(1)}, u32[]{:S(2)}, u32[]{:S(2)}) %all-to-all-start.2) | async-done | bytes 262176 | tf_op jit(solution)/shard_map/all_to_all | solution.py:17
  81.1 2.3 %shard_map.111 = bf16[4,64,896]{2,1,0:T(8,128)(2,1)} custom-call(s32[4]{0:T(128)S(1)} %dynamic-slice_reduce_fusion.1.lengths, bf16[4,64,512]{2,1,0:T(8,128)(2,1)S(1)} %all-to-all-done.2.qa, bf16[512,256]{1,0:T(8,128)(2,1)S(1)} %convolution_convert_fusion.2.kv), custom_call_target="tpu_custom_call" | custom-call | tf_op jit(solution)/shard_map/pallas_call | solution.py:173
  83.5 3.5 %all-to-all-start.3 = ((bf16[4,64,896]{2,1,0:T(8,128)(2,1)}), bf16[4,64,896]{2,1,0:T(8,128)(2,1)S(1)}, u32[]{:S(2)}, u32[]{:S(2)}) async-start(bf16[4,64,896]{2,1,0:T(8,128)(2,1)} %shard_map.111), calls=%async_computation.3 | async-start | bytes 917504 | tf_op jit(solution)/shard_map/all_to_all | solution.py:238
  88.1 2.2 collective-permute-start.1
  90.3 3.7 %collective-permute-start.2 = (bf16[64,1024]{1,0:T(8,128)(2,1)S(1)}, bf16[64,1024]{1,0:T(8,128)(2,1)S(1)}, u32[]{:S(2)}, u32[]{:S(2)}) collective-permute-start(bf16[64,1024]{1,0:T(8,128)(2,1)S(1)} %get-tuple-element.80), channel_id=1, source_target_pairs={{0,256},{128,384},{256,0},{384,128},{1,257},{129,385},{257,1},{385... | collective-permute-start | bytes 393224 | tf_op jit(solution)/shard_map/ppermute | solution.py:243
  94.0 2.5 %collective-permute-start.3 = (bf16[64,1024]{1,0:T(8,128)(2,1)S(1)}, bf16[64,1024]{1,0:T(8,128)(2,1)S(1)}, u32[]{:S(2)}, u32[]{:S(2)}) collective-permute-start(bf16[64,1024]{1,0:T(8,128)(2,1)S(1)} %get-tuple-element.79), channel_id=1, source_target_pairs={{0,384},{128,0},{256,128},{384,256},{1,385},{129,1},{257,129},{385... | collective-permute-start | bytes 393224 | tf_op jit(solution)/shard_map/ppermute | solution.py:243
  97.2 1.5 collective-permute-done.2.third
  101.2 1.8 shard_map.112
  103.9 5.1 %collective-permute-start.4 = (bf16[16,64,256]{2,1,0:T(8,128)(2,1)S(1)}, bf16[16,64,256]{2,1,0:T(8,128)(2,1)S(1)}, u32[]{:S(2)}, u32[]{:S(2)}) collective-permute-start(bf16[16,64,256]{2,1,0:T(8,128)(2,1)S(1)} %get-tuple-element.56), channel_id=1, source_target_pairs={{0,16},{16,0},{1,17},{17,1},{2,18},{18,2},{3,19},{19,3},{4,20},{20... | collective-permute-start | bytes 1572872 | tf_op jit(solution)/shard_map/ppermute | solution.py:25
  109.0 1.5 collective-permute-done.4
  111.7 3.5 %all-to-all-start.4 = ((bf16[4,384,256]{2,1,0:T(8,128)(2,1)}), bf16[4,384,256]{2,1,0:T(8,128)(2,1)S(1)}, u32[]{:S(2)}, u32[]{:S(2)}) async-start(bf16[4,384,256]{2,1,0:T(8,128)(2,1)} %pad_maximum_fusion.1), calls=%async_computation.4 | async-start | bytes 1572864 | tf_op jit(solution)/shard_map/all_to_all | solution.py:250
  115.3 11.9 %all-to-all-done.4.moved = bf16[4,384,256]{2,1,0:T(8,128)(2,1)S(1)} async-done(((bf16[4,384,256]{2,1,0:T(8,128)(2,1)}), bf16[4,384,256]{2,1,0:T(8,128)(2,1)S(1)}, u32[]{:S(2)}, u32[]{:S(2)}) %all-to-all-start.4) | async-done | bytes 786464 | tf_op jit(solution)/shard_map/all_to_all | solution.py:250
  128.5 3.1 %collective-permute-start.5 = (bf16[256,512]{1,0:T(8,128)(2,1)S(1)}, bf16[256,512]{1,0:T(8,128)(2,1)S(1)}, u32[]{:S(2)}, u32[]{:S(2)}) collective-permute-start(bf16[256,512]{1,0:T(8,128)(2,1)S(1)} %get-tuple-element.62), channel_id=1, source_target_pairs={{0,16},{16,0},{1,17},{17,1},{2,18},{18,2},{3,19},{19,3},{4,20},{20... | collective-permute-start | bytes 786440 | tf_op jit(solution)/shard_map/ppermute | solution.py:25
  133.6 12.6 %all-to-all-start.5 = ((bf16[4,64,768]{2,1,0:T(8,128)(2,1)}), bf16[4,64,768]{2,1,0:T(8,128)(2,1)S(1)}, u32[]{:S(2)}, u32[]{:S(2)}) async-start(bf16[4,64,768]{2,1,0:T(8,128)(2,1)} %bitcast.25), calls=%async_computation.5 | async-start | bytes 786432 | tf_op jit(solution)/shard_map/all_to_all | solution.py:21
  146.2 1.7 convolution_convert_fusion.1
  148.4 13.4 %all-to-all-done.5 = bf16[4,64,768]{2,1,0:T(8,128)(2,1)S(1)} async-done(((bf16[4,64,768]{2,1,0:T(8,128)(2,1)}), bf16[4,64,768]{2,1,0:T(8,128)(2,1)S(1)}, u32[]{:S(2)}, u32[]{:S(2)}) %all-to-all-start.5) | async-done | bytes 393248 | tf_op jit(solution)/shard_map/all_to_all | solution.py:21
  162.7 3.5 %all-to-all-start.6 = ((bf16[4,64,1280]{2,1,0:T(8,128)(2,1)}), bf16[4,64,1280]{2,1,0:T(8,128)(2,1)S(1)}, u32[]{:S(2)}, u32[]{:S(2)}) async-start(bf16[4,64,1280]{2,1,0:T(8,128)(2,1)} %pad_maximum_fusion.2), calls=%async_computation.6 | async-start | bytes 1310720 | tf_op jit(solution)/shard_map/all_to_all | solution.py:21
  166.2 16.7 %all_gather.13 = bf16[256,512]{1,0:T(8,128)(2,1)S(1)} all-gather(bf16[64,512]{1,0:T(8,128)(2,1)S(1)} %slice.73), channel_id=1, replica_groups=mesh['x'=4,'zh'=4,'co'=2,'y'=4,'zl'=4] {'zh'}, dimensions={0}, use_global_device_ids=true | all-gather | bytes 327680 | tf_op jit(solution)/shard_map/all_gather | solution.py:268
  184.1 3.5 %all-to-all-start.7 = ((bf16[4,256,512]{2,1,0:T(8,128)(2,1)}), bf16[4,256,512]{2,1,0:T(8,128)(2,1)S(1)}, u32[]{:S(2)}, u32[]{:S(2)}) async-start(bf16[4,256,512]{2,1,0:T(8,128)(2,1)} %broadcast_in_dim.23), calls=%async_computation.7 | async-start | bytes 2097152 | tf_op jit(solution)/shard_map/all_to_all | solution.py:271
  187.6 20.6 %all-gather = bf16[256,768]{1,0:T(8,128)(2,1)S(1)} all-gather(bf16[64,768]{1,0:T(8,128)(2,1)S(1)} %slice.75), channel_id=2, replica_groups=mesh['x'=4,'zh'=4,'co'=2,'y'=4,'zl'=4] {'zl'}, dimensions={0}, use_global_device_ids=true | all-gather | bytes 491520 | tf_op jit(solution)/shard_map/all_gather | solution.py:274
  208.2 7.5 %collective-permute-start.6 = (bf16[4,256,512]{2,1,0:T(8,128)(2,1)S(1)}, bf16[4,256,512]{2,1,0:T(8,128)(2,1)S(1)}, u32[]{:S(2)}, u32[]{:S(2)}) collective-permute-start(bf16[4,256,512]{2,1,0:T(8,128)(2,1)S(1)} %all-to-all-done.7.mine), channel_id=1, source_target_pairs={{0,16},{16,0},{1,17},{17,1},{2,18},{18,2},{3,19},{19,3},{4,20},{20... | collective-permute-start | bytes 3145736 | tf_op jit(solution)/shard_map/ppermute | solution.py:25
  217.3 2.5 %fusion = bf16[1,128,2048]{2,1,0:T(8,128)(2,1)} fusion(bf16[2048,768]{1,0:T(8,128)(2,1)} %bitcast.68, bf16[64,256]{1,0:T(8,128)(2,1)S(1)} %get-tuple-element.92, bf16[64,256]{1,0:T(8,128)(2,1)S(1)} %get-tuple-element.91), kind=kOutput, calls=%fused_computation.2 | convolution fusion | flops 134610944 | bytes 1638400 | tf_op jit(solution)/shard_map/dot_general | solution.py:273
  219.8 2.2 %shard_map.115 = (f32[2048,256]{1,0:T(8,128)}, bf16[256,2048]{1,0:T(8,128)(2,1)}) custom-call(s32[1]{0:T(128)} %bitcast.core, bf16[4,256,512]{2,1,0:T(8,128)(2,1)S(1)} %all-to-all-done.7.mine, bf16[4,256,512]{2,1,0:T(8,128)(2,1)S(1)} %collective-permute-done.6.theirs), custom_call_target="tpu_custom_call" | custom-call | tf_op jit(solution)/shard_map/pallas_call | solution.py:184
  (88 shorter events, 23.5 us)
Async XLA Ops:
  3.2 5.2 %copy-start.12 = (bf16[256,64]{0,1:T(8,128)(2,1)S(1)}, bf16[256,64]{0,1:T(8,128)(2,1)}, u32[]{:S(2)}) copy-start(bf16[256,64]{0,1:T(8,128)(2,1)} %param.12) | copy-start | bytes 98308
  3.3 5.2 %copy-start.13 = (bf16[64,256]{1,0:T(8,128)(2,1)S(1)}, bf16[64,256]{1,0:T(8,128)(2,1)}, u32[]{:S(2)}) copy-start(bf16[64,256]{1,0:T(8,128)(2,1)} %param.11) | copy-start | bytes 98308
  3.3 5.2 %copy-start.14 = (bf16[64,256]{1,0:T(8,128)(2,1)S(1)}, bf16[64,256]{1,0:T(8,128)(2,1)}, u32[]{:S(2)}) copy-start(bf16[64,256]{1,0:T(8,128)(2,1)} %param.10) | copy-start | bytes 98308
  3.3 30.7 %all-to-all-start = ((bf16[4,128,2048]{2,1,0:T(8,128)(2,1)}), bf16[4,128,2048]{2,1,0:T(8,128)(2,1)S(1)}, u32[]{:S(2)}, u32[]{:S(2)}) async-start(bf16[4,128,2048]{2,1,0:T(8,128)(2,1)} %broadcast_in_dim.19), calls=%async_computation | async-start | bytes 4194304 | tf_op jit(solution)/shard_map/all_to_all | solution.py:17
  33.9 1.8 copy-start
  35.3 4.5 %copy-start.10 = (bf16[1,64,2048]{2,1,0:T(8,128)(2,1)S(1)}, bf16[1,64,2048]{2,1,0:T(8,128)(2,1)}, u32[]{:S(2)}) copy-start(bf16[1,64,2048]{2,1,0:T(8,128)(2,1)} %param.7) | copy-start | bytes 786436
  35.3 5.0 %copy-start.11 = (bf16[1,64,2048]{2,1,0:T(8,128)(2,1)S(1)}, bf16[1,64,2048]{2,1,0:T(8,128)(2,1)}, u32[]{:S(2)}) copy-start(bf16[1,64,2048]{2,1,0:T(8,128)(2,1)} %param.13) | copy-start | bytes 786436
  35.8 18.7 %all-to-all-start.1 = ((bf16[4,256,768]{2,1,0:T(8,128)(2,1)}), bf16[4,256,768]{2,1,0:T(8,128)(2,1)S(1)}, u32[]{:S(2)}, u32[]{:S(2)}) async-start(bf16[4,256,768]{2,1,0:T(8,128)(2,1)} %broadcast_in_dim.20), calls=%async_computation.1 | async-start | bytes 3145728 | tf_op jit(solution)/shard_map/all_to_all | solution.py:17
  41.0 22.8 %copy-start.15 = (s32[1,16]{1,0:T(1,128)S(1)}, s32[1,16]{1,0:T(1,128)}, u32[]{:S(2)}) copy-start(s32[1,16]{1,0:T(1,128)} %param.9) | copy-start | bytes 196
  54.5 12.4 %collective-permute-start = (bf16[1024,768]{1,0:T(8,128)(2,1)S(1)}, bf16[1024,768]{1,0:T(8,128)(2,1)S(1)}, u32[]{:S(2)}, u32[]{:S(2)}) collective-permute-start(bf16[1024,768]{1,0:T(8,128)(2,1)S(1)} %bitcast.60), channel_id=1, source_target_pairs={{0,16},{16,0},{1,17},{17,1},{2,18},{18,2},{3,19},{19,3},{4,20},{20... | collective-permute-start | bytes 4718600 | tf_op jit(solution)/shard_map/ppermute | solution.py:25
  64.8 2.1 copy-start.2
  68.1 13.0 %all-to-all-start.2 = ((bf16[4,64,512]{2,1,0:T(8,128)(2,1)}), bf16[4,64,512]{2,1,0:T(8,128)(2,1)S(1)}, u32[]{:S(2)}, u32[]{:S(2)}) async-start(bf16[4,64,512]{2,1,0:T(8,128)(2,1)} %broadcast_in_dim.21), calls=%async_computation.2 | async-start | bytes 524288 | tf_op jit(solution)/shard_map/all_to_all | solution.py:17
  73.8 2.4 %copy-start.1 = (bf16[4,128,2048]{2,1,0:T(8,128)(2,1)S(1)}, bf16[4,128,2048]{2,1,0:T(8,128)(2,1)}, u32[]{:S(2)}) copy-start(bf16[4,128,2048]{2,1,0:T(8,128)(2,1)} %copy-done) | copy-start | bytes 6291460
  74.2 1.6 copy-start.9
  83.5 17.8 %all-to-all-start.3 = ((bf16[4,64,896]{2,1,0:T(8,128)(2,1)}), bf16[4,64,896]{2,1,0:T(8,128)(2,1)S(1)}, u32[]{:S(2)}, u32[]{:S(2)}) async-start(bf16[4,64,896]{2,1,0:T(8,128)(2,1)} %shard_map.111), calls=%async_computation.3 | async-start | bytes 917504 | tf_op jit(solution)/shard_map/all_to_all | solution.py:238
  88.1 8.5 %collective-permute-start.1 = (bf16[64,1024]{1,0:T(8,128)(2,1)S(1)}, bf16[64,1024]{1,0:T(8,128)(2,1)S(1)}, u32[]{:S(2)}, u32[]{:S(2)}) collective-permute-start(bf16[64,1024]{1,0:T(8,128)(2,1)S(1)} %get-tuple-element.81), channel_id=1, source_target_pairs={{0,128},{128,256},{256,384},{384,0},{1,129},{129,257},{257,385},{3... | collective-permute-start | bytes 393224 | tf_op jit(solution)/shard_map/ppermute | solution.py:243
  90.3 8.4 %collective-permute-start.2 = (bf16[64,1024]{1,0:T(8,128)(2,1)S(1)}, bf16[64,1024]{1,0:T(8,128)(2,1)S(1)}, u32[]{:S(2)}, u32[]{:S(2)}) collective-permute-start(bf16[64,1024]{1,0:T(8,128)(2,1)S(1)} %get-tuple-element.80), channel_id=1, source_target_pairs={{0,256},{128,384},{256,0},{384,128},{1,257},{129,385},{257,1},{385... | collective-permute-start | bytes 393224 | tf_op jit(solution)/shard_map/ppermute | solution.py:243
  94.0 6.6 %collective-permute-start.3 = (bf16[64,1024]{1,0:T(8,128)(2,1)S(1)}, bf16[64,1024]{1,0:T(8,128)(2,1)S(1)}, u32[]{:S(2)}, u32[]{:S(2)}) collective-permute-start(bf16[64,1024]{1,0:T(8,128)(2,1)S(1)} %get-tuple-element.79), channel_id=1, source_target_pairs={{0,384},{128,0},{256,128},{384,256},{1,385},{129,1},{257,129},{385... | collective-permute-start | bytes 393224 | tf_op jit(solution)/shard_map/ppermute | solution.py:243
  96.6 0.7 copy-start.3
  98.7 0.7 copy-start.5
  100.6 0.6 copy-start.7
  103.9 6.6 %collective-permute-start.4 = (bf16[16,64,256]{2,1,0:T(8,128)(2,1)S(1)}, bf16[16,64,256]{2,1,0:T(8,128)(2,1)S(1)}, u32[]{:S(2)}, u32[]{:S(2)}) collective-permute-start(bf16[16,64,256]{2,1,0:T(8,128)(2,1)S(1)} %get-tuple-element.56), channel_id=1, source_target_pairs={{0,16},{16,0},{1,17},{17,1},{2,18},{18,2},{3,19},{19,3},{4,20},{20... | collective-permute-start | bytes 1572872 | tf_op jit(solution)/shard_map/ppermute | solution.py:25
  110.7 16.5 %copy-start.4 = (bf16[64,1024]{1,0:T(8,128)(2,1)S(1)}, bf16[64,1024]{1,0:T(8,128)(2,1)}, u32[]{:S(2)}) copy-start(bf16[64,1024]{1,0:T(8,128)(2,1)} %copy-done.3) | copy-start | bytes 393220
  110.7 16.5 %copy-start.6 = (bf16[64,1024]{1,0:T(8,128)(2,1)S(1)}, bf16[64,1024]{1,0:T(8,128)(2,1)}, u32[]{:S(2)}) copy-start(bf16[64,1024]{1,0:T(8,128)(2,1)} %copy-done.5) | copy-start | bytes 393220
  110.7 16.5 %copy-start.8 = (bf16[64,1024]{1,0:T(8,128)(2,1)S(1)}, bf16[64,1024]{1,0:T(8,128)(2,1)}, u32[]{:S(2)}) copy-start(bf16[64,1024]{1,0:T(8,128)(2,1)} %copy-done.7) | copy-start | bytes 393220
  111.7 15.5 %all-to-all-start.4 = ((bf16[4,384,256]{2,1,0:T(8,128)(2,1)}), bf16[4,384,256]{2,1,0:T(8,128)(2,1)S(1)}, u32[]{:S(2)}, u32[]{:S(2)}) async-start(bf16[4,384,256]{2,1,0:T(8,128)(2,1)} %pad_maximum_fusion.1), calls=%async_computation.4 | async-start | bytes 1572864 | tf_op jit(solution)/shard_map/all_to_all | solution.py:250
  128.5 4.3 %collective-permute-start.5 = (bf16[256,512]{1,0:T(8,128)(2,1)S(1)}, bf16[256,512]{1,0:T(8,128)(2,1)S(1)}, u32[]{:S(2)}, u32[]{:S(2)}) collective-permute-start(bf16[256,512]{1,0:T(8,128)(2,1)S(1)} %get-tuple-element.62), channel_id=1, source_target_pairs={{0,16},{16,0},{1,17},{17,1},{2,18},{18,2},{3,19},{19,3},{4,20},{20... | collective-permute-start | bytes 786440 | tf_op jit(solution)/shard_map/ppermute | solution.py:25
  133.6 28.1 %all-to-all-start.5 = ((bf16[4,64,768]{2,1,0:T(8,128)(2,1)}), bf16[4,64,768]{2,1,0:T(8,128)(2,1)S(1)}, u32[]{:S(2)}, u32[]{:S(2)}) async-start(bf16[4,64,768]{2,1,0:T(8,128)(2,1)} %bitcast.25), calls=%async_computation.5 | async-start | bytes 786432 | tf_op jit(solution)/shard_map/all_to_all | solution.py:21
  162.7 20.2 %all-to-all-start.6 = ((bf16[4,64,1280]{2,1,0:T(8,128)(2,1)}), bf16[4,64,1280]{2,1,0:T(8,128)(2,1)S(1)}, u32[]{:S(2)}, u32[]{:S(2)}) async-start(bf16[4,64,1280]{2,1,0:T(8,128)(2,1)} %pad_maximum_fusion.2), calls=%async_computation.6 | async-start | bytes 1310720 | tf_op jit(solution)/shard_map/all_to_all | solution.py:21
  184.1 24.1 %all-to-all-start.7 = ((bf16[4,256,512]{2,1,0:T(8,128)(2,1)}), bf16[4,256,512]{2,1,0:T(8,128)(2,1)S(1)}, u32[]{:S(2)}, u32[]{:S(2)}) async-start(bf16[4,256,512]{2,1,0:T(8,128)(2,1)} %broadcast_in_dim.23), calls=%async_computation.7 | async-start | bytes 2097152 | tf_op jit(solution)/shard_map/all_to_all | solution.py:271
  208.2 11.6 %collective-permute-start.6 = (bf16[4,256,512]{2,1,0:T(8,128)(2,1)S(1)}, bf16[4,256,512]{2,1,0:T(8,128)(2,1)S(1)}, u32[]{:S(2)}, u32[]{:S(2)}) collective-permute-start(bf16[4,256,512]{2,1,0:T(8,128)(2,1)S(1)} %all-to-all-done.7.mine), channel_id=1, source_target_pairs={{0,16},{16,0},{1,17},{17,1},{2,18},{18,2},{3,19},{19,3},{4,20},{20... | collective-permute-start | bytes 3145736 | tf_op jit(solution)/shard_map/ppermute | solution.py:25
